TPU v7x, 256 devices: a whole 4x4x8 slice. The times are simulated.
256 devices in a mesh: ctx: 64 (over z, y_lo, x), tp: 4 (over y_hi, core).
Axes of the slice: x: 4, y: 4 (y_hi: 2, y_lo: 2; y = y_hi * 2 + y_lo), z: 8, core: 2. Of those that a mesh axis runs over, the one named last changes fastest.
Arguments:
- prefill_queries: bfloat16 [12288, 5120], P('ctx', 'tp'), may hold values from -20 to 20
- prefill_keys: bfloat16 [12288, 1024], P('ctx', 'tp'), may hold values from -5 to 5
- prefill_values: bfloat16 [12288, 1024], P('ctx', 'tp'), may hold values from -6 to 6
- segments: int32 [12288], replicated, may hold values from 0 to 7, never falling along the last dimension, each value on 1 to 9216 neighbouring positions
- decode_queries: bfloat16 [3, 64, 5120], P(None, None, 'tp'), may hold values from -152 to 152
- decode_keys: bfloat16 [3, 64, 1024], P(None, 'ctx', 'tp'), may hold values from -12 to 12
- decode_values: bfloat16 [3, 64, 1024], P(None, 'ctx', 'tp'), may hold values from -4 to 4
- row_request: int32 [64], replicated, may hold values from 0 to 7
- norm_gain: float32 [5120], P('tp'), may hold values from 0.25 to 1.75
- head_weight: bfloat16 [5120, 98304], P('tp', 'ctx'), may hold values from -0.27155765 to 0.27155765
- allowed_tiles: int32 [3, 64, 32], replicated, may hold values from 0 to 767, as said below
- tokens: int32 [3, 64], replicated, may hold values from 0 to 98303, as said below
Outputs:
- prefill_output: bfloat16 [12288, 5120], P('ctx', 'tp')
- target_logprob: float32 [3, 64], P(None, 'ctx')
Inputs may be any that keep to these rules, and one draw needn't show every extreme that they name: `segments`: positions are grouped by request in order, each request's prompt spans 1 to 9216 positions and one spans exactly 9216. `allowed_tiles`: the 32 tiles of a row are distinct; tile k holds ids k * 128 to k * 128 + 127. `tokens`: each token lies in one of the allowed tiles of its row and step.
All inputs are finite; a program needn't handle non-finite values.
Results may differ from a plain program's by a relative error of at most 0.011.
Values may be sent and summed in bfloat16 or wider, within the bound.
No kernel may reach another device: no remote copies, remote signals or barrier semaphores. Data moves between devices by JAX's collectives and lax.ppermute only.
A program may use at most 192 MiB of HBM per device.

v0:
```python
import jax
import jax.numpy as jnp
from jax import lax
from jax.sharding import PartitionSpec as P

D = 5120
HD = 128
TILE = 128


epsilon = 1e-06
floor_value = -1e30


def from_behind(block, axis, distance):
    devices = range(lax.axis_size(axis))
    route = [(i - distance, i) for i in devices if i - distance in devices]
    return lax.ppermute(block, axis, route)


def joined(value, axis, join):
    gathered = jax.tree.map(
        lambda a, kind: lax.all_gather(a.astype(kind), axis),
        value,
        (jnp.bfloat16, jnp.bfloat16, jnp.bfloat16),
    )

    def take(source):
        return jax.tree.map(
            lambda a, own: lax.dynamic_index_in_dim(a, source, 0, False).astype(own.dtype),
            gathered,
            value,
        )

    return lax.fori_loop(
        1, lax.axis_size(axis), lambda source, state: join(state, take(source)), take(0)
    )


def fold_block(carry_state, queries, key_rows, values, key_mask, score_scale):
    row_peak, row_total, row_output = carry_state
    scores = (
        jnp.einsum("qhgd,khd->qhgk", queries, key_rows, preferred_element_type=jnp.float32)
        * score_scale
    )
    masked = jnp.where(key_mask, scores, floor_value)
    new_peak = jnp.maximum(row_peak, jnp.max(masked, axis=-1))
    weights = jnp.where(key_mask, jnp.exp(masked - new_peak[..., None]), 0.0)
    rescale = jnp.exp(row_peak - new_peak)
    row_total = row_total * rescale + jnp.sum(weights, axis=-1)
    row_output = row_output * rescale[..., None] + jnp.einsum(
        "qhgk,khd->qhgd", weights.astype(jnp.bfloat16), values, preferred_element_type=jnp.float32
    )
    return (new_peak, row_total, row_output)


def join_states(first_state, second_state):
    joint_peak = jnp.maximum(first_state[0], second_state[0])
    first_scale = jnp.exp(first_state[0] - joint_peak)
    second_scale = jnp.exp(second_state[0] - joint_peak)
    joint_total = first_state[1] * first_scale + second_state[1] * second_scale
    joint_output = (
        first_state[2] * first_scale[..., None] + second_state[2] * second_scale[..., None]
    )
    return (joint_peak, joint_total, joint_output)


def empty_state(leading, head_size):
    return (
        jnp.full(leading, floor_value, jnp.float32),
        jnp.zeros(leading, jnp.float32),
        jnp.zeros(leading + (head_size,), jnp.float32),
    )


def local(
    prefill_queries,
    prefill_keys,
    prefill_values,
    segments,
    decode_queries,
    decode_keys,
    decode_values,
    row_request,
    norm_gain,
    head_weight,
    allowed_tiles,
    tokens,
):
    axis_count = lax.axis_size("ctx")
    my_index = lax.axis_index("ctx")
    local_rows = prefill_queries.shape[0]
    kv_heads = prefill_keys.shape[1] // HD
    group_size = prefill_queries.shape[1] // prefill_keys.shape[1]
    score_scale = HD ** (-0.5)
    queries = prefill_queries.reshape(local_rows, kv_heads, group_size, HD)
    inside = jnp.arange(local_rows, dtype=jnp.int32)
    query_places = my_index * local_rows + inside
    query_segment = lax.dynamic_slice_in_dim(segments, my_index * local_rows, local_rows)

    def block_mask(source):
        first_key = jnp.maximum(source, 0) * local_rows
        key_segment = lax.dynamic_slice_in_dim(segments, first_key, local_rows)
        causal = (source * local_rows + inside)[None, :] <= query_places[:, None]
        valid = source >= 0
        return (causal & valid & (key_segment[None, :] == query_segment[:, None]))[:, None, None, :]

    def attend(carry_state, key_value, source):
        key_rows = key_value[0].reshape(local_rows, kv_heads, HD)
        values = key_value[1].reshape(local_rows, kv_heads, HD)
        return fold_block(carry_state, queries, key_rows, values, block_mask(source), score_scale)

    initial = empty_state((local_rows, kv_heads, group_size), HD)
    key_value = jnp.stack([prefill_keys, prefill_values])
    carry_state = attend(initial, key_value, my_index)
    turn_count = axis_count - 1

    def pass_turn(turn_index, carry):
        moving, inner_state = carry
        moving = from_behind(moving, "ctx", 1)
        source = my_index - turn_index - 1
        return (moving, attend(inner_state, moving, source))

    key_value, carry_state = lax.fori_loop(0, turn_count, pass_turn, (key_value, carry_state))
    prefill_output = (
        (carry_state[2] / carry_state[1][..., None]).reshape(local_rows, -1).astype(jnp.bfloat16)
    )
    step_count, row_count, feature_width = decode_queries.shape
    own_rows = decode_keys.shape[1]
    flat_queries = decode_queries.reshape(step_count * row_count, kv_heads, group_size, HD)
    request_mask = row_request[:, None] == query_segment[None, :]
    wide_mask = jnp.broadcast_to(request_mask[None], (step_count, row_count, local_rows))
    wide_mask = wide_mask.reshape(step_count * row_count, local_rows)[:, None, None, :]
    local_keys = prefill_keys.reshape(local_rows, kv_heads, HD)
    local_values = prefill_values.reshape(local_rows, kv_heads, HD)
    part_peak, part_total, part_output = fold_block(
        empty_state((step_count * row_count, kv_heads, group_size), HD),
        flat_queries,
        local_keys,
        local_values,
        wide_mask,
        score_scale,
    )
    part_peak = part_peak.reshape(step_count, row_count, kv_heads, group_size)
    part_total = part_total.reshape(step_count, row_count, kv_heads, group_size)
    part_output = part_output.reshape(step_count, row_count, kv_heads, group_size, HD)
    merged_peak, merged_total, merged_output = joined(
        (part_peak, part_total, part_output), "ctx", join_states
    )
    row_peak = lax.dynamic_slice_in_dim(merged_peak, my_index * own_rows, own_rows, 1)
    row_total = lax.dynamic_slice_in_dim(merged_total, my_index * own_rows, own_rows, 1)
    row_output = lax.dynamic_slice_in_dim(merged_output, my_index * own_rows, own_rows, 1)
    own_queries = lax.dynamic_slice_in_dim(decode_queries, my_index * own_rows, own_rows, 1)
    own_queries = own_queries.reshape(step_count, own_rows, kv_heads, group_size, HD)
    own_keys = decode_keys.reshape(step_count, own_rows, kv_heads, HD)
    own_values = decode_values.reshape(step_count, own_rows, kv_heads, HD)
    own_scores = (
        jnp.einsum("srhgd,jrhd->srhgj", own_queries, own_keys, preferred_element_type=jnp.float32)
        * score_scale
    )
    step_order = jnp.arange(step_count, dtype=jnp.int32)
    own_mask = (step_order[None, :] <= step_order[:, None])[:, None, None, None, :]
    own_masked = jnp.where(own_mask, own_scores, floor_value)
    new_peak = jnp.maximum(row_peak, jnp.max(own_masked, axis=-1))
    rescale = jnp.exp(row_peak - new_peak)
    weights = jnp.where(own_mask, jnp.exp(own_masked - new_peak[..., None]), 0.0)
    row_total = row_total * rescale + jnp.sum(weights, axis=-1)
    row_output = row_output * rescale[..., None] + jnp.einsum(
        "srhgj,jrhd->srhgd",
        weights.astype(jnp.bfloat16),
        own_values,
        preferred_element_type=jnp.float32,
    )
    attention = (
        (row_output / row_total[..., None])
        .reshape(step_count, own_rows, feature_width)
        .astype(jnp.bfloat16)
    )
    gathered = lax.all_gather(attention, "ctx", axis=1, tiled=True)
    widened = gathered.astype(jnp.float32)
    squares = jnp.sum(widened * widened, axis=-1)
    scaled = (widened * norm_gain).astype(jnp.bfloat16)
    partial_value = jnp.einsum(
        "srf,fv->srv", scaled, head_weight, preferred_element_type=jnp.float32
    )
    tp_size = lax.axis_size("tp")
    spread = jnp.broadcast_to(squares[..., None], (step_count, row_count, tp_size))
    summed, total_squares = (
        lax.psum_scatter(
            partial_value.astype(jnp.bfloat16), "tp", scatter_dimension=2, tiled=True
        ).astype(jnp.float32),
        lax.psum_scatter(spread.astype(jnp.bfloat16), "tp", scatter_dimension=2, tiled=True).astype(
            jnp.float32
        ),
    )
    logits = lax.rsqrt(total_squares / D + epsilon) * summed
    vocab_span = summed.shape[2]
    first_id = my_index * vocab_span * tp_size + lax.axis_index("tp") * vocab_span
    tiles_here = first_id // TILE + jnp.arange(vocab_span // TILE, dtype=jnp.int32)
    allowed = jnp.any(allowed_tiles[..., None] == tiles_here, axis=2)
    keep_mask = allowed[..., None]
    blocks = logits.reshape(step_count, row_count, vocab_span // TILE, TILE)
    masked = jnp.where(keep_mask, blocks, floor_value)
    score_peak = jnp.max(masked, axis=(2, 3))
    exp_mass = jnp.sum(
        jnp.where(keep_mask, jnp.exp(masked - score_peak[..., None, None]), 0.0), axis=(2, 3)
    )
    id_places = jnp.arange(vocab_span, dtype=jnp.int32)
    target = jnp.sum(
        jnp.where(id_places[None, None, :] == (tokens - first_id)[..., None], logits, 0.0), axis=-1
    )
    global_peak = lax.pmax(score_peak, ("ctx", "tp"))
    exp_mass, target = lax.psum(
        (exp_mass * jnp.exp(score_peak - global_peak), target), ("ctx", "tp")
    )
    score_peak = global_peak
    result = target - (score_peak + jnp.log(exp_mass))
    target_logprob = lax.dynamic_slice_in_dim(result, my_index * own_rows, own_rows, 1)
    return (prefill_output, target_logprob)


def solution(mesh):
    placed = (
        P("ctx", "tp"),
        P("ctx", "tp"),
        P("ctx", "tp"),
        P(),
        P(None, None, "tp"),
        P(None, "ctx", "tp"),
        P(None, "ctx", "tp"),
        P(),
        P("tp"),
        P("tp", "ctx"),
        P(),
        P(),
    )
    return jax.shard_map(
        local,
        mesh=mesh,
        in_specs=placed,
        out_specs=(P("ctx", "tp"), P(None, "ctx")),
        check_vma=False,
    )
```

profile of v0, /device:TPU:96, one launch (start us, length us, event | category | flops | bytes accessed | tf_op | source)
XLA Modules:
  0.0 1960.6 jit_solution(702790421649652330)
XLA Ops:
  17.9 143.9 %all_gather.16 = bf16[64,3,64,2,5]{2,3,4,1,0:T(2,128)(2,1)S(1)} all-gather(bf16[1,3,64,2,5]{2,3,4,1,0:T(2,128)(2,1)S(1)} %copy.180), channel_id=1, replica_groups=mesh['ctx'=64,'tp'=4] {'ctx'}, dimensions={0}, use_global_device_ids=true | all-gather | bytes 249600 | tf_op jit(solution)/shard_map/all_gather | solution.py:23
  161.9 154.4 %all_gather.15 = bf16[64,3,64,2,5]{2,3,4,1,0:T(2,128)(2,1)S(1)} all-gather(bf16[1,3,64,2,5]{2,3,4,1,0:T(2,128)(2,1)S(1)} %copy.178), channel_id=1, replica_groups=mesh['ctx'=64,'tp'=4] {'ctx'}, dimensions={0}, use_global_device_ids=true | all-gather | bytes 249600 | tf_op jit(solution)/shard_map/all_gather | solution.py:23
  319.3 62.0 %all-gather.2.cloned.1.call-done = bf16[64,3,64,2,5,128]{5,2,4,3,1,0:T(8,128)(2,1)} async-done(((bf16[1,3,64,2,5,128]{5,2,4,3,1,0:T(8,128)(2,1)}), bf16[64,3,64,2,5,128]{5,2,4,3,1,0:T(8,128)(2,1)}) %all-gather.2.cloned.1.call-update) | async-done | bytes 31457296 | tf_op jit(solution)/shard_map/all_gather | solution.py:23
  383.0 257.6 %while.41 = (s32[]{:T(128)}, f32[3,64,2,5]{1,2,3,0:T(2,128)S(1)}, f32[3,64,2,5]{1,2,3,0:T(2,128)S(1)}, f32[3,64,2,5,128]{4,3,2,1,0:T(8,128)S(1)}, bf16[64,3,64,2...) while((s32[]{:T(128)}, f32[3,64,2,5]{1,2,3,0:T(2,128)S(1)}, ...), condition=%wide.region_9.10_spmd, body=%wide.region_8.9_spmd.sunk | while | flops 998405 | bytes 3540631 | solution.py:35
  641.4 150.6 %all_gather.18 = bf16[3,64,1280]{2,0,1:T(4,128)(2,1)S(1)} all-gather(bf16[3,1,1280]{2,0,1:T(4,128)(2,1)S(1)} %convert_element_type.168), channel_id=1, replica_groups=mesh['ctx'=64,'tp'=4] {'ctx'}, dimensions={1}, use_global_device_ids=true | all-gather | bytes 499200 | tf_op jit(solution)/shard_map/all_gather | solution.py:179
  798.2 953.9 %while.42 = (s32[]{:T(128)}, bf16[2,192,256]{2,1,0:T(8,128)(2,1)S(1)}, f32[192,2,5]{0,2,1:T(8,128)S(1)}, f32[192,2,5]{0,2,1:T(8,128)S(1)}, f32[192,2,5,128]{3,0,...) while((s32[]{:T(128)}, ...), condition=%wide.region_5.6_spmd.clone, body=%wide.region_2.5_spmd.clone.sunk | while | flops 194179200 | bytes 17185120 | solution.py:124
  958.6 9.5 collective-permute-done
  974.4 9.0 collective-permute-done
  1085.8 8.6 collective-permute-start
  1237.8 8.8 collective-permute-start
  1254.4 9.2 collective-permute-start
  1272.3 8.9 collective-permute-start
  1288.6 9.1 collective-permute-start
  1425.7 8.6 collective-permute-start
  1441.0 8.8 collective-permute-start
  1457.6 9.2 collective-permute-start
  1475.5 8.9 collective-permute-start
  1491.8 9.1 collective-permute-start
  1598.4 8.6 collective-permute-start
  1690.0 8.9 collective-permute-start
  1705.6 8.9 collective-permute-start
  1721.2 8.9 collective-permute-start
  1765.0 113.5 %pmax.7 = f32[3,64]{1,0:T(4,128)S(1)} all-reduce(f32[3,64]{1,0:T(4,128)S(1)} %fusion.62), channel_id=1, replica_groups=mesh['ctx'=64,'tp'=4] {'ctx','tp'}, use_global_device_ids=true, to_apply=%region_19.20 | all-reduce | flops 192 | bytes 1536 | tf_op jit(solution)/shard_map/pmax | solution.py:212
  1878.9 74.2 %all-reduce.1 = (f32[3,64]{1,0:T(4,128)S(1)}, f32[3,64]{1,0:T(4,128)S(1)}) all-reduce(f32[3,64]{1,0:T(4,128)S(1)} %get-tuple-element.551, f32[3,64]{1,0:T(4,128)S(1)} %exponential_multiply_fusion.2), channel_id=1, replica_groups=mesh['ctx'=64,'tp'=4] {'ctx','tp'}, use_global_device_ids=true, to_apply=%region_16.17 | all-reduce | flops 384 | bytes 3072 | tf_op jit(solution)/shard_map/psum | solution.py:213
  (1659 shorter events, 1094.1 us)
Async XLA Ops:
  7.2 374.1 %all-gather.2.cloned.1.call-start = ((), (), s32[]{:S(2)}) async-start(), calls=%async_computation.1 | async-start | bytes 31948800 | tf_op jit(solution)/shard_map/all_gather | solution.py:23
  14.5 1749.0 %reduce-scatter.4.cloned.1.call-start = ((), (), s32[]{:S(2)}) async-start(), calls=%async_computation.2 | async-start | bytes 983040
  798.2 12.1 collective-permute-start
  955.7 12.3 collective-permute-start
  971.6 11.9 collective-permute-start
  1085.8 11.8 collective-permute-start
  1176.7 11.8 collective-permute-start
  1207.3 11.8 collective-permute-start
  1222.5 11.8 collective-permute-start
  1237.8 13.1 collective-permute-start
  1254.4 14.3 collective-permute-start
  1272.3 12.9 collective-permute-start
  1288.6 12.3 collective-permute-start
  1410.5 11.8 collective-permute-start
  1425.7 11.8 collective-permute-start
  1441.0 13.1 collective-permute-start
  1457.6 14.3 collective-permute-start
  1475.5 12.9 collective-permute-start
  1491.8 12.3 collective-permute-start
  1598.4 11.8 collective-permute-start
  1659.5 11.8 collective-permute-start
  1690.0 12.1 collective-permute-start
  1705.6 12.1 collective-permute-start
  1721.2 12.1 collective-permute-start
  (179 other events, 1818.3 us)
Sparse Core Ops, SparseCore 0:
  14.6 366.5 all-gather.1
  798.3 49.3 reduce-scatter.3
where the time goes:
time: 1980 us; the launch traced here: 1960 us
  blocking collectives  644 us (33%)
  starting transfers between devices  416 us (21%)
  waiting for transfers between devices  319 us (16%)
  local copies, waits for them, and re-layouts  220 us (11%)
  other arithmetic  218 us (11%)
  matrix products  119 us (6%)
    ppermute x63, starting transfers between devices, from_behind(): return lax.ppermute(block, axis, route)  416 us
    all_gather x2, blocking collectives, joined(): lax.all_gather(a.astype(kind), axis)  298 us
    ppermute x63, waiting for transfers between devices, from_behind(): return lax.ppermute(block, axis, route)  257 us
    all_gather x1, blocking collectives, local(): gathered = lax.all_gather(attention, 'ctx', axis=1, tiled=True)  151 us
    add x63, other arithmetic, join_states(): first_state[2] * first_scale[..., None]  120 us
    pmax x1, blocking collectives, local(): global_peak = lax.pmax(score_peak, ('ctx', 'tp'))  114 us
    dot_general x65, matrix products, fold_block(): jnp.einsum('qhgk,khd->qhgd', weights.astype(jnp.bfloat16), values, prefer...  82.6 us
    psum x1, blocking collectives, local(): lax.psum((exp_mass * jnp.exp(score_peak - global_peak), target), ('ctx',...  74.2 us
  transfers between devices with their start and end apart: 65, of which 64 were waited for; matrix products, arithmetic and copies ran while one was open for 11% of the time, Pallas kernels for 0%

commit v1 on v0

v1 whole, which is shorter than its diff:
```python
import functools
import math

import jax
import jax.numpy as jnp
from jax import lax
from jax.experimental import pallas as pl
from jax.experimental.pallas import tpu as pltpu
from jax.sharding import Mesh, PartitionSpec as P

HD = 128
TILE = 128
EPS = 1e-06
FLOOR = -1e30
BELOW = -2e30
LOG2E = 1.4426950408889634
BF = jnp.bfloat16
F32 = jnp.float32
CTX = ("z", "yl", "x")
TP = ("yh", "core")
KT = 512


def dot_t(a, b):
    return lax.dot_general(a, b, (((1,), (1,)), ((), ())), preferred_element_type=F32)


def dot(a, b):
    return lax.dot_general(a, b, (((1,), (0,)), ((), ())), preferred_element_type=F32)


def two_parts(value):
    high = value.astype(BF)
    return high, (value - high.astype(F32)).astype(BF)


def attend_kernel(
    shape, info, q_ref, start_ref, place_ref, kv_hbm, out_ref, keys, vals, qs, peak, acc, sem
):
    nz, ny, nx, rows, group = shape
    copies = []
    for z in range(nz):
        for x in range(nx):
            for y in range(ny):
                there = pl.ds(((z * ny + y) * nx + x) * rows, rows)
                k, v = kv_hbm.at[z * nx + x, 0, y], kv_hbm.at[z * nx + x, 1, y]
                copies.append(pltpu.make_async_copy(k, keys.at[there, 0:HD], sem))
                copies.append(pltpu.make_async_copy(k, keys.at[there, HD : 2 * HD], sem))
                copies.append(pltpu.make_async_copy(v, vals.at[there, 0:HD], sem))
    for copy in copies:
        copy.start()
    scale = HD**-0.5 * LOG2E
    for tile in range(ny):
        for h in range(group):
            q = q_ref[tile, :, h * HD : (h + 1) * HD].astype(F32) * scale
            high, low = two_parts(q)
            qs[tile, h, :, 0:HD] = high
            qs[tile, h, :, HD : 2 * HD] = low
    vals[:, HD : 2 * HD] = jnp.ones((vals.shape[0], HD), BF)
    for copy in copies:
        copy.wait()
    for tile in range(ny):
        first, last, inner_first, inner_last = (info[tile, i] for i in range(4))
        peak[...] = jnp.full(peak.shape, FLOOR, F32)
        acc[...] = jnp.zeros(acc.shape, F32)

        def step(turn, masked):
            base = pl.multiple_of(turn * KT, KT)
            k = keys[pl.ds(base, KT), :]
            v = vals[pl.ds(base, KT), :]
            if masked:
                at = base + lax.broadcasted_iota(jnp.int32, (rows, KT), 1)
                keep = (at >= start_ref[tile]) & (at <= place_ref[tile])
            for h in range(group):
                s = dot_t(qs[tile, h], k)
                if masked:
                    s = jnp.where(keep, s, BELOW)
                old = peak[h]
                new = jnp.maximum(old, jnp.max(s, axis=1, keepdims=True))
                peak[h] = new
                p = jnp.exp2(s - new).astype(BF)
                acc[h] = acc[h] * jnp.exp2(old - new) + dot(p, v)

        def turn_of(turn, _):
            inside = (turn >= inner_first) & (turn < inner_last)

            @pl.when(inside)
            def _():
                step(turn, False)

            @pl.when(jnp.logical_not(inside))
            def _():
                step(turn, True)

            return 0

        lax.fori_loop(first, last, turn_of, 0)
        for h in range(group):
            out_ref[tile, :, h * HD : (h + 1) * HD] = (acc[h, :, 0:HD] / acc[h, :, HD : 2 * HD]).astype(BF)


def attend(sizes, info, q, start, place, kv):
    nz, ny, nx = sizes
    rows, width = q.shape[1], q.shape[2]
    group = width // HD
    total = nz * ny * nx * rows
    vmem = pl.BlockSpec(memory_space=pltpu.VMEM)
    hbm = pl.BlockSpec(memory_space=pl.ANY)
    return pl.pallas_call(
        functools.partial(attend_kernel, (nz, ny, nx, rows, group)),
        out_shape=jax.ShapeDtypeStruct(q.shape, BF),
        in_specs=[pl.BlockSpec(memory_space=pltpu.SMEM), vmem, vmem, vmem, hbm],
        out_specs=vmem,
        scratch_shapes=[
            pltpu.VMEM((total, 2 * HD), BF),
            pltpu.VMEM((total, 2 * HD), BF),
            pltpu.VMEM((ny, group, rows, 2 * HD), BF),
            pltpu.VMEM((group, rows, 1), F32),
            pltpu.VMEM((group, rows, 2 * HD), F32),
            pltpu.SemaphoreType.DMA,
        ],
        compiler_params=pltpu.CompilerParams(vmem_limit_bytes=40 * 2**20),
        cost_estimate=pl.CostEstimate(
            flops=20_000_000_000, bytes_accessed=8_000_000, transcendentals=17_000_000
        ),
    )(info, q, start, place, kv)


def state_kernel(shape, q_ref, k_ref, v_ref, ok_ref, ov_ref, keep_ref, out_ref):
    steps, lines, kv_heads, group = shape
    rows, own = k_ref.shape[0], ok_ref.shape[0]
    count = keep_ref.shape[1]
    scale = HD**-0.5 * LOG2E
    keep = keep_ref[...] > 0
    lane = lax.broadcasted_iota(jnp.int32, (steps * lines, HD), 1)
    tail = jnp.zeros((steps * lines, HD), F32)
    for kh in range(kv_heads):
        at = slice(kh * HD, (kh + 1) * HD)
        pad = jnp.zeros((count - rows - own, HD), BF)
        k = jnp.concatenate([k_ref[:, at], ok_ref[:, at], pad], axis=0)
        v = jnp.concatenate([v_ref[:, at], ov_ref[:, at], pad], axis=0)
        for g in range(group):
            h = kh * group + g
            high, low = two_parts(q_ref[:, h * HD : (h + 1) * HD].astype(F32) * scale)
            s = jnp.where(keep, dot_t(high, k) + dot_t(low, k), BELOW)
            top = jnp.maximum(jnp.max(s, axis=1, keepdims=True), FLOOR)
            p = jnp.exp2(s - top)
            total = jnp.sum(p, axis=1, keepdims=True)
            some = total > 0.0
            o = dot(p.astype(BF), v) / jnp.where(some, total, 1.0)
            out_ref[:, h * HD : (h + 1) * HD] = o.astype(BF)
            size = jnp.where(some, top + jnp.log2(jnp.where(some, total, 1.0)), FLOOR)
            high, low = two_parts(size)
            tail = jnp.where(lane == h, high.astype(F32), tail)
            tail = jnp.where(lane == h + 64, low.astype(F32), tail)
    width = kv_heads * group * HD
    out_ref[:, width : width + HD] = tail.astype(BF)


def states(shape, q, k, v, own_k, own_v, keep):
    vmem = pl.BlockSpec(memory_space=pltpu.VMEM)
    return pl.pallas_call(
        functools.partial(state_kernel, shape),
        out_shape=jax.ShapeDtypeStruct((q.shape[0], q.shape[1] + HD), BF),
        in_specs=[vmem] * 6,
        out_specs=vmem,
        compiler_params=pltpu.CompilerParams(vmem_limit_bytes=32 * 2**20),
        cost_estimate=pl.CostEstimate(flops=1_000_000_000, bytes_accessed=1_500_000, transcendentals=400_000),
    )(q, k, v, own_k, own_v, keep)


def swap(value, axis):
    return lax.ppermute(value, axis, [(0, 1), (1, 0)])


def local(
    prefill_queries,
    prefill_keys,
    prefill_values,
    segments,
    decode_queries,
    decode_keys,
    decode_values,
    row_request,
    norm_gain,
    head_weight,
    allowed_tiles,
    tokens,
):
    nz, ny, nx = (lax.axis_size(a) for a in CTX)
    nctx = nz * ny * nx
    z, yl, x = (lax.axis_index(a) for a in CTX)
    yh, core = (lax.axis_index(a) for a in TP)
    me = (z * ny + yl) * nx + x
    rows = prefill_queries.shape[0]
    kv_heads = prefill_keys.shape[1] // HD
    width = prefill_queries.shape[1]
    group = width // HD // kv_heads
    half = width // 2
    steps, lines, _ = decode_queries.shape
    model = width * lax.axis_size(TP)

    requests = jnp.arange(8, dtype=jnp.int32)
    begins = jnp.sum((segments[None, :] < requests[:, None]).astype(jnp.int32), axis=1)

    own_segment = lax.dynamic_slice_in_dim(segments, me * rows, rows)
    line_of = jnp.arange(steps * lines, dtype=jnp.int32) % lines
    step_of = jnp.arange(steps * lines, dtype=jnp.int32) // lines
    request_of = jnp.tile(row_request, steps)
    own_lines = decode_keys.shape[1]
    count = 256
    slot = jnp.arange(count, dtype=jnp.int32) - rows
    key_segment = jnp.concatenate([own_segment, jnp.full((count - rows,), -1, jnp.int32)])
    keep = (request_of[:, None] == key_segment[None, :]) | (
        (line_of[:, None] == me) & (slot[None, :] >= 0) & (slot[None, :] <= step_of[:, None])
    )
    own_k = jnp.pad(decode_keys[:, 0], ((0, 16 - steps), (0, 0)))
    own_v = jnp.pad(decode_values[:, 0], ((0, 16 - steps), (0, 0)))
    state = states(
        (steps, lines, kv_heads, group),
        decode_queries.reshape(steps * lines, width),
        prefill_keys,
        prefill_values,
        own_k,
        own_v,
        keep.astype(jnp.int32),
    )
    state = state.reshape(steps, lines, width + HD).transpose(1, 0, 2)

    def mine_and_other(a, w):
        first, second = a[:, :w], a[:, w:]
        return jnp.where(yl == 0, first, second), jnp.where(yl == 0, second, first)

    k_mine, k_other = mine_and_other(prefill_keys, HD)
    v_mine, v_other = mine_and_other(prefill_values, HD)
    got = swap(jnp.stack([k_other, v_other]), "yl")

    def both(mine, other):
        return jnp.where(yl == 0, jnp.stack([mine, other]), jnp.stack([other, mine]))

    k_pair, v_pair = both(k_mine, got[0]), both(v_mine, got[1])
    kv_all = lax.all_gather(jnp.stack([k_pair, v_pair]), ("z", "x"), axis=0)
    q_mine, q_other = mine_and_other(prefill_queries, half)
    q_pair = both(q_mine, swap(q_other, "yl"))

    inside = jnp.arange(rows, dtype=jnp.int32)
    places, starts, infos = [], [], []
    for y in range(ny):
        base = ((z * ny + y) * nx + x) * rows
        place = base + inside
        segment = lax.dynamic_slice_in_dim(segments, base, rows)
        start = jnp.sum(jnp.where(segment[:, None] == requests[None, :], begins[None, :], 0), axis=1)
        places.append(place)
        starts.append(start)
        low, high = jnp.min(start), jnp.max(start)
        infos.append(
            jnp.stack([low // KT, (base + rows - 1) // KT + 1, (high + KT - 1) // KT, (base + 1) // KT])
        )
    output = attend(
        (nz, ny, nx),
        jnp.stack(infos),
        q_pair,
        jnp.stack(starts)[..., None],
        jnp.stack(places)[..., None],
        kv_all,
    )

    met = lax.all_to_all(state, CTX, 0, 0, tiled=True)
    tail = met[:, :, width:].astype(F32)
    heads = kv_heads * group
    size = tail[:, :, 0:heads] + tail[:, :, 64 : 64 + heads]
    share = jnp.exp2(size - jnp.max(size, axis=0))
    share = share / jnp.sum(share, axis=0)
    parts = met[:, :, :width].reshape(nctx, steps, heads, HD).astype(F32)
    attention = jnp.sum(parts * share[..., None], axis=0).reshape(steps, width).astype(BF)

    spread = lax.all_to_all(
        jnp.broadcast_to(attention[None], (nctx, steps, width)), CTX, 0, 0, tiled=True
    ).reshape(lines * steps, width)
    widened = spread.astype(F32)
    squares = jnp.sum(widened * widened, axis=1, keepdims=True)
    scaled = (widened * norm_gain).astype(BF)
    partial_logits = dot(scaled, head_weight)
    span = partial_logits.shape[1]

    def fold(logits, squares, axis, mine):
        wide = logits.shape[1] // 2
        first, second = logits[:, :wide], logits[:, wide:]
        high, low = two_parts(squares)
        lane = lax.broadcasted_iota(jnp.int32, (squares.shape[0], HD), 1)
        extra = jnp.where(lane == 0, high, jnp.where(lane == 1, low, jnp.zeros((), BF)))
        sent = jnp.where(mine == 0, second, first).astype(BF)
        there = swap(jnp.concatenate([sent, extra], axis=1), axis).astype(F32)
        kept = jnp.where(mine == 0, first, second)
        total = squares + there[:, wide : wide + 1] + there[:, wide + 1 : wide + 2]
        return kept + there[:, :wide], total

    logits, squares = fold(partial_logits, squares, "core", core)
    logits, squares = fold(logits, squares, "yh", yh)
    logits = lax.rsqrt(squares / model + EPS) * logits

    quarter = span // 4
    first_id = me * span + core * (span // 2) + yh * quarter
    tiles = first_id // TILE + jnp.arange(quarter // TILE, dtype=jnp.int32)
    allowed = jnp.any(allowed_tiles[..., None] == tiles, axis=2)
    allowed = allowed.transpose(1, 0, 2).reshape(lines * steps, quarter // TILE)
    wanted = tokens.T.reshape(lines * steps, 1) - first_id
    keep_ids = jnp.repeat(allowed, TILE, axis=1)
    masked = jnp.where(keep_ids, logits, FLOOR)
    top = jnp.max(masked, axis=1)
    mass = jnp.sum(jnp.where(keep_ids, jnp.exp(masked - top[:, None]), 0.0), axis=1)
    ids = jnp.arange(quarter, dtype=jnp.int32)
    target = jnp.sum(jnp.where(ids[None, :] == wanted, logits, 0.0), axis=1)

    def joined(top, mass, target, axis):
        peak = jnp.max(top, axis=axis)
        mass = jnp.sum(mass * jnp.exp(top - jnp.expand_dims(peak, axis)), axis=axis)
        return peak, mass, jnp.sum(target, axis=axis)

    stats = jnp.stack([top, mass, target], axis=-1).reshape(lines, steps * 3)
    stats = lax.all_to_all(stats, CTX, 0, 0, tiled=True).reshape(nctx, steps, 3)
    stats = jnp.stack(joined(*(stats[..., i] for i in range(3)), 0))
    stats = lax.all_gather(stats, TP, axis=0)
    top, mass, target = joined(*(stats[:, i] for i in range(3)), 0)
    result = target - (top + jnp.log(mass))

    mine, other = output[0], output[1]
    back = swap(jnp.where(yl == 0, other, mine), "yl")
    kept = jnp.where(yl == 0, mine, other)
    prefill_output = jnp.where(
        yl == 0, jnp.concatenate([kept, back], axis=1), jnp.concatenate([back, kept], axis=1)
    )
    return prefill_output, result[:, None]


def solution(mesh):
    fine = Mesh(mesh.devices.reshape(8, 2, 4, 2, 2), CTX + TP)
    placed = (
        P(CTX, TP),
        P(CTX, TP),
        P(CTX, TP),
        P(),
        P(None, None, TP),
        P(None, CTX, TP),
        P(None, CTX, TP),
        P(),
        P(TP),
        P(TP, CTX),
        P(),
        P(),
    )
    return jax.shard_map(
        local, mesh=fine, in_specs=placed, out_specs=(P(CTX, TP), P(None, CTX)), check_vma=False
    )
```

time: 1980 us -> 233 us (0.12)
  the two profiles are of different devices: /device:TPU:96 before, /device:TPU:166 now
where the time goes in v1:
time: 233 us; the launch traced here: 229 us
  Pallas kernels  80.8 us (35%)
  blocking collectives  39.7 us (17%)
  waiting for transfers between devices  38.6 us (17%)
  starting transfers between devices  27.5 us (12%)
  between operations  20.9 us (9%)
  other arithmetic  8.72 us (4%)
  local copies, waits for them, and re-layouts  8.55 us (4%)
  matrix products  3.79 us (2%)
    pallas_call x1, Pallas kernels, attend(): pl.pallas_call(functools.partial(attend_kernel, (nz, ny, nx, rows, group)...  77.5 us
    all_to_all x1, blocking collectives, local(): met = lax.all_to_all(state, CTX, 0, 0, tiled=True)  33.1 us
    ppermute x5, waiting for transfers between devices, swap(): return lax.ppermute(value, axis, [(0, 1), (1, 0)])  17.4 us
    all_to_all x1, waiting for transfers between devices, local(): lax.all_to_all(jnp.broadcast_to(attention[None], (nctx, steps, width)), C...  16.4 us
    all_to_all x1, starting transfers between devices, local(): stats = lax.all_to_all(stats, CTX, 0, 0, tiled=True).reshape(nctx, steps, 3)  10.3 us
    all_to_all x1, starting transfers between devices, local(): lax.all_to_all(jnp.broadcast_to(attention[None], (nctx, steps, width)), C...  10.2 us
    ppermute x5, starting transfers between devices, swap(): return lax.ppermute(value, axis, [(0, 1), (1, 0)])  6.97 us
    all_gather x1, blocking collectives, local(): stats = lax.all_gather(stats, TP, axis=0)  6.67 us
  transfers between devices with their start and end apart: 8, of which 5 were waited for; matrix products, arithmetic and copies ran while one was open for 6% of the time, Pallas kernels for 1%

profile of v1, /device:TPU:166, one launch (start us, length us, event | category | flops | bytes accessed | tf_op | source)
XLA Modules:
  0.0 228.6 jit_solution(8057924604520800212)
XLA Ops:
  7.3 1.0 select_bitcast_fusion.6
  8.2 0.8 select_bitcast_fusion.3
  9.1 1.7 collective-permute-start.1
  10.8 3.0 %collective-permute-done.1 = bf16[2,192,128]{2,1,0:T(8,128)(2,1)S(1)} collective-permute-done((bf16[2,192,128]{2,1,0:T(8,128)(2,1)S(1)}, bf16[2,192,128]{2,1,0:T(8,128)(2,1)S(1)}, u32[]{:S(2)}, u32[]{:S(2)}) %collective-permute-start.1) | collective-permute-done | bytes 98336 | tf_op jit(solution)/shard_map/ppermute | solution.py:173
  14.7 0.9 fusion.17
  15.8 3.3 %shard_map.132 = bf16[192,1408]{1,0:T(8,128)(2,1)S(1)} custom-call(bf16[192,1280]{1,0:T(8,128)(2,1)S(1)} %bitcast.90, bf16[192,256]{1,0:T(8,128)(2,1)S(1)} %copy-done.1, bf16[192,256]{1,0:T(8,128)(2,1)S(1)} %copy-done, bf16[16,256]{1,0:T(8,128)(2,1)S(1)} %pad.8.ok_ref, bf16[16,256]{1,0:T(8,128)(2,1)S(1)} %pad.9.ov_ref, s32[192,256]{1,0:T(8,128)S(1)} %or_convert_fusion.keep_ref), custom_call_target="tpu_custom_call" | custom-call | flops 1000000000 | bytes 1500000 | tf_op jit(solution)/shard_map/pallas_call | solution.py:162
  19.6 33.1 %all_to_all.19 = bf16[64,3,1408]{2,1,0:T(4,128)(2,1)S(1)} all-to-all(bf16[64,3,1408]{2,1,0:T(4,128)(2,1)S(1)} %bitcast.91), channel_id=1, replica_groups=mesh['z'=8,'yl'=2,'x'=4,'yh'=2,'core'=2] {'z','yl','x'}, dimensions={0} | all-to-all | bytes 1081344 | tf_op jit(solution)/shard_map/all_to_all | solution.py:268
  54.2 1.0 broadcast_in_dim.109
  55.2 10.2 %all-to-all-start.1 = ((bf16[64,3,1280]{2,1,0:T(4,128)(2,1)}), bf16[64,3,1280]{2,1,0:T(4,128)(2,1)S(1)}, u32[]{:S(2)}, u32[]{:S(2)}) async-start(bf16[64,3,1280]{2,1,0:T(4,128)(2,1)} %broadcast_in_dim.109), calls=%async_computation.1 | async-start | bytes 1310720 | tf_op jit(solution)/shard_map/all_to_all | solution.py:277
  65.4 0.7 select_bitcast_fusion.2
  66.2 1.5 collective-permute-start
  68.0 0.7 fusion.14
  68.9 16.4 %all-to-all-done.1 = bf16[64,3,1280]{2,1,0:T(4,128)(2,1)S(1)} async-done(((bf16[64,3,1280]{2,1,0:T(4,128)(2,1)}), bf16[64,3,1280]{2,1,0:T(4,128)(2,1)S(1)}, u32[]{:S(2)}, u32[]{:S(2)}) %all-to-all-start.1) | async-done | bytes 491552 | tf_op jit(solution)/shard_map/all_to_all | solution.py:277
  86.3 3.8 %fusion = f32[192,1536]{0,1:T(8,128)S(1)} fusion(bf16[1280,1536]{1,0:T(8,128)(2,1)} %param.21, f32[192,1280]{1,0:T(8,128)S(1)} %reshape.279, f32[1280]{0:T(1024)S(1)} %copy-done.7), kind=kOutput, calls=%fused_computation.8 | convolution fusion | flops 755466240 | bytes 6099968 | tf_op jit(solution)/shard_map/dot_general | solution.py:29
  98.4 3.0 %collective-permute-start.4 = (bf16[192,512]{0,1:T(8,128)(2,1)S(1)}, bf16[192,512]{0,1:T(8,128)(2,1)S(1)}, u32[]{:S(2)}, u32[]{:S(2)}) collective-permute-start(bf16[192,512]{0,1:T(8,128)(2,1)S(1)} %pad_maximum_fusion.1), channel_id=1, source_target_pairs={{0,2},{2,0},{1,3},{3,1},{4,6},{6,4},{5,7},{7,5},{8,10},{10,8},{9,1... | collective-permute-start | bytes 589832 | tf_op jit(solution)/shard_map/ppermute | solution.py:173
  101.5 7.2 %collective-permute-done.4 = bf16[192,512]{0,1:T(8,128)(2,1)S(1)} collective-permute-done((bf16[192,512]{0,1:T(8,128)(2,1)S(1)}, bf16[192,512]{0,1:T(8,128)(2,1)S(1)}, u32[]{:S(2)}, u32[]{:S(2)}) %collective-permute-start.4) | collective-permute-done | bytes 196640 | tf_op jit(solution)/shard_map/ppermute | solution.py:173
  109.2 0.7 all_to_all.14
  109.9 10.3 %all-to-all-start.2 = ((f32[64,1,9]{2,1,0:T(1,128)}), f32[64,1,9]{2,1,0:T(1,128)S(1)}, u32[]{:S(2)}, u32[]{:S(2)}) async-start(f32[64,1,9]{2,1,0:T(1,128)} %bitcast.36), calls=%async_computation.2 | async-start | bytes 65536 | tf_op jit(solution)/shard_map/all_to_all | solution.py:321
  120.3 4.8 %all-to-all-done.2 = f32[64,1,9]{2,1,0:T(1,128)S(1)} async-done(((f32[64,1,9]{2,1,0:T(1,128)}), f32[64,1,9]{2,1,0:T(1,128)S(1)}, u32[]{:S(2)}, u32[]{:S(2)}) %all-to-all-start.2) | async-done | bytes 2336 | tf_op jit(solution)/shard_map/all_to_all | solution.py:321
  125.5 6.7 %all-gather.2 = f32[4,3,3]{2,1,0:T(4,128)S(1)} all-gather(f32[1,3,3]{2,1,0:T(4,128)S(1)} %maximum_bitcast_fusion), channel_id=3, replica_groups=mesh['z'=8,'yl'=2,'x'=4,'yh'=2,'core'=2] {'yh','core'}, dimensions={0}, use_global_device_ids=true | all-gather | bytes 180 | tf_op jit(solution)/shard_map/all_gather | solution.py:323
  132.2 2.8 %copy-done.2 = bf16[64,2,192,128]{3,2,1,0:T(8,128)(2,1)S(1)} copy-done((bf16[64,2,192,128]{3,2,1,0:T(8,128)(2,1)S(1)}, bf16[64,2,192,128]{3,2,1,0:T(8,128)(2,1)}, u32[]{:S(2)}) %copy-start.2) | copy-done | bytes 6291480
  135.0 77.5 %shard_map.131 = bf16[2,192,640]{2,1,0:T(8,128)(2,1)S(1)} custom-call(s32[2,4]{1,0:T(2,128)S(1)} %pad_add_fusion.info, bf16[2,192,640]{2,1,0:T(8,128)(2,1)S(1)} %maximum_select_fusion.q_ref, s32[2,192,1]{2,1,0:T(8,128)S(1)} %copy.48.start_ref, s32[2,192,1]{2,1,0:T(8,128)S(1)} %copy.49.place_ref, bf16[32,2,2,192,128]{4,3,2,1,0:T(8,128)(2,1)S(1)} %bitcast.89), custom_call_target="tpu_custom_call" | custom-call | flops 20000000000 | bytes 8000000 | tf_op jit(solution)/shard_map/pallas_call | solution.py:109
  213.7 7.1 %collective-permute-done.2 = bf16[192,640]{1,0:T(8,128)(2,1)S(1)} collective-permute-done((bf16[192,640]{1,0:T(8,128)(2,1)S(1)}, bf16[192,640]{1,0:T(8,128)(2,1)S(1)}, u32[]{:S(2)}, u32[]{:S(2)}) %collective-permute-start.2) | collective-permute-done | bytes 245792 | tf_op jit(solution)/shard_map/ppermute | solution.py:173
  220.8 0.9 maximum_select_fusion.1
  (110 shorter events, 8.6 us)
Async XLA Ops:
  7.2 8.6 %copy-start.1 = (bf16[192,256]{1,0:T(8,128)(2,1)S(1)}, bf16[192,256]{1,0:T(8,128)(2,1)}, u32[]{:S(2)}) copy-start(bf16[192,256]{1,0:T(8,128)(2,1)} %k_ref.1) | copy-start | bytes 294916
  7.2 8.6 %copy-start = (bf16[192,256]{1,0:T(8,128)(2,1)S(1)}, bf16[192,256]{1,0:T(8,128)(2,1)}, u32[]{:S(2)}) copy-start(bf16[192,256]{1,0:T(8,128)(2,1)} %v_ref.1) | copy-start | bytes 294916
  7.2 7.4 %copy-start.15 = (s32[64]{0:T(128)S(1)}, s32[64]{0:T(128)}, u32[]{:S(2)}) copy-start(s32[64]{0:T(128)} %param.19) | copy-start | bytes 772
  7.2 7.5 %copy-start.13 = (bf16[3,1,256]{2,0,1:T(4,128)(2,1)S(1)}, bf16[3,1,256]{2,0,1:T(4,128)(2,1)}, u32[]{:S(2)}) copy-start(bf16[3,1,256]{2,0,1:T(4,128)(2,1)} %param.17) | copy-start | bytes 4612
  7.2 7.5 %copy-start.14 = (bf16[3,1,256]{2,0,1:T(4,128)(2,1)S(1)}, bf16[3,1,256]{2,0,1:T(4,128)(2,1)}, u32[]{:S(2)}) copy-start(bf16[3,1,256]{2,0,1:T(4,128)(2,1)} %param.18) | copy-start | bytes 4612
  7.2 8.6 %copy-start.3 = (bf16[3,64,1280]{2,1,0:T(8,128)(2,1)S(1)}, bf16[3,64,1280]{2,1,0:T(8,128)(2,1)}, u32[]{:S(2)}) copy-start(bf16[3,64,1280]{2,1,0:T(8,128)(2,1)} %param.16) | copy-start | bytes 1474564
  7.2 125.0 %all-gather.5.cloned.1.call-start = ((), (), s32[]{:S(2)}) async-start(), calls=%async_computation.3 | async-start | bytes 6488064 | tf_op jit(solution)/shard_map/all_gather | solution.py:242
  9.1 4.7 %collective-permute-start.1 = (bf16[2,192,128]{2,1,0:T(8,128)(2,1)S(1)}, bf16[2,192,128]{2,1,0:T(8,128)(2,1)S(1)}, u32[]{:S(2)}, u32[]{:S(2)}) collective-permute-start(bf16[2,192,128]{2,1,0:T(8,128)(2,1)S(1)} %pad_maximum_fusion.3), channel_id=1, source_target_pairs={{0,16},{16,0},{1,17},{17,1},{2,18},{18,2},{3,19},{19,3},{4,20},{20... | collective-permute-start | bytes 294920 | tf_op jit(solution)/shard_map/ppermute | solution.py:173
  54.0 11.4 %copy-start.4 = (bf16[192,1280]{1,0:T(8,128)(2,1)S(1)}, bf16[192,1280]{1,0:T(8,128)(2,1)}, u32[]{:S(2)}) copy-start(bf16[192,1280]{1,0:T(8,128)(2,1)} %param.12) | copy-start | bytes 1474564
  54.2 13.5 %copy-start.5 = (s32[12288]{0:T(1024)S(1)}, s32[12288]{0:T(1024)}, u32[]{:S(2)}) copy-start(s32[12288]{0:T(1024)} %param.15) | copy-start | bytes 147460
  54.2 14.6 %copy-start.6 = (s32[3,64,32]{1,2,0:T(8,128)S(1)}, s32[3,64,32]{1,2,0:T(8,128)}, u32[]{:S(2)}) copy-start(s32[3,64,32]{1,2,0:T(8,128)} %param.22) | copy-start | bytes 73732
  54.2 14.7 %copy-start.12 = (s32[3,64]{1,0:T(4,128)S(1)}, s32[3,64]{1,0:T(4,128)}, u32[]{:S(2)}) copy-start(s32[3,64]{1,0:T(4,128)} %param.23) | copy-start | bytes 2308
  55.2 30.0 %all-to-all-start.1 = ((bf16[64,3,1280]{2,1,0:T(4,128)(2,1)}), bf16[64,3,1280]{2,1,0:T(4,128)(2,1)S(1)}, u32[]{:S(2)}, u32[]{:S(2)}) async-start(bf16[64,3,1280]{2,1,0:T(4,128)(2,1)} %broadcast_in_dim.109), calls=%async_computation.1 | async-start | bytes 1310720 | tf_op jit(solution)/shard_map/all_to_all | solution.py:277
  65.4 20.9 %copy-start.7 = (f32[1280]{0:T(1024)S(1)}, f32[1280]{0:T(1024)}, u32[]{:S(2)}) copy-start(f32[1280]{0:T(1024)} %param.20) | copy-start | bytes 15364
  66.2 54.0 %collective-permute-start = (bf16[192,640]{1,0:T(8,128)(2,1)}, bf16[192,640]{1,0:T(8,128)(2,1)S(1)}, u32[]{:S(2)}, u32[]{:S(2)}) collective-permute-start(bf16[192,640]{1,0:T(8,128)(2,1)} %get-tuple-element.24), channel_id=1, source_target_pairs={{0,16},{16,0},{1,17},{17,1},{2,18},{18,2},{3,19},{19,3},{4,20},{20... | collective-permute-start | bytes 737288 | tf_op jit(solution)/shard_map/ppermute | solution.py:173
  67.7 22.5 %copy-start.8 = (pred[128]{0:T(512)(128)(4,1)}, pred[128]{0:T(512)(128)(4,1)S(1)}, u32[]{:S(2)}) copy-start(pred[128]{0:T(512)(128)(4,1)S(1)} %get-tuple-element.44) | copy-start | bytes 388
  67.7 22.5 %copy-start.10 = (pred[128]{0:T(512)(128)(4,1)}, pred[128]{0:T(512)(128)(4,1)S(1)}, u32[]{:S(2)}) copy-start(pred[128]{0:T(512)(128)(4,1)S(1)} %get-tuple-element.45) | copy-start | bytes 388
  90.2 7.8 %copy-start.9 = (pred[128]{0:T(512)(128)(4,1)S(1)}, pred[128]{0:T(512)(128)(4,1)}, u32[]{:S(2)}) copy-start(pred[128]{0:T(512)(128)(4,1)} %copy-done.8) | copy-start | bytes 388
  90.3 7.8 %copy-start.11 = (pred[128]{0:T(512)(128)(4,1)S(1)}, pred[128]{0:T(512)(128)(4,1)}, u32[]{:S(2)}) copy-start(pred[128]{0:T(512)(128)(4,1)} %copy-done.10) | copy-start | bytes 388
  90.3 7.6 %collective-permute-start.3 = (bf16[192,896]{0,1:T(8,128)(2,1)S(1)}, bf16[192,896]{0,1:T(8,128)(2,1)S(1)}, u32[]{:S(2)}, u32[]{:S(2)}) collective-permute-start(bf16[192,896]{0,1:T(8,128)(2,1)S(1)} %pad_maximum_fusion), channel_id=1, source_target_pairs={{0,1},{1,0},{2,3},{3,2},{4,5},{5,4},{6,7},{7,6},{8,9},{9,8},{10,11... | collective-permute-start | bytes 1032200 | tf_op jit(solution)/shard_map/ppermute | solution.py:173
  98.4 10.3 %collective-permute-start.4 = (bf16[192,512]{0,1:T(8,128)(2,1)S(1)}, bf16[192,512]{0,1:T(8,128)(2,1)S(1)}, u32[]{:S(2)}, u32[]{:S(2)}) collective-permute-start(bf16[192,512]{0,1:T(8,128)(2,1)S(1)} %pad_maximum_fusion.1), channel_id=1, source_target_pairs={{0,2},{2,0},{1,3},{3,1},{4,6},{6,4},{5,7},{7,5},{8,10},{10,8},{9,1... | collective-permute-start | bytes 589832 | tf_op jit(solution)/shard_map/ppermute | solution.py:173
  109.9 15.2 %all-to-all-start.2 = ((f32[64,1,9]{2,1,0:T(1,128)}), f32[64,1,9]{2,1,0:T(1,128)S(1)}, u32[]{:S(2)}, u32[]{:S(2)}) async-start(f32[64,1,9]{2,1,0:T(1,128)} %bitcast.36), calls=%async_computation.2 | async-start | bytes 65536 | tf_op jit(solution)/shard_map/all_to_all | solution.py:321
  132.2 2.8 %copy-start.2 = (bf16[64,2,192,128]{3,2,1,0:T(8,128)(2,1)S(1)}, bf16[64,2,192,128]{3,2,1,0:T(8,128)(2,1)}, u32[]{:S(2)}) copy-start(bf16[64,2,192,128]{3,2,1,0:T(8,128)(2,1)} %all-gather.5.cloned.1.call-done) | copy-start | bytes 18874372
  212.6 8.3 %collective-permute-start.2 = (bf16[192,640]{1,0:T(8,128)(2,1)S(1)}, bf16[192,640]{1,0:T(8,128)(2,1)S(1)}, u32[]{:S(2)}, u32[]{:S(2)}) collective-permute-start(bf16[192,640]{1,0:T(8,128)(2,1)S(1)} %get-tuple-element.22), channel_id=1, source_target_pairs={{0,16},{16,0},{1,17},{17,1},{2,18},{18,2},{3,19},{19,3},{4,20},{20... | collective-permute-start | bytes 737288 | tf_op jit(solution)/shard_map/ppermute | solution.py:173
Sparse Core Ops, SparseCore 0:
  14.7 94.7 all-gather.4

commit v2 on v1

--- a/solution.py
+++ b/solution.py
@@ -18,7 +18,8 @@
 F32 = jnp.float32
 CTX = ("z", "yl", "x")
 TP = ("yh", "core")
-KT = 512
+CHUNK = 320
+REQUESTS = 8
 
 
 def dot_t(a, b):
@@ -34,96 +35,130 @@
     return high, (value - high.astype(F32)).astype(BF)
 
 
-def attend_kernel(
-    shape, info, q_ref, start_ref, place_ref, kv_hbm, out_ref, keys, vals, qs, peak, acc, sem
-):
-    nz, ny, nx, rows, group = shape
-    copies = []
-    for z in range(nz):
-        for x in range(nx):
-            for y in range(ny):
-                there = pl.ds(((z * ny + y) * nx + x) * rows, rows)
-                k, v = kv_hbm.at[z * nx + x, 0, y], kv_hbm.at[z * nx + x, 1, y]
-                copies.append(pltpu.make_async_copy(k, keys.at[there, 0:HD], sem))
-                copies.append(pltpu.make_async_copy(k, keys.at[there, HD : 2 * HD], sem))
-                copies.append(pltpu.make_async_copy(v, vals.at[there, 0:HD], sem))
-    for copy in copies:
-        copy.start()
-    scale = HD**-0.5 * LOG2E
-    for tile in range(ny):
+def bound(plan, at, big):
+    return functools.reduce(
+        jnp.minimum, [jnp.where(plan[2 + i] > at, plan[2 + i], big) for i in range(REQUESTS)]
+    )
+
+
+def attend_kernel(plan, q_ref, row_ref, k_ref, v_ref, out_ref, qs, peak, acc):
+    rows, width = q_ref.shape
+    group = width // HD
+    keys = k_ref.shape[1] * rows
+    step = pl.program_id(0)
+    first_row = plan[1]
+
+    @pl.when(step == 0)
+    def _():
         for h in range(group):
-            q = q_ref[tile, :, h * HD : (h + 1) * HD].astype(F32) * scale
+            q = q_ref[:, h * HD : (h + 1) * HD].astype(F32) * (HD**-0.5 * LOG2E)
             high, low = two_parts(q)
-            qs[tile, h, :, 0:HD] = high
-            qs[tile, h, :, HD : 2 * HD] = low
-    vals[:, HD : 2 * HD] = jnp.ones((vals.shape[0], HD), BF)
-    for copy in copies:
-        copy.wait()
-    for tile in range(ny):
-        first, last, inner_first, inner_last = (info[tile, i] for i in range(4))
+            qs[h * rows : (h + 1) * rows, 0:HD] = high
+            qs[h * rows : (h + 1) * rows, HD:] = low
         peak[...] = jnp.full(peak.shape, FLOOR, F32)
         acc[...] = jnp.zeros(acc.shape, F32)
 
-        def step(turn, masked):
-            base = pl.multiple_of(turn * KT, KT)
-            k = keys[pl.ds(base, KT), :]
-            v = vals[pl.ds(base, KT), :]
+    base = (plan[0] + step) * keys
+
+    def part(masked):
+        block = (keys, HD)
+        k = k_ref[0, :, 0, 0].reshape(block).T
+        k = jnp.concatenate([k, k], axis=0)
+        v = jnp.concatenate([v_ref[0, :, 0, 0].reshape(block), jnp.ones(block, BF)], axis=1)
+        if masked:
+            at = base + lax.broadcasted_iota(jnp.int32, (1, keys), 1)
+            end = bound(plan, at, 2**30) - first_row
+            at = at - first_row
+        count = qs.shape[0] // CHUNK
+        ahead = dot(qs[0:CHUNK], k)
+        for i in range(count):
+            s = ahead
+            if i + 1 < count:
+                ahead = dot(qs[(i + 1) * CHUNK : (i + 2) * CHUNK], k)
+            here = slice(i * CHUNK, (i + 1) * CHUNK)
             if masked:
-                at = base + lax.broadcasted_iota(jnp.int32, (rows, KT), 1)
-                keep = (at >= start_ref[tile]) & (at <= place_ref[tile])
-            for h in range(group):
-                s = dot_t(qs[tile, h], k)
-                if masked:
-                    s = jnp.where(keep, s, BELOW)
-                old = peak[h]
-                new = jnp.maximum(old, jnp.max(s, axis=1, keepdims=True))
-                peak[h] = new
-                p = jnp.exp2(s - new).astype(BF)
-                acc[h] = acc[h] * jnp.exp2(old - new) + dot(p, v)
-
-        def turn_of(turn, _):
-            inside = (turn >= inner_first) & (turn < inner_last)
-
-            @pl.when(inside)
-            def _():
-                step(turn, False)
-
-            @pl.when(jnp.logical_not(inside))
-            def _():
-                step(turn, True)
-
-            return 0
-
-        lax.fori_loop(first, last, turn_of, 0)
+                row = row_ref[here]
+                s = jnp.where((at <= row) & (row < end), s, BELOW)
+            old = peak[here]
+            new = jnp.maximum(old, jnp.max(s, axis=1, keepdims=True))
+            peak[here] = new
+            p = jnp.exp2(s - new).astype(BF)
+            acc[here] = acc[here] * jnp.exp2(old - new) + dot(p, v)
+
+    last = base + keys - 1
+    last_row = first_row + rows - 1
+    need = (bound(plan, last, 2**30) > first_row) & (base <= last_row)
+    inside = (last <= first_row) & (bound(plan, base, 2**30) > last_row)
+    pl.when(need & inside)(functools.partial(part, False))
+    pl.when(need & jnp.logical_not(inside))(functools.partial(part, True))
+
+    @pl.when(step == pl.num_programs(0) - 1)
+    def _():
         for h in range(group):
-            out_ref[tile, :, h * HD : (h + 1) * HD] = (acc[h, :, 0:HD] / acc[h, :, HD : 2 * HD]).astype(BF)
-
-
-def attend(sizes, info, q, start, place, kv):
-    nz, ny, nx = sizes
-    rows, width = q.shape[1], q.shape[2]
-    group = width // HD
-    total = nz * ny * nx * rows
+            here = slice(h * rows, (h + 1) * rows)
+            out_ref[:, h * HD : (h + 1) * HD] = (acc[here, 0:HD] / acc[here, HD:]).astype(BF)
+
+
+def attend(plan, q, row, kv):
+    rows, width = q.shape
+    nz, nx, _, ny, _, _ = kv.shape
+
+    def whole(shape):
+        return pl.BlockSpec(shape, lambda i, plan: (0,) * len(shape))
+
+    def tiles(kind):
+        def index(i, plan):
+            at = jnp.minimum(plan[0] + i, (plan[1] + rows - 1) // (nx * rows))
+            return (at // ny, 0, kind, at % ny, 0, 0)
+
+        return pl.BlockSpec((1, nx, 1, 1, rows, HD), index)
+
+    flat = width // HD * rows
+    return pl.pallas_call(
+        attend_kernel,
+        out_shape=jax.ShapeDtypeStruct(q.shape, BF),
+        grid_spec=pltpu.PrefetchScalarGridSpec(
+            num_scalar_prefetch=1,
+            grid=(nz * ny,),
+            in_specs=[whole(q.shape), whole(row.shape), tiles(0), tiles(1)],
+            out_specs=whole(q.shape),
+            scratch_shapes=[
+                pltpu.VMEM((flat, 2 * HD), BF),
+                pltpu.VMEM((flat, 1), F32),
+                pltpu.VMEM((flat, 2 * HD), F32),
+            ],
+        ),
+        compiler_params=pltpu.CompilerParams(
+            vmem_limit_bytes=24 * 2**20, dimension_semantics=("arbitrary",)
+        ),
+        cost_estimate=pl.CostEstimate(
+            flops=15_000_000_000, bytes_accessed=8_000_000, transcendentals=5_000_000
+        ),
+    )(plan, q, row, kv, kv)
+
+
+def merge_kernel(met_ref, out_ref):
+    width = out_ref.shape[2]
+    tail = met_ref[:, :, width:].astype(F32)
+    size = tail + pltpu.roll(tail, HD // 2, 2)
+    share = jnp.exp2(size - jnp.max(size, axis=0, keepdims=True))
+    share = share / jnp.sum(share, axis=0, keepdims=True)
+    for h in range(width // HD):
+        here = slice(h * HD, (h + 1) * HD)
+        total = jnp.sum(met_ref[:, :, here].astype(F32) * share[:, :, h : h + 1], axis=0, keepdims=True)
+        out_ref[:, :, here] = jnp.broadcast_to(total.astype(BF), (out_ref.shape[0], out_ref.shape[1], HD))
+
+
+def merge(met):
     vmem = pl.BlockSpec(memory_space=pltpu.VMEM)
-    hbm = pl.BlockSpec(memory_space=pl.ANY)
     return pl.pallas_call(
-        functools.partial(attend_kernel, (nz, ny, nx, rows, group)),
-        out_shape=jax.ShapeDtypeStruct(q.shape, BF),
-        in_specs=[pl.BlockSpec(memory_space=pltpu.SMEM), vmem, vmem, vmem, hbm],
+        merge_kernel,
+        out_shape=jax.ShapeDtypeStruct((met.shape[0], met.shape[1], met.shape[2] - HD), BF),
+        in_specs=[vmem],
         out_specs=vmem,
-        scratch_shapes=[
-            pltpu.VMEM((total, 2 * HD), BF),
-            pltpu.VMEM((total, 2 * HD), BF),
-            pltpu.VMEM((ny, group, rows, 2 * HD), BF),
-            pltpu.VMEM((group, rows, 1), F32),
-            pltpu.VMEM((group, rows, 2 * HD), F32),
-            pltpu.SemaphoreType.DMA,
-        ],
-        compiler_params=pltpu.CompilerParams(vmem_limit_bytes=40 * 2**20),
-        cost_estimate=pl.CostEstimate(
-            flops=20_000_000_000, bytes_accessed=8_000_000, transcendentals=17_000_000
-        ),
-    )(info, q, start, place, kv)
+        compiler_params=pltpu.CompilerParams(vmem_limit_bytes=16 * 2**20),
+        cost_estimate=pl.CostEstimate(flops=500_000_000, bytes_accessed=1_500_000, transcendentals=0),
+    )(met)
 
 
 def state_kernel(shape, q_ref, k_ref, v_ref, ok_ref, ov_ref, keep_ref, out_ref):
@@ -164,9 +199,13 @@
         out_shape=jax.ShapeDtypeStruct((q.shape[0], q.shape[1] + HD), BF),
         in_specs=[vmem] * 6,
         out_specs=vmem,
-        compiler_params=pltpu.CompilerParams(vmem_limit_bytes=32 * 2**20),
-        cost_estimate=pl.CostEstimate(flops=1_000_000_000, bytes_accessed=1_500_000, transcendentals=400_000),
+        compiler_params=pltpu.CompilerParams(vmem_limit_bytes=16 * 2**20),
+        cost_estimate=pl.CostEstimate(flops=4_000_000_000, bytes_accessed=1_500_000, transcendentals=400_000),
     )(q, k, v, own_k, own_v, keep)
+
+
+def after(values):
+    return lax.optimization_barrier(values)
 
 
 def swap(value, axis):
@@ -200,7 +239,7 @@
     steps, lines, _ = decode_queries.shape
     model = width * lax.axis_size(TP)
 
-    requests = jnp.arange(8, dtype=jnp.int32)
+    requests = jnp.arange(REQUESTS, dtype=jnp.int32)
     begins = jnp.sum((segments[None, :] < requests[:, None]).astype(jnp.int32), axis=1)
 
     own_segment = lax.dynamic_slice_in_dim(segments, me * rows, rows)
@@ -233,50 +272,33 @@
 
     k_mine, k_other = mine_and_other(prefill_keys, HD)
     v_mine, v_other = mine_and_other(prefill_values, HD)
-    got = swap(jnp.stack([k_other, v_other]), "yl")
-
-    def both(mine, other):
-        return jnp.where(yl == 0, jnp.stack([mine, other]), jnp.stack([other, mine]))
-
-    k_pair, v_pair = both(k_mine, got[0]), both(v_mine, got[1])
-    kv_all = lax.all_gather(jnp.stack([k_pair, v_pair]), ("z", "x"), axis=0)
-    q_mine, q_other = mine_and_other(prefill_queries, half)
-    q_pair = both(q_mine, swap(q_other, "yl"))
-
-    inside = jnp.arange(rows, dtype=jnp.int32)
-    places, starts, infos = [], [], []
-    for y in range(ny):
-        base = ((z * ny + y) * nx + x) * rows
-        place = base + inside
-        segment = lax.dynamic_slice_in_dim(segments, base, rows)
-        start = jnp.sum(jnp.where(segment[:, None] == requests[None, :], begins[None, :], 0), axis=1)
-        places.append(place)
-        starts.append(start)
-        low, high = jnp.min(start), jnp.max(start)
-        infos.append(
-            jnp.stack([low // KT, (base + rows - 1) // KT + 1, (high + KT - 1) // KT, (base + 1) // KT])
-        )
-    output = attend(
-        (nz, ny, nx),
-        jnp.stack(infos),
-        q_pair,
-        jnp.stack(starts)[..., None],
-        jnp.stack(places)[..., None],
-        kv_all,
-    )
+    kv_mine = jnp.stack([k_mine, v_mine])
+    kv_got = swap(jnp.stack([k_other, v_other]), "yl")
+    kv_pair = jnp.where(yl == 0, jnp.stack([kv_mine, kv_got], 1), jnp.stack([kv_got, kv_mine], 1))
+    kv_pair, state = after((kv_pair, state))
+    kv_all = lax.all_gather(kv_pair, ("z", "x"), axis=0)
+    kv_all = kv_all.reshape((nz, nx) + kv_pair.shape)
 
     met = lax.all_to_all(state, CTX, 0, 0, tiled=True)
-    tail = met[:, :, width:].astype(F32)
-    heads = kv_heads * group
-    size = tail[:, :, 0:heads] + tail[:, :, 64 : 64 + heads]
-    share = jnp.exp2(size - jnp.max(size, axis=0))
-    share = share / jnp.sum(share, axis=0)
-    parts = met[:, :, :width].reshape(nctx, steps, heads, HD).astype(F32)
-    attention = jnp.sum(parts * share[..., None], axis=0).reshape(steps, width).astype(BF)
-
-    spread = lax.all_to_all(
-        jnp.broadcast_to(attention[None], (nctx, steps, width)), CTX, 0, 0, tiled=True
-    ).reshape(lines * steps, width)
+    attention = merge(met)
+    spread = lax.all_to_all(attention, CTX, 0, 0, tiled=True).reshape(lines * steps, width)
+
+    def mirror(value):
+        return lax.ppermute(value, "z", [(i, nz - 1 - i) for i in range(nz)])
+
+    q_own, _ = after((prefill_queries, attention))
+    q_mine, q_other = mine_and_other(q_own, half)
+    q_near, q_far = swap(q_other, "yl"), mirror(q_mine)
+    row = jnp.tile(jnp.arange(rows, dtype=jnp.int32), group)[:, None]
+
+    def plan_of(block):
+        first_row = block * rows
+        start = jnp.max(jnp.where(begins <= first_row, begins, 0))
+        return jnp.concatenate([jnp.stack([start // (nx * rows), first_row]), begins])
+
+    near_plan = plan_of((z * ny + 1 - yl) * nx + x)
+    far_plan = plan_of(((nz - 1 - z) * ny + yl) * nx + x)
+
     widened = spread.astype(F32)
     squares = jnp.sum(widened * widened, axis=1, keepdims=True)
     scaled = (widened * norm_gain).astype(BF)
@@ -318,17 +340,21 @@
         return peak, mass, jnp.sum(target, axis=axis)
 
     stats = jnp.stack([top, mass, target], axis=-1).reshape(lines, steps * 3)
-    stats = lax.all_to_all(stats, CTX, 0, 0, tiled=True).reshape(nctx, steps, 3)
+    q_far, q_near, stats = after((q_far, q_near, stats))
+    far = attend(far_plan, q_far, row, kv_all)
+    near = attend(near_plan, q_near, row, kv_all)
+    out_mine, out_other = mirror(far), swap(near, "yl")
+    stats, _, _ = after((lax.all_to_all(stats, CTX, 0, 0, tiled=True), far, near))
+    stats = stats.reshape(nctx, steps, 3)
     stats = jnp.stack(joined(*(stats[..., i] for i in range(3)), 0))
     stats = lax.all_gather(stats, TP, axis=0)
     top, mass, target = joined(*(stats[:, i] for i in range(3)), 0)
     result = target - (top + jnp.log(mass))
 
-    mine, other = output[0], output[1]
-    back = swap(jnp.where(yl == 0, other, mine), "yl")
-    kept = jnp.where(yl == 0, mine, other)
     prefill_output = jnp.where(
-        yl == 0, jnp.concatenate([kept, back], axis=1), jnp.concatenate([back, kept], axis=1)
+        yl == 0,
+        jnp.concatenate([out_mine, out_other], axis=1),
+        jnp.concatenate([out_other, out_mine], axis=1),
     )
     return prefill_output, result[:, None]
 

time: 233 us -> 186 us (0.80)
  the two profiles are of different devices: /device:TPU:166 before, /device:TPU:193 now
where the time goes in v2:
time: 186 us; the launch traced here: 185 us
  starting transfers between devices  49.1 us (26%)
  blocking collectives  37.5 us (20%)
  Pallas kernels  31.5 us (17%)
  waiting for transfers between devices  26.8 us (14%)
  between operations  18.1 us (10%)
  local copies, waits for them, and re-layouts  11.8 us (6%)
  other arithmetic  6.15 us (3%)
  matrix products  3.84 us (2%)
    all_to_all x1, blocking collectives, local(): met = lax.all_to_all(state, CTX, 0, 0, tiled=True)  28.5 us
    pallas_call x2, Pallas kernels, attend(): pl.pallas_call(attend_kernel, out_shape=jax.ShapeDtypeStruct(q.shape, BF)...  26.4 us
    ppermute x2, starting transfers between devices, mirror(): return lax.ppermute(value, 'z', [(i, nz - 1 - i) for i in range(nz)])  16 us
    all_to_all x1, waiting for transfers between devices, local(): lax.all_to_all(attention, CTX, 0, 0, tiled=True)  15.4 us
    all_to_all x1, starting transfers between devices, local(): lax.all_to_all(stats, CTX, 0, 0, tiled=True)  11.4 us
    ppermute x5, starting transfers between devices, swap(): return lax.ppermute(value, axis, [(0, 1), (1, 0)])  11.1 us
    all_to_all x1, starting transfers between devices, local(): lax.all_to_all(attention, CTX, 0, 0, tiled=True)  10.6 us
    all_gather x1, blocking collectives, local(): stats = lax.all_gather(stats, TP, axis=0)  9.04 us
  transfers between devices with their start and end apart: 10, of which 3 were waited for; matrix products, arithmetic and copies ran while one was open for 9% of the time, Pallas kernels for 17%

profile of v2, /device:TPU:193, one launch (start us, length us, event | category | flops | bytes accessed | tf_op | source)
XLA Modules:
  0.0 184.9 jit_solution(3023903881740776497)
XLA Ops:
  7.2 0.9 select_bitcast_fusion.2
  8.1 1.4 collective-permute-start
  13.5 0.9 copy-done.1
  14.4 1.0 copy-done.2
  15.4 3.3 %shard_map.131 = bf16[192,1408]{1,0:T(8,128)(2,1)S(1)} custom-call(bf16[192,1280]{1,0:T(8,128)(2,1)S(1)} %bitcast.72, bf16[192,256]{1,0:T(8,128)(2,1)S(1)} %copy-done.1, bf16[192,256]{1,0:T(8,128)(2,1)S(1)} %copy-done, bf16[16,256]{1,0:T(8,128)(2,1)S(1)} %pad.8.ok_ref, bf16[16,256]{1,0:T(8,128)(2,1)S(1)} %pad.9.ov_ref, s32[192,256]{1,0:T(8,128)S(1)} %or_convert_fusion.keep_ref), custom_call_target="tpu_custom_call" | custom-call | flops 4000000000 | bytes 1500000 | tf_op jit(solution)/shard_map/pallas_call | solution.py:197
  20.0 28.5 %all_to_all.22.met_ref = bf16[64,3,1408]{2,1,0:T(4,128)(2,1)S(1)} all-to-all(bf16[64,3,1408]{2,1,0:T(4,128)(2,1)S(1)} %bitcast.73), channel_id=1, replica_groups=mesh['z'=8,'yl'=2,'x'=4,'yh'=2,'core'=2] {'z','yl','x'}, dimensions={0} | all-to-all | bytes 1081344 | tf_op jit(solution)/shard_map/all_to_all | solution.py:282
  48.4 1.9 %shard_map.132 = bf16[64,3,1280]{2,1,0:T(4,128)(2,1)} custom-call(bf16[64,3,1408]{2,1,0:T(4,128)(2,1)S(1)} %all_to_all.22.met_ref), custom_call_target="tpu_custom_call" | custom-call | flops 500000000 | bytes 1500000 | tf_op jit(solution)/shard_map/pallas_call | solution.py:154
  50.3 10.6 %all-to-all-start.1 = ((bf16[64,3,1280]{2,1,0:T(4,128)(2,1)}), bf16[64,3,1280]{2,1,0:T(4,128)(2,1)S(1)}, u32[]{:S(2)}, u32[]{:S(2)}) async-start(bf16[64,3,1280]{2,1,0:T(4,128)(2,1)} %shard_map.132), calls=%async_computation.1 | async-start | bytes 1310720 | tf_op jit(solution)/shard_map/all_to_all | solution.py:284
  61.3 15.4 %all-to-all-done.1 = bf16[64,3,1280]{2,1,0:T(4,128)(2,1)S(1)} async-done(((bf16[64,3,1280]{2,1,0:T(4,128)(2,1)}), bf16[64,3,1280]{2,1,0:T(4,128)(2,1)S(1)}, u32[]{:S(2)}, u32[]{:S(2)}) %all-to-all-start.1) | async-done | bytes 491552 | tf_op jit(solution)/shard_map/all_to_all | solution.py:284
  77.8 3.8 %fusion = f32[192,1536]{0,1:T(8,128)S(1)} fusion(bf16[1280,1536]{1,0:T(8,128)(2,1)} %param.21, f32[192,1280]{1,0:T(8,128)S(1)} %reshape.138, f32[1280]{0:T(1024)S(1)} %copy-done.6), kind=kOutput, calls=%fused_computation.7 | convolution fusion | flops 755466240 | bytes 6099968 | tf_op jit(solution)/shard_map/dot_general | solution.py:30
  81.8 4.2 %collective-permute-start.3 = (bf16[192,896]{0,1:T(8,128)(2,1)S(1)}, bf16[192,896]{0,1:T(8,128)(2,1)S(1)}, u32[]{:S(2)}, u32[]{:S(2)}) collective-permute-start(bf16[192,896]{0,1:T(8,128)(2,1)S(1)} %pad_maximum_fusion), channel_id=1, source_target_pairs={{0,1},{1,0},{2,3},{3,2},{4,5},{5,4},{6,7},{7,6},{8,9},{9,8},{10,11... | collective-permute-start | bytes 1032200 | tf_op jit(solution)/shard_map/ppermute | solution.py:212
  92.0 3.0 %collective-permute-start.4 = (bf16[192,512]{0,1:T(8,128)(2,1)S(1)}, bf16[192,512]{0,1:T(8,128)(2,1)S(1)}, u32[]{:S(2)}, u32[]{:S(2)}) collective-permute-start(bf16[192,512]{0,1:T(8,128)(2,1)S(1)} %pad_maximum_fusion.1), channel_id=1, source_target_pairs={{0,2},{2,0},{1,3},{3,1},{4,6},{6,4},{5,7},{7,5},{8,10},{10,8},{9,1... | collective-permute-start | bytes 589832 | tf_op jit(solution)/shard_map/ppermute | solution.py:212
  95.1 2.4 %collective-permute-start.1 = (bf16[192,640]{1,0:T(8,128)(2,1)S(1)}, bf16[192,640]{1,0:T(8,128)(2,1)S(1)}, u32[]{:S(2)}, u32[]{:S(2)}) collective-permute-start(bf16[192,640]{1,0:T(8,128)(2,1)S(1)} %get-tuple-element.32), channel_id=1, source_target_pairs={{0,224},{32,192},{64,160},{96,128},{128,96},{160,64},{192,32},{224... | collective-permute-start | bytes 737288 | tf_op jit(solution)/shard_map/ppermute | solution.py:287
  97.4 1.2 collective-permute-start.2
  98.6 3.1 %collective-permute-done.4 = bf16[192,512]{0,1:T(8,128)(2,1)S(1)} collective-permute-done((bf16[192,512]{0,1:T(8,128)(2,1)S(1)}, bf16[192,512]{0,1:T(8,128)(2,1)S(1)}, u32[]{:S(2)}, u32[]{:S(2)}) %collective-permute-start.4) | collective-permute-done | bytes 196640 | tf_op jit(solution)/shard_map/ppermute | solution.py:212
  102.9 8.2 %collective-permute-done.1.q_ref = bf16[192,640]{1,0:T(8,128)(2,1)S(1)} collective-permute-done((bf16[192,640]{1,0:T(8,128)(2,1)S(1)}, bf16[192,640]{1,0:T(8,128)(2,1)S(1)}, u32[]{:S(2)}, u32[]{:S(2)}) %collective-permute-start.1) | collective-permute-done | bytes 245792 | tf_op jit(solution)/shard_map/ppermute | solution.py:287
  111.1 11.4 %all-to-all-start.2 = ((f32[64,1,9]{2,1,0:T(1,128)}), f32[64,1,9]{2,1,0:T(1,128)S(1)}, u32[]{:S(2)}, u32[]{:S(2)}) async-start(f32[64,1,9]{2,1,0:T(1,128)} %bitcast.23), calls=%async_computation.2 | async-start | bytes 65536 | tf_op jit(solution)/shard_map/all_to_all | solution.py:347
  122.5 3.2 %copy.58 = bf16[64,2,192,128]{3,2,1,0:T(8,128)(2,1)S(1)} copy(bf16[64,2,192,128]{3,2,0,1:T(8,128)(2,1)} %all-gather.5.cloned.1.call-done) | data formatting | bytes 12582912 | tf_op jit(solution)/shard_map/all_gather | solution.py:279
  125.8 6.2 %shard_map.133 = bf16[192,640]{1,0:T(8,128)(2,1)S(1)} custom-call(s32[10]{0:T(128)S(1)} %get-tuple-element.41.plan, bf16[192,640]{1,0:T(8,128)(2,1)S(1)} %collective-permute-done.1.q_ref, s32[960,1]{1,0:T(8,128)S(1)} %broadcast_in_dim_tile.7.row_ref, bf16[8,4,2,2,192,128]{5,4,3,2,1,0:T(8,128)(2,1)S(1)} %bitcast.67, bf16[8,4,2,2,192,128]{5,4,3,2,1,0:T(8,128)(2,1)S(1)} %bitcast.68), custom_call_target="tpu_custom_call" | custom-call | flops 15000000512 | bytes 8000000 | tf_op jit(solution)/shard_map/pallas_call | solution.py:117
  131.9 13.7 %collective-permute-start.5 = (bf16[192,640]{1,0:T(8,128)(2,1)S(1)}, bf16[192,640]{1,0:T(8,128)(2,1)S(1)}, u32[]{:S(2)}, u32[]{:S(2)}) collective-permute-start(bf16[192,640]{1,0:T(8,128)(2,1)S(1)} %shard_map.133), channel_id=1, source_target_pairs={{0,224},{32,192},{64,160},{96,128},{128,96},{160,64},{192,32},{224... | collective-permute-start | bytes 737288 | tf_op jit(solution)/shard_map/ppermute | solution.py:287
  145.6 20.2 %shard_map.134 = bf16[192,640]{1,0:T(8,128)(2,1)S(1)} custom-call(s32[10]{0:T(128)S(1)} %get-tuple-element.42.plan, bf16[192,640]{1,0:T(8,128)(2,1)S(1)} %collective-permute-done.2.q_ref, s32[960,1]{1,0:T(8,128)S(1)} %broadcast_in_dim_tile.7.row_ref, bf16[8,4,2,2,192,128]{5,4,3,2,1,0:T(8,128)(2,1)S(1)} %bitcast.69, bf16[8,4,2,2,192,128]{5,4,3,2,1,0:T(8,128)(2,1)S(1)} %bitcast.70), custom_call_target="tpu_custom_call" | custom-call | flops 15000000512 | bytes 8000000 | tf_op jit(solution)/shard_map/pallas_call | solution.py:117
  165.9 1.3 collective-permute-start.6
  167.5 9.0 %all-gather.2 = f32[4,3,3]{2,1,0:T(4,128)S(1)} all-gather(f32[1,3,3]{2,1,0:T(4,128)S(1)} %maximum_bitcast_fusion.1), channel_id=3, replica_groups=mesh['z'=8,'yl'=2,'x'=4,'yh'=2,'core'=2] {'yh','core'}, dimensions={0}, use_global_device_ids=true | all-gather | bytes 180 | tf_op jit(solution)/shard_map/all_gather | solution.py:350
  177.2 0.9 maximum_select_fusion
  (81 shorter events, 11.1 us)
Async XLA Ops:
  7.2 115.4 %all-gather.5.cloned.1.call-start = ((), (), s32[]{:S(2)}) async-start(), calls=%async_computation.3 | async-start | bytes 6488064 | tf_op jit(solution)/shard_map/all_gather | solution.py:279
  8.1 11.1 %collective-permute-start = (bf16[2,192,128]{2,1,0:T(8,128)(2,1)S(1)}, bf16[2,192,128]{2,1,0:T(8,128)(2,1)S(1)}, u32[]{:S(2)}, u32[]{:S(2)}) collective-permute-start(bf16[2,192,128]{2,1,0:T(8,128)(2,1)S(1)} %pad_maximum_fusion.2), channel_id=1, source_target_pairs={{0,16},{16,0},{1,17},{17,1},{2,18},{18,2},{3,19},{19,3},{4,20},{20... | collective-permute-start | bytes 294920 | tf_op jit(solution)/shard_map/ppermute | solution.py:212
  12.6 0.9 copy-start
  13.5 0.9 copy-start.1
  14.4 1.0 copy-start.2
  18.7 42.2 %copy-start.5 = (s32[3,64,32]{1,2,0:T(8,128)S(1)}, s32[3,64,32]{1,2,0:T(8,128)}, u32[]{:S(2)}) copy-start(s32[3,64,32]{1,2,0:T(8,128)} %param.22) | copy-start | bytes 73732
  18.7 42.4 %copy-start.4 = (s32[12288]{0:T(1024)S(1)}, s32[12288]{0:T(1024)}, u32[]{:S(2)}) copy-start(s32[12288]{0:T(1024)} %param.15) | copy-start | bytes 147460
  19.2 58.6 %copy-start.6 = (f32[1280]{0:T(1024)S(1)}, f32[1280]{0:T(1024)}, u32[]{:S(2)}) copy-start(f32[1280]{0:T(1024)} %param.20) | copy-start | bytes 15364
  50.3 26.4 %all-to-all-start.1 = ((bf16[64,3,1280]{2,1,0:T(4,128)(2,1)}), bf16[64,3,1280]{2,1,0:T(4,128)(2,1)S(1)}, u32[]{:S(2)}, u32[]{:S(2)}) async-start(bf16[64,3,1280]{2,1,0:T(4,128)(2,1)} %shard_map.132), calls=%async_computation.1 | async-start | bytes 1310720 | tf_op jit(solution)/shard_map/all_to_all | solution.py:284
  77.8 12.9 %copy-start.7 = (s32[3,64]{1,0:T(4,128)S(1)}, s32[3,64]{1,0:T(4,128)}, u32[]{:S(2)}) copy-start(s32[3,64]{1,0:T(4,128)} %param.23) | copy-start | bytes 2308
  81.7 13.3 %copy-start.3 = (bf16[192,1280]{1,0:T(8,128)(2,1)S(1)}, bf16[192,1280]{1,0:T(8,128)(2,1)}, u32[]{:S(2)}) copy-start(bf16[192,1280]{1,0:T(8,128)(2,1)} %param.12) | copy-start | bytes 1474564
  81.8 9.7 %collective-permute-start.3 = (bf16[192,896]{0,1:T(8,128)(2,1)S(1)}, bf16[192,896]{0,1:T(8,128)(2,1)S(1)}, u32[]{:S(2)}, u32[]{:S(2)}) collective-permute-start(bf16[192,896]{0,1:T(8,128)(2,1)S(1)} %pad_maximum_fusion), channel_id=1, source_target_pairs={{0,1},{1,0},{2,3},{3,2},{4,5},{5,4},{6,7},{7,6},{8,9},{9,8},{10,11... | collective-permute-start | bytes 1032200 | tf_op jit(solution)/shard_map/ppermute | solution.py:212
  92.0 9.7 %collective-permute-start.4 = (bf16[192,512]{0,1:T(8,128)(2,1)S(1)}, bf16[192,512]{0,1:T(8,128)(2,1)S(1)}, u32[]{:S(2)}, u32[]{:S(2)}) collective-permute-start(bf16[192,512]{0,1:T(8,128)(2,1)S(1)} %pad_maximum_fusion.1), channel_id=1, source_target_pairs={{0,2},{2,0},{1,3},{3,1},{4,6},{6,4},{5,7},{7,5},{8,10},{10,8},{9,1... | collective-permute-start | bytes 589832 | tf_op jit(solution)/shard_map/ppermute | solution.py:212
  95.1 16.0 %collective-permute-start.1 = (bf16[192,640]{1,0:T(8,128)(2,1)S(1)}, bf16[192,640]{1,0:T(8,128)(2,1)S(1)}, u32[]{:S(2)}, u32[]{:S(2)}) collective-permute-start(bf16[192,640]{1,0:T(8,128)(2,1)S(1)} %get-tuple-element.32), channel_id=1, source_target_pairs={{0,224},{32,192},{64,160},{96,128},{128,96},{160,64},{192,32},{224... | collective-permute-start | bytes 737288 | tf_op jit(solution)/shard_map/ppermute | solution.py:287
  97.4 13.7 %collective-permute-start.2 = (bf16[192,640]{1,0:T(8,128)(2,1)S(1)}, bf16[192,640]{1,0:T(8,128)(2,1)S(1)}, u32[]{:S(2)}, u32[]{:S(2)}) collective-permute-start(bf16[192,640]{1,0:T(8,128)(2,1)S(1)} %get-tuple-element.31), channel_id=1, source_target_pairs={{0,16},{16,0},{1,17},{17,1},{2,18},{18,2},{3,19},{19,3},{4,20},{20... | collective-permute-start | bytes 737288 | tf_op jit(solution)/shard_map/ppermute | solution.py:212
  111.1 56.0 %all-to-all-start.2 = ((f32[64,1,9]{2,1,0:T(1,128)}), f32[64,1,9]{2,1,0:T(1,128)S(1)}, u32[]{:S(2)}, u32[]{:S(2)}) async-start(f32[64,1,9]{2,1,0:T(1,128)} %bitcast.23), calls=%async_computation.2 | async-start | bytes 65536 | tf_op jit(solution)/shard_map/all_to_all | solution.py:347
  131.9 45.2 %collective-permute-start.5 = (bf16[192,640]{1,0:T(8,128)(2,1)S(1)}, bf16[192,640]{1,0:T(8,128)(2,1)S(1)}, u32[]{:S(2)}, u32[]{:S(2)}) collective-permute-start(bf16[192,640]{1,0:T(8,128)(2,1)S(1)} %shard_map.133), channel_id=1, source_target_pairs={{0,224},{32,192},{64,160},{96,128},{128,96},{160,64},{192,32},{224... | collective-permute-start | bytes 737288 | tf_op jit(solution)/shard_map/ppermute | solution.py:287
  165.9 11.3 %collective-permute-start.6 = (bf16[192,640]{1,0:T(8,128)(2,1)S(1)}, bf16[192,640]{1,0:T(8,128)(2,1)S(1)}, u32[]{:S(2)}, u32[]{:S(2)}) collective-permute-start(bf16[192,640]{1,0:T(8,128)(2,1)S(1)} %shard_map.134), channel_id=1, source_target_pairs={{0,16},{16,0},{1,17},{17,1},{2,18},{18,2},{3,19},{19,3},{4,20},{20... | collective-permute-start | bytes 737288 | tf_op jit(solution)/shard_map/ppermute | solution.py:212
Sparse Core Ops, SparseCore 0:
  20.1 99.5 all-gather.4

commit v3 on v2

v3 whole, which is shorter than its diff:
```python
import functools
import math

import jax
import jax.numpy as jnp
from jax import lax
from jax.experimental import pallas as pl
from jax.experimental.pallas import tpu as pltpu
from jax.sharding import Mesh, PartitionSpec as P

HD = 128
TILE = 128
EPS = 1e-06
FLOOR = -1e30
BELOW = -2e30
LOG2E = 1.4426950408889634
BF = jnp.bfloat16
F32 = jnp.float32
CTX = ("z", "yl", "x")
TP = ("yh", "core")
CHUNK = 320
REQUESTS = 8


def dot_t(a, b):
    return lax.dot_general(a, b, (((1,), (1,)), ((), ())), preferred_element_type=F32)


def dot(a, b):
    return lax.dot_general(a, b, (((1,), (0,)), ((), ())), preferred_element_type=F32)


def two_parts(value):
    high = value.astype(BF)
    return high, (value - high.astype(F32)).astype(BF)


def bound(plan, at):
    return functools.reduce(
        jnp.minimum, [jnp.where(plan[4 + i] > at, plan[4 + i], 2**30) for i in range(REQUESTS)]
    )


def place(plan, step, rows, keys):
    count = lax.div(plan[2] + rows - 1, keys) - lax.div(plan[0], keys) + 1
    which = jnp.where(step >= count, 1, 0)
    tile = jnp.where(step >= count, lax.div(plan[1], keys) + step - count, lax.div(plan[0], keys) + step)
    return which, tile


def attend_kernel(plan, q_ref, row_ref, k_ref, v_ref, out_ref, qs, peak, acc):
    blocks, rows, width = q_ref.shape
    group = width // HD
    keys = k_ref.shape[1] * rows
    step = pl.program_id(0)
    which, tile = place(plan, step, rows, keys)
    first_row = jnp.where(which == 1, plan[3], plan[2])

    @pl.when(step == 0)
    def _():
        for b in range(blocks):
            for h in range(group):
                q = q_ref[b, :, h * HD : (h + 1) * HD].astype(F32) * (HD**-0.5 * LOG2E)
                high, low = two_parts(q)
                qs[b, h * rows : (h + 1) * rows, 0:HD] = high
                qs[b, h * rows : (h + 1) * rows, HD:] = low
        peak[...] = jnp.full(peak.shape, FLOOR, F32)
        acc[...] = jnp.zeros(acc.shape, F32)

    base = tile * keys

    def part(masked):
        block = (keys, HD)
        k = k_ref[0, :, 0, 0].reshape(block).T
        k = jnp.concatenate([k, k], axis=0)
        v = jnp.concatenate([v_ref[0, :, 0, 0].reshape(block), jnp.ones(block, BF)], axis=1)
        if masked:
            at = base + lax.broadcasted_iota(jnp.int32, (1, keys), 1)
            end = bound(plan, at) - first_row
            at = at - first_row
        count = qs.shape[1] // CHUNK
        ahead = dot(qs[which, 0:CHUNK], k)
        for i in range(count):
            s = ahead
            if i + 1 < count:
                ahead = dot(qs[which, (i + 1) * CHUNK : (i + 2) * CHUNK], k)
            here = slice(i * CHUNK, (i + 1) * CHUNK)
            if masked:
                row = row_ref[here]
                s = jnp.where((at <= row) & (row < end), s, BELOW)
            old = peak[which, here]
            new = jnp.maximum(old, jnp.max(s, axis=1, keepdims=True))
            peak[which, here] = new
            p = jnp.exp2(s - new).astype(BF)
            acc[which, here] = acc[which, here] * jnp.exp2(old - new) + dot(p, v)

    last = base + keys - 1
    last_row = first_row + rows - 1
    need = base <= last_row
    inside = (last <= first_row) & (bound(plan, base) > last_row)
    pl.when(need & inside)(functools.partial(part, False))
    pl.when(need & jnp.logical_not(inside))(functools.partial(part, True))

    @pl.when(step == pl.num_programs(0) - 1)
    def _():
        for b in range(blocks):
            for h in range(group):
                here = slice(h * rows, (h + 1) * rows)
                out_ref[b, :, h * HD : (h + 1) * HD] = (acc[b, here, 0:HD] / acc[b, here, HD:]).astype(BF)


def attend(plan, q, row, kv):
    blocks, rows, width = q.shape
    nz, nx, ny, _, _, _ = kv.shape
    keys = nx * rows

    def whole(shape):
        return pl.BlockSpec(shape, lambda i, plan: (0,) * len(shape))

    def tiles(kind):
        def index(i, plan):
            at = jnp.minimum(place(plan, i, rows, keys)[1], nz * ny - 1)
            return (lax.div(at, ny), 0, lax.rem(at, ny), kind, 0, 0)

        return pl.BlockSpec((1, nx, 1, 1, rows, HD), index)

    flat = width // HD * rows
    return pl.pallas_call(
        attend_kernel,
        out_shape=jax.ShapeDtypeStruct(q.shape, BF),
        grid_spec=pltpu.PrefetchScalarGridSpec(
            num_scalar_prefetch=1,
            grid=(nz * ny + 2,),
            in_specs=[whole(q.shape), whole(row.shape), tiles(0), tiles(1)],
            out_specs=whole(q.shape),
            scratch_shapes=[
                pltpu.VMEM((blocks, flat, 2 * HD), BF),
                pltpu.VMEM((blocks, flat, 1), F32),
                pltpu.VMEM((blocks, flat, 2 * HD), F32),
            ],
        ),
        compiler_params=pltpu.CompilerParams(
            vmem_limit_bytes=24 * 2**20, dimension_semantics=("arbitrary",)
        ),
        cost_estimate=pl.CostEstimate(
            flops=20_000_000_000, bytes_accessed=8_000_000, transcendentals=10_000_000
        ),
    )(plan, q, row, kv, kv)


def merge_kernel(met_ref, out_ref):
    width = out_ref.shape[2]
    tail = met_ref[:, :, width:].astype(F32)
    size = tail + pltpu.roll(tail, HD // 2, 2)
    share = jnp.exp2(size - jnp.max(size, axis=0, keepdims=True))
    share = share / jnp.sum(share, axis=0, keepdims=True)
    for h in range(width // HD):
        here = slice(h * HD, (h + 1) * HD)
        total = jnp.sum(met_ref[:, :, here].astype(F32) * share[:, :, h : h + 1], axis=0, keepdims=True)
        out_ref[:, :, here] = jnp.broadcast_to(total.astype(BF), (out_ref.shape[0], out_ref.shape[1], HD))


def merge(met):
    vmem = pl.BlockSpec(memory_space=pltpu.VMEM)
    return pl.pallas_call(
        merge_kernel,
        out_shape=jax.ShapeDtypeStruct((met.shape[0], met.shape[1], met.shape[2] - HD), BF),
        in_specs=[vmem],
        out_specs=vmem,
        compiler_params=pltpu.CompilerParams(vmem_limit_bytes=16 * 2**20),
        cost_estimate=pl.CostEstimate(flops=500_000_000, bytes_accessed=1_500_000, transcendentals=0),
    )(met)


def state_kernel(shape, q_ref, k_ref, v_ref, own_ref, keep_ref, out_ref):
    steps, lines, kv_heads, group = shape
    rows, own = k_ref.shape[0], own_ref.shape[0]
    count = keep_ref.shape[1]
    scale = HD**-0.5 * LOG2E
    keep = keep_ref[...] > 0
    lane = lax.broadcasted_iota(jnp.int32, (steps * lines, HD), 1)
    tail = jnp.zeros((steps * lines, HD), F32)
    for kh in range(kv_heads):
        at = slice(kh * HD, (kh + 1) * HD)
        pad = jnp.zeros((count - rows - own, HD), BF)
        past = slice((kv_heads + kh) * HD, (kv_heads + kh + 1) * HD)
        k = jnp.concatenate([k_ref[:, at], own_ref[:, at], pad], axis=0)
        v = jnp.concatenate([v_ref[:, at], own_ref[:, past], pad], axis=0)
        for g in range(group):
            h = kh * group + g
            high, low = two_parts(q_ref[:, h * HD : (h + 1) * HD].astype(F32) * scale)
            s = jnp.where(keep, dot_t(high, k) + dot_t(low, k), BELOW)
            top = jnp.maximum(jnp.max(s, axis=1, keepdims=True), FLOOR)
            p = jnp.exp2(s - top)
            total = jnp.sum(p, axis=1, keepdims=True)
            some = total > 0.0
            o = dot(p.astype(BF), v) / jnp.where(some, total, 1.0)
            out_ref[:, h * HD : (h + 1) * HD] = o.astype(BF)
            size = jnp.where(some, top + jnp.log2(jnp.where(some, total, 1.0)), FLOOR)
            high, low = two_parts(size)
            tail = jnp.where(lane == h, high.astype(F32), tail)
            tail = jnp.where(lane == h + 64, low.astype(F32), tail)
    width = kv_heads * group * HD
    out_ref[:, width : width + HD] = tail.astype(BF)


def states(shape, q, k, v, own, keep):
    vmem = pl.BlockSpec(memory_space=pltpu.VMEM)
    return pl.pallas_call(
        functools.partial(state_kernel, shape),
        out_shape=jax.ShapeDtypeStruct((q.shape[0], q.shape[1] + HD), BF),
        in_specs=[vmem] * 5,
        out_specs=vmem,
        compiler_params=pltpu.CompilerParams(vmem_limit_bytes=16 * 2**20),
        cost_estimate=pl.CostEstimate(flops=4_000_000_000, bytes_accessed=1_500_000, transcendentals=400_000),
    )(q, k, v, own, keep)


def after(values):
    return lax.optimization_barrier(values)


def swap(value, axis):
    return lax.ppermute(value, axis, [(0, 1), (1, 0)])


def local(
    prefill_queries,
    prefill_keys,
    prefill_values,
    segments,
    decode_queries,
    decode_keys,
    decode_values,
    row_request,
    norm_gain,
    head_weight,
    allowed_tiles,
    tokens,
):
    nz, ny, nx = (lax.axis_size(a) for a in CTX)
    nctx = nz * ny * nx
    z, yl, x = (lax.axis_index(a) for a in CTX)
    yh, core = (lax.axis_index(a) for a in TP)
    me = (z * ny + yl) * nx + x
    rows = prefill_queries.shape[0]
    kv_heads = prefill_keys.shape[1] // HD
    width = prefill_queries.shape[1]
    group = width // HD // kv_heads
    half = width // 2
    steps, lines, _ = decode_queries.shape
    model = width * lax.axis_size(TP)

    requests = jnp.arange(REQUESTS, dtype=jnp.int32)
    begins = jnp.sum((segments[None, :] < requests[:, None]).astype(jnp.int32), axis=1)

    own_segment = lax.dynamic_slice_in_dim(segments, me * rows, rows)
    slot = jnp.arange(256, dtype=jnp.int32)[None, None, :] - rows
    key_segment = jnp.pad(own_segment, (0, 256 - rows), constant_values=-1)[None, None, :]
    line = jnp.arange(lines, dtype=jnp.int32)[None, :, None]
    turn = jnp.arange(steps, dtype=jnp.int32)[:, None, None]
    keep = (row_request[None, :, None] == key_segment) | (
        (line == me) & (slot >= 0) & (slot <= turn)
    )
    def mine_and_other(a, w):
        first, second = a[:, :w], a[:, w:]
        return jnp.where(yl == 0, first, second), jnp.where(yl == 0, second, first)

    k_mine, k_other = mine_and_other(prefill_keys, HD)
    v_mine, v_other = mine_and_other(prefill_values, HD)
    kv_mine = jnp.stack([k_mine, v_mine])
    kv_got = swap(jnp.stack([k_other, v_other]), "yl")
    kv_pair = jnp.where(yl == 0, jnp.stack([kv_mine, kv_got]), jnp.stack([kv_got, kv_mine]))
    def mirror(value):
        return lax.ppermute(value, "z", [(i, nz - 1 - i) for i in range(nz)])

    q_mine, q_other = mine_and_other(prefill_queries, half)
    q_far = mirror(q_mine)

    own = jnp.concatenate([decode_keys[:, 0], decode_values[:, 0]], axis=1)
    state = states(
        (steps, lines, kv_heads, group),
        decode_queries.reshape(steps * lines, width),
        prefill_keys,
        prefill_values,
        jnp.pad(own, ((0, 16 - steps), (0, 0))),
        keep.astype(jnp.int32).reshape(steps * lines, 256),
    )
    state = state.reshape(steps, lines, width + HD).transpose(1, 0, 2)
    kv_pair, state = after((kv_pair, state))
    kv_all = lax.all_gather(kv_pair, ("z", "x"), axis=0).reshape((nz, nx) + kv_pair.shape)

    met = lax.all_to_all(state, CTX, 0, 0, tiled=True)
    met, q_far = after((met, q_far))
    attention = merge(met)
    q_other, attention = after((q_other, attention))
    spread = lax.all_to_all(attention, CTX, 0, 0, tiled=True).reshape(lines * steps, width)

    q_near = swap(q_other, "yl")
    spread, q_near = after((spread, q_near))
    row = jnp.tile(jnp.arange(rows, dtype=jnp.int32), group)[:, None]
    first_rows = jnp.stack([((z * ny + 1 - yl) * nx + x) * rows, ((nz - 1 - z) * ny + yl) * nx * rows + x * rows])
    first_keys = jnp.max(jnp.where(begins[None, :] <= first_rows[:, None], begins[None, :], 0), axis=1)
    plan = jnp.concatenate([first_keys, first_rows, begins])

    widened = spread.astype(F32)
    squares = jnp.sum(widened * widened, axis=1, keepdims=True)
    scaled = (widened * norm_gain).astype(BF)
    partial_logits = dot(scaled, head_weight)
    span = partial_logits.shape[1]

    quarter = span // 4
    high, low = two_parts(squares)
    lane = lax.broadcasted_iota(jnp.int32, (squares.shape[0], 16), 1)
    extra = jnp.where(lane == 0, high, jnp.where(lane == 1, low, jnp.zeros((), BF)))

    def part_of(yh, core):
        return lax.dynamic_slice_in_dim(partial_logits, (core * 2 + yh) * quarter, quarter, 1)

    logits = part_of(yh, core)
    for away in (3, 2, 1):
        sent = part_of(yh ^ (away >> 1), core ^ (away & 1)).astype(BF)
        there = lax.ppermute(
            jnp.concatenate([sent, extra], axis=1), TP, [(i, i ^ away) for i in range(4)]
        )
        logits = logits + there[:, :quarter].astype(F32)
        squares = squares + jnp.sum(there[:, quarter:].astype(F32), axis=1, keepdims=True)
    logits = lax.rsqrt(squares / model + EPS) * logits

    first_id = me * span + core * (span // 2) + yh * quarter
    tiles = first_id // TILE + jnp.arange(quarter // TILE, dtype=jnp.int32)
    allowed = jnp.any(allowed_tiles[..., None] == tiles, axis=2)
    allowed = allowed.transpose(1, 0, 2).reshape(lines * steps, quarter // TILE)
    wanted = tokens.T.reshape(lines * steps, 1) - first_id
    keep_ids = jnp.repeat(allowed, TILE, axis=1)
    masked = jnp.where(keep_ids, logits, FLOOR)
    top = jnp.max(masked, axis=1)
    mass = jnp.sum(jnp.where(keep_ids, jnp.exp(masked - top[:, None]), 0.0), axis=1)
    ids = jnp.arange(quarter, dtype=jnp.int32)
    target = jnp.sum(jnp.where(ids[None, :] == wanted, logits, 0.0), axis=1)

    def joined(top, mass, target, axis):
        peak = jnp.max(top, axis=axis)
        mass = jnp.sum(mass * jnp.exp(top - jnp.expand_dims(peak, axis)), axis=axis)
        return peak, mass, jnp.sum(target, axis=axis)

    stats = jnp.stack([top, mass, target], axis=-1).reshape(lines, steps * 3)
    q_both, stats = after((jnp.stack([q_near, q_far]), stats))
    output = attend(plan, q_both, row, kv_all)
    stats = lax.all_to_all(stats, CTX, 0, 0, tiled=True)
    stats, output = after((stats, output))
    out_other, out_mine = swap(output[0], "yl"), mirror(output[1])
    stats = stats.reshape(nctx, steps, 3)
    stats = jnp.stack(joined(*(stats[..., i] for i in range(3)), 0))
    stats = lax.all_gather(stats, TP, axis=0)
    top, mass, target = joined(*(stats[:, i] for i in range(3)), 0)
    result = target - (top + jnp.log(mass))

    prefill_output = jnp.where(
        yl == 0,
        jnp.concatenate([out_mine, out_other], axis=1),
        jnp.concatenate([out_other, out_mine], axis=1),
    )
    return prefill_output, result[:, None]


def solution(mesh):
    fine = Mesh(mesh.devices.reshape(8, 2, 4, 2, 2), CTX + TP)
    placed = (
        P(CTX, TP),
        P(CTX, TP),
        P(CTX, TP),
        P(),
        P(None, None, TP),
        P(None, CTX, TP),
        P(None, CTX, TP),
        P(),
        P(TP),
        P(TP, CTX),
        P(),
        P(),
    )
    return jax.shard_map(
        local, mesh=fine, in_specs=placed, out_specs=(P(CTX, TP), P(None, CTX)), check_vma=False
    )
```

time: 186 us -> 184 us (0.989)
  the two profiles are of different devices: /device:TPU:193 before, /device:TPU:1 now
where the time goes in v3:
time: 184 us; the launch traced here: 182 us
  waiting for transfers between devices  63 us (34%)
  starting transfers between devices  46.6 us (25%)
  Pallas kernels  29.4 us (16%)
  between operations  14.4 us (8%)
  local copies, waits for them, and re-layouts  10.5 us (6%)
  blocking collectives  7.97 us (4%)
  other arithmetic  6.9 us (4%)
  matrix products  3.08 us (2%)
    ppermute x2, waiting for transfers between devices, mirror(): return lax.ppermute(value, 'z', [(i, nz - 1 - i) for i in range(nz)])  34.5 us
    pallas_call x1, Pallas kernels, attend(): pl.pallas_call(attend_kernel, out_shape=jax.ShapeDtypeStruct(q.shape, BF)...  24.2 us
    all_to_all x1, waiting for transfers between devices, local(): lax.all_to_all(attention, CTX, 0, 0, tiled=True)  19.4 us
    all_to_all x1, starting transfers between devices, local(): met = lax.all_to_all(state, CTX, 0, 0, tiled=True)  11.7 us
    ppermute x3, starting transfers between devices, local(): lax.ppermute(jnp.concatenate([sent, extra], axis=1), TP, [(i, i ^ away) f...  9.77 us
    all_to_all x1, starting transfers between devices, local(): lax.all_to_all(attention, CTX, 0, 0, tiled=True)  9.44 us
    ppermute x3, waiting for transfers between devices, local(): lax.ppermute(jnp.concatenate([sent, extra], axis=1), TP, [(i, i ^ away) f...  8.96 us
    all_gather x1, blocking collectives, local(): stats = lax.all_gather(stats, TP, axis=0)  7.97 us
  transfers between devices with their start and end apart: 12, of which 5 were waited for; matrix products, arithmetic and copies ran while one was open for 7% of the time, Pallas kernels for 16%

profile of v3, /device:TPU:1, one launch (start us, length us, event | category | flops | bytes accessed | tf_op | source)
XLA Modules:
  0.0 181.8 jit_solution(11028704238249756223)
XLA Ops:
  7.2 0.9 select_bitcast_fusion.2
  8.1 2.2 %collective-permute-start = (bf16[2,192,128]{2,1,0:T(8,128)(2,1)S(1)}, bf16[2,192,128]{2,1,0:T(8,128)(2,1)S(1)}, u32[]{:S(2)}, u32[]{:S(2)}) collective-permute-start(bf16[2,192,128]{2,1,0:T(8,128)(2,1)S(1)} %pad_maximum_fusion.4), channel_id=1, source_target_pairs={{0,16},{16,0},{1,17},{17,1},{2,18},{18,2},{3,19},{19,3},{4,20},{20... | collective-permute-start | bytes 294920 | tf_op jit(solution)/shard_map/ppermute | solution.py:224
  14.5 1.0 copy-done.3
  15.6 3.3 %shard_map.131 = bf16[192,1408]{1,0:T(8,128)(2,1)S(1)} custom-call(bf16[192,1280]{1,0:T(8,128)(2,1)S(1)} %bitcast.74, bf16[192,256]{1,0:T(8,128)(2,1)S(1)} %copy-done.1, bf16[192,256]{1,0:T(8,128)(2,1)S(1)} %copy-done, bf16[16,512]{1,0:T(8,128)(2,1)S(1)} %fusion.8.own_ref, s32[192,256]{1,0:T(8,128)S(1)} %bitcast.71), custom_call_target="tpu_custom_call" | custom-call | flops 4000000000 | bytes 1500000 | tf_op jit(solution)/shard_map/pallas_call | solution.py:209
  18.9 1.3 copy.47
  21.0 11.7 %all-to-all-start = ((bf16[64,3,1408]{2,1,0:T(4,128)(2,1)}), bf16[64,3,1408]{2,1,0:T(4,128)(2,1)S(1)}, u32[]{:S(2)}, u32[]{:S(2)}) async-start(bf16[64,3,1408]{2,1,0:T(4,128)(2,1)} %bitcast.69), calls=%async_computation | async-start | bytes 1441792 | tf_op jit(solution)/shard_map/all_to_all | solution.py:293
  32.7 2.6 %collective-permute-start.1 = (bf16[192,640]{1,0:T(8,128)(2,1)S(1)}, bf16[192,640]{1,0:T(8,128)(2,1)S(1)}, u32[]{:S(2)}, u32[]{:S(2)}) collective-permute-start(bf16[192,640]{1,0:T(8,128)(2,1)S(1)} %get-tuple-element.42), channel_id=1, source_target_pairs={{0,224},{32,192},{64,160},{96,128},{128,96},{160,64},{192,32},{224... | collective-permute-start | bytes 737288 | tf_op jit(solution)/shard_map/ppermute | solution.py:275
  35.3 32.2 %collective-permute-done.1 = bf16[192,640]{1,0:T(8,128)(2,1)S(1)} collective-permute-done((bf16[192,640]{1,0:T(8,128)(2,1)S(1)}, bf16[192,640]{1,0:T(8,128)(2,1)S(1)}, u32[]{:S(2)}, u32[]{:S(2)}) %collective-permute-start.1) | collective-permute-done | bytes 245792 | tf_op jit(solution)/shard_map/ppermute | solution.py:275
  67.5 1.9 %shard_map.132 = bf16[64,3,1280]{2,1,0:T(4,128)(2,1)} custom-call(bf16[64,3,1408]{2,1,0:T(4,128)(2,1)S(1)} %all-to-all-done.met_ref), custom_call_target="tpu_custom_call" | custom-call | flops 500000000 | bytes 1500000 | tf_op jit(solution)/shard_map/pallas_call | solution.py:165
  69.3 9.4 %all-to-all-start.1 = ((bf16[64,3,1280]{2,1,0:T(4,128)(2,1)}), bf16[64,3,1280]{2,1,0:T(4,128)(2,1)S(1)}, u32[]{:S(2)}, u32[]{:S(2)}) async-start(bf16[64,3,1280]{2,1,0:T(4,128)(2,1)} %shard_map.132), calls=%async_computation.1 | async-start | bytes 1310720 | tf_op jit(solution)/shard_map/all_to_all | solution.py:297
  79.4 1.1 collective-permute-start.2
  80.5 19.4 %all-to-all-done.1 = bf16[64,3,1280]{2,1,0:T(4,128)(2,1)S(1)} async-done(((bf16[64,3,1280]{2,1,0:T(4,128)(2,1)}), bf16[64,3,1280]{2,1,0:T(4,128)(2,1)S(1)}, u32[]{:S(2)}, u32[]{:S(2)}) %all-to-all-start.1) | async-done | bytes 491552 | tf_op jit(solution)/shard_map/all_to_all | solution.py:297
  100.4 3.1 %fusion.2 = f32[192,1536]{1,0:T(8,128)S(1)} fusion(bf16[1280,1536]{1,0:T(8,128)(2,1)} %param.21, bf16[192,1280]{1,0:T(8,128)(2,1)S(1)} %reshape.217, f32[1280]{0:T(1024)S(1)} %copy-done.7), kind=kOutput, calls=%fused_computation.5 | convolution fusion | flops 755712000 | bytes 5608448 | tf_op jit(solution)/shard_map/dot_general | solution.py:30
  103.9 6.5 %collective-permute-start.5 = (bf16[192,400]{1,0:T(8,128)(2,1)S(1)}, bf16[192,400]{1,0:T(8,128)(2,1)S(1)}, u32[]{:S(2)}, u32[]{:S(2)}) collective-permute-start(bf16[192,400]{1,0:T(8,128)(2,1)S(1)} %get-tuple-element.49), channel_id=1, source_target_pairs={{0,1},{1,0},{2,3},{3,2},{4,5},{5,4},{6,7},{7,6},{8,9},{9,8},{10,11... | collective-permute-start | bytes 460808 | tf_op jit(solution)/shard_map/ppermute | solution.py:323
  111.6 3.1 %collective-permute-start.4 = (bf16[192,400]{1,0:T(8,128)(2,1)S(1)}, bf16[192,400]{1,0:T(8,128)(2,1)S(1)}, u32[]{:S(2)}, u32[]{:S(2)}) collective-permute-start(bf16[192,400]{1,0:T(8,128)(2,1)S(1)} %get-tuple-element.48), channel_id=1, source_target_pairs={{0,2},{1,3},{2,0},{3,1},{4,6},{5,7},{6,4},{7,5},{8,10},{9,11},{10,... | collective-permute-start | bytes 460808 | tf_op jit(solution)/shard_map/ppermute | solution.py:323
  115.0 4.7 %collective-permute-done.4 = bf16[192,400]{1,0:T(8,128)(2,1)S(1)} collective-permute-done((bf16[192,400]{1,0:T(8,128)(2,1)S(1)}, bf16[192,400]{1,0:T(8,128)(2,1)S(1)}, u32[]{:S(2)}, u32[]{:S(2)}) %collective-permute-start.4) | collective-permute-done | bytes 153632 | tf_op jit(solution)/shard_map/ppermute | solution.py:323
  119.8 4.2 %collective-permute-done.3 = bf16[192,400]{1,0:T(8,128)(2,1)S(1)} collective-permute-done((bf16[192,400]{1,0:T(8,128)(2,1)S(1)}, bf16[192,400]{1,0:T(8,128)(2,1)S(1)}, u32[]{:S(2)}, u32[]{:S(2)}) %collective-permute-start.3) | collective-permute-done | bytes 153632 | tf_op jit(solution)/shard_map/ppermute | solution.py:323
  125.8 5.8 %all-to-all-start.2 = ((f32[64,1,9]{2,1,0:T(1,128)}), f32[64,1,9]{2,1,0:T(1,128)S(1)}, u32[]{:S(2)}, u32[]{:S(2)}) async-start(f32[64,1,9]{2,1,0:T(1,128)} %bitcast.20), calls=%async_computation.2 | async-start | bytes 65536 | tf_op jit(solution)/shard_map/all_to_all | solution.py:350
  131.7 2.8 %copy-done.2 = bf16[64,2,192,128]{3,2,1,0:T(8,128)(2,1)S(1)} copy-done((bf16[64,2,192,128]{3,2,1,0:T(8,128)(2,1)S(1)}, bf16[64,2,192,128]{3,2,1,0:T(8,128)(2,1)}, u32[]{:S(2)}) %copy-start.2) | copy-done | bytes 6291480
  134.5 24.2 %shard_map.133 = bf16[2,192,640]{2,1,0:T(8,128)(2,1)S(1)} custom-call(s32[12]{0:T(128)S(1)} %pad_add_fusion.1.plan, bf16[2,192,640]{2,1,0:T(8,128)(2,1)S(1)} %pad_maximum_fusion.q_ref, s32[960,1]{1,0:T(8,128)S(1)} %broadcast_in_dim_tile.4.row_ref, bf16[8,4,2,2,192,128]{5,4,3,2,1,0:T(8,128)(2,1)S(1)} %bitcast.72, bf16[8,4,2,2,192,128]{5,4,3,2,1,0:T(8,128)(2,1)S(1)} %bitcast.73), custom_call_target="tpu_custom_call" | custom-call | flops 20000000000 | bytes 8000000 | tf_op jit(solution)/shard_map/pallas_call | solution.py:128
  159.3 3.4 %collective-permute-start.6 = (bf16[192,640]{1,0:T(8,128)(2,1)S(1)}, bf16[192,640]{1,0:T(8,128)(2,1)S(1)}, u32[]{:S(2)}, u32[]{:S(2)}) collective-permute-start(bf16[192,640]{1,0:T(8,128)(2,1)S(1)} %get-tuple-element.39), channel_id=1, source_target_pairs={{0,224},{32,192},{64,160},{96,128},{128,96},{160,64},{192,32},{224... | collective-permute-start | bytes 737288 | tf_op jit(solution)/shard_map/ppermute | solution.py:275
  163.1 8.0 %all-gather.2 = f32[4,3,3]{2,1,0:T(4,128)S(1)} all-gather(f32[1,3,3]{2,1,0:T(4,128)S(1)} %maximum_bitcast_fusion.1), channel_id=3, replica_groups=mesh['z'=8,'yl'=2,'x'=4,'yh'=2,'core'=2] {'yh','core'}, dimensions={0}, use_global_device_ids=true | all-gather | bytes 180 | tf_op jit(solution)/shard_map/all_gather | solution.py:355
  171.7 2.4 %collective-permute-done.6 = bf16[192,640]{1,0:T(8,128)(2,1)S(1)} collective-permute-done((bf16[192,640]{1,0:T(8,128)(2,1)S(1)}, bf16[192,640]{1,0:T(8,128)(2,1)S(1)}, u32[]{:S(2)}, u32[]{:S(2)}) %collective-permute-start.6) | collective-permute-done | bytes 245792 | tf_op jit(solution)/shard_map/ppermute | solution.py:275
  174.0 0.9 maximum_select_fusion
  (82 shorter events, 11.3 us)
Async XLA Ops:
  7.2 124.5 %all-gather.5.cloned.1.call-start = ((), (), s32[]{:S(2)}) async-start(), calls=%async_computation.3 | async-start | bytes 6488064 | tf_op jit(solution)/shard_map/all_gather | solution.py:291
  8.1 12.1 %collective-permute-start = (bf16[2,192,128]{2,1,0:T(8,128)(2,1)S(1)}, bf16[2,192,128]{2,1,0:T(8,128)(2,1)S(1)}, u32[]{:S(2)}, u32[]{:S(2)}) collective-permute-start(bf16[2,192,128]{2,1,0:T(8,128)(2,1)S(1)} %pad_maximum_fusion.4), channel_id=1, source_target_pairs={{0,16},{16,0},{1,17},{17,1},{2,18},{18,2},{3,19},{19,3},{4,20},{20... | collective-permute-start | bytes 294920 | tf_op jit(solution)/shard_map/ppermute | solution.py:224
  12.7 0.9 copy-start
  13.6 0.9 copy-start.1
  14.5 1.0 copy-start.3
  15.6 17.1 %copy-start.4 = (bf16[192,1280]{1,0:T(8,128)(2,1)S(1)}, bf16[192,1280]{1,0:T(8,128)(2,1)}, u32[]{:S(2)}) copy-start(bf16[192,1280]{1,0:T(8,128)(2,1)} %param.12) | copy-start | bytes 1474564
  18.8 60.1 %copy-start.5 = (s32[12288]{0:T(1024)S(1)}, s32[12288]{0:T(1024)}, u32[]{:S(2)}) copy-start(s32[12288]{0:T(1024)} %param.15) | copy-start | bytes 147460
  18.8 60.5 %copy-start.6 = (s32[3,64,32]{1,2,0:T(8,128)S(1)}, s32[3,64,32]{1,2,0:T(8,128)}, u32[]{:S(2)}) copy-start(s32[3,64,32]{1,2,0:T(8,128)} %param.22) | copy-start | bytes 73732
  18.9 61.7 %copy-start.8 = (s32[3,64]{1,0:T(4,128)S(1)}, s32[3,64]{1,0:T(4,128)}, u32[]{:S(2)}) copy-start(s32[3,64]{1,0:T(4,128)} %param.23) | copy-start | bytes 2308
  20.2 80.2 %copy-start.7 = (f32[1280]{0:T(1024)S(1)}, f32[1280]{0:T(1024)}, u32[]{:S(2)}) copy-start(f32[1280]{0:T(1024)} %param.20) | copy-start | bytes 15364
  21.0 46.5 %all-to-all-start = ((bf16[64,3,1408]{2,1,0:T(4,128)(2,1)}), bf16[64,3,1408]{2,1,0:T(4,128)(2,1)S(1)}, u32[]{:S(2)}, u32[]{:S(2)}) async-start(bf16[64,3,1408]{2,1,0:T(4,128)(2,1)} %bitcast.69), calls=%async_computation | async-start | bytes 1441792 | tf_op jit(solution)/shard_map/all_to_all | solution.py:293
  32.7 34.8 %collective-permute-start.1 = (bf16[192,640]{1,0:T(8,128)(2,1)S(1)}, bf16[192,640]{1,0:T(8,128)(2,1)S(1)}, u32[]{:S(2)}, u32[]{:S(2)}) collective-permute-start(bf16[192,640]{1,0:T(8,128)(2,1)S(1)} %get-tuple-element.42), channel_id=1, source_target_pairs={{0,224},{32,192},{64,160},{96,128},{128,96},{160,64},{192,32},{224... | collective-permute-start | bytes 737288 | tf_op jit(solution)/shard_map/ppermute | solution.py:275
  69.3 30.6 %all-to-all-start.1 = ((bf16[64,3,1280]{2,1,0:T(4,128)(2,1)}), bf16[64,3,1280]{2,1,0:T(4,128)(2,1)S(1)}, u32[]{:S(2)}, u32[]{:S(2)}) async-start(bf16[64,3,1280]{2,1,0:T(4,128)(2,1)} %shard_map.132), calls=%async_computation.1 | async-start | bytes 1310720 | tf_op jit(solution)/shard_map/all_to_all | solution.py:297
  79.4 20.9 %collective-permute-start.2 = (bf16[192,640]{1,0:T(8,128)(2,1)S(1)}, bf16[192,640]{1,0:T(8,128)(2,1)S(1)}, u32[]{:S(2)}, u32[]{:S(2)}) collective-permute-start(bf16[192,640]{1,0:T(8,128)(2,1)S(1)} %get-tuple-element.17), channel_id=1, source_target_pairs={{0,16},{16,0},{1,17},{17,1},{2,18},{18,2},{3,19},{19,3},{4,20},{20... | collective-permute-start | bytes 737288 | tf_op jit(solution)/shard_map/ppermute | solution.py:224
  103.9 11.0 %collective-permute-start.5 = (bf16[192,400]{1,0:T(8,128)(2,1)S(1)}, bf16[192,400]{1,0:T(8,128)(2,1)S(1)}, u32[]{:S(2)}, u32[]{:S(2)}) collective-permute-start(bf16[192,400]{1,0:T(8,128)(2,1)S(1)} %get-tuple-element.49), channel_id=1, source_target_pairs={{0,1},{1,0},{2,3},{3,2},{4,5},{5,4},{6,7},{7,6},{8,9},{9,8},{10,11... | collective-permute-start | bytes 460808 | tf_op jit(solution)/shard_map/ppermute | solution.py:323
  111.6 8.1 %collective-permute-start.4 = (bf16[192,400]{1,0:T(8,128)(2,1)S(1)}, bf16[192,400]{1,0:T(8,128)(2,1)S(1)}, u32[]{:S(2)}, u32[]{:S(2)}) collective-permute-start(bf16[192,400]{1,0:T(8,128)(2,1)S(1)} %get-tuple-element.48), channel_id=1, source_target_pairs={{0,2},{1,3},{2,0},{3,1},{4,6},{5,7},{6,4},{7,5},{8,10},{9,11},{10,... | collective-permute-start | bytes 460808 | tf_op jit(solution)/shard_map/ppermute | solution.py:323
  114.6 9.4 %collective-permute-start.3 = (bf16[192,400]{1,0:T(8,128)(2,1)S(1)}, bf16[192,400]{1,0:T(8,128)(2,1)S(1)}, u32[]{:S(2)}, u32[]{:S(2)}) collective-permute-start(bf16[192,400]{1,0:T(8,128)(2,1)S(1)} %get-tuple-element.47), channel_id=1, source_target_pairs={{0,3},{1,2},{2,1},{3,0},{4,7},{5,6},{6,5},{7,4},{8,11},{9,10},{10,... | collective-permute-start | bytes 460808 | tf_op jit(solution)/shard_map/ppermute | solution.py:323
  125.8 32.9 %all-to-all-start.2 = ((f32[64,1,9]{2,1,0:T(1,128)}), f32[64,1,9]{2,1,0:T(1,128)S(1)}, u32[]{:S(2)}, u32[]{:S(2)}) async-start(f32[64,1,9]{2,1,0:T(1,128)} %bitcast.20), calls=%async_computation.2 | async-start | bytes 65536 | tf_op jit(solution)/shard_map/all_to_all | solution.py:350
  131.7 2.8 %copy-start.2 = (bf16[64,2,192,128]{3,2,1,0:T(8,128)(2,1)S(1)}, bf16[64,2,192,128]{3,2,1,0:T(8,128)(2,1)}, u32[]{:S(2)}) copy-start(bf16[64,2,192,128]{3,2,1,0:T(8,128)(2,1)} %all-gather.5.cloned.1.call-done) | copy-start | bytes 18874372
  158.7 12.9 %collective-permute-start.7 = (bf16[192,640]{1,0:T(8,128)(2,1)S(1)}, bf16[192,640]{1,0:T(8,128)(2,1)S(1)}, u32[]{:S(2)}, u32[]{:S(2)}) collective-permute-start(bf16[192,640]{1,0:T(8,128)(2,1)S(1)} %get-tuple-element.40), channel_id=1, source_target_pairs={{0,16},{16,0},{1,17},{17,1},{2,18},{18,2},{3,19},{19,3},{4,20},{20... | collective-permute-start | bytes 737288 | tf_op jit(solution)/shard_map/ppermute | solution.py:224
  159.3 14.7 %collective-permute-start.6 = (bf16[192,640]{1,0:T(8,128)(2,1)S(1)}, bf16[192,640]{1,0:T(8,128)(2,1)S(1)}, u32[]{:S(2)}, u32[]{:S(2)}) collective-permute-start(bf16[192,640]{1,0:T(8,128)(2,1)S(1)} %get-tuple-element.39), channel_id=1, source_target_pairs={{0,224},{32,192},{64,160},{96,128},{128,96},{160,64},{192,32},{224... | collective-permute-start | bytes 737288 | tf_op jit(solution)/shard_map/ppermute | solution.py:275
Sparse Core Ops, SparseCore 0:
  21.1 105.2 all-gather.4

commit v4 on v3

--- a/solution.py
+++ b/solution.py
@@ -140,7 +140,7 @@
             ],
         ),
         compiler_params=pltpu.CompilerParams(
-            vmem_limit_bytes=24 * 2**20, dimension_semantics=("arbitrary",)
+            vmem_limit_bytes=58 * 2**20, dimension_semantics=("arbitrary",)
         ),
         cost_estimate=pl.CostEstimate(
             flops=20_000_000_000, bytes_accessed=8_000_000, transcendentals=10_000_000
@@ -289,9 +289,9 @@
     state = state.reshape(steps, lines, width + HD).transpose(1, 0, 2)
     kv_pair, state = after((kv_pair, state))
     kv_all = lax.all_gather(kv_pair, ("z", "x"), axis=0).reshape((nz, nx) + kv_pair.shape)
+    state, q_far = after((state, q_far))
 
     met = lax.all_to_all(state, CTX, 0, 0, tiled=True)
-    met, q_far = after((met, q_far))
     attention = merge(met)
     q_other, attention = after((q_other, attention))
     spread = lax.all_to_all(attention, CTX, 0, 0, tiled=True).reshape(lines * steps, width)

time: 184 us -> 188 us (1.022)
  the two profiles are of different devices: /device:TPU:1 before, /device:TPU:96 now
where the time goes in v4:
time: 188 us; the launch traced here: 186 us
  waiting for transfers between devices  44.7 us (24%)
  blocking collectives  39.6 us (21%)
  Pallas kernels  35.6 us (19%)
  starting transfers between devices  31.7 us (17%)
  between operations  14.4 us (8%)
  local copies, waits for them, and re-layouts  8.7 us (5%)
  other arithmetic  8.19 us (4%)
  matrix products  3.11 us (2%)
    all_to_all x1, blocking collectives, local(): met = lax.all_to_all(state, CTX, 0, 0, tiled=True)  33 us
    pallas_call x1, Pallas kernels, attend(): pl.pallas_call(attend_kernel, out_shape=jax.ShapeDtypeStruct(q.shape, BF)...  30.5 us
    all_to_all x1, waiting for transfers between devices, local(): lax.all_to_all(attention, CTX, 0, 0, tiled=True)  22 us
    ppermute x2, waiting for transfers between devices, mirror(): return lax.ppermute(value, 'z', [(i, nz - 1 - i) for i in range(nz)])  14.4 us
    all_to_all x1, starting transfers between devices, local(): stats = lax.all_to_all(stats, CTX, 0, 0, tiled=True)  9.08 us
    all_to_all x1, starting transfers between devices, local(): lax.all_to_all(attention, CTX, 0, 0, tiled=True)  8.38 us
    ppermute x3, waiting for transfers between devices, local(): lax.ppermute(jnp.concatenate([sent, extra], axis=1), TP, [(i, i ^ away) f...  8.22 us
    all_gather x1, blocking collectives, local(): stats = lax.all_gather(stats, TP, axis=0)  6.67 us
  transfers between devices with their start and end apart: 11, of which 5 were waited for; matrix products, arithmetic and copies ran while one was open for 7% of the time, Pallas kernels for 19%

profile of v4, /device:TPU:96, one launch (start us, length us, event | category | flops | bytes accessed | tf_op | source)
XLA Modules:
  0.0 186.0 jit_solution(8883415312416707942)
XLA Ops:
  7.2 0.9 select_bitcast_fusion.2
  8.1 1.7 collective-permute-start
  14.0 1.0 copy-done.2
  15.0 3.3 %shard_map.131 = bf16[192,1408]{1,0:T(8,128)(2,1)S(1)} custom-call(bf16[192,1280]{1,0:T(8,128)(2,1)S(1)} %bitcast.72, bf16[192,256]{1,0:T(8,128)(2,1)S(1)} %copy-done.1, bf16[192,256]{1,0:T(8,128)(2,1)S(1)} %copy-done, bf16[16,512]{1,0:T(8,128)(2,1)S(1)} %fusion.8.own_ref, s32[192,256]{1,0:T(8,128)S(1)} %bitcast.71), custom_call_target="tpu_custom_call" | custom-call | flops 4000000000 | bytes 1500000 | tf_op jit(solution)/shard_map/pallas_call | solution.py:209
  19.6 3.2 %collective-permute-start.1 = (bf16[192,640]{1,0:T(8,128)(2,1)S(1)}, bf16[192,640]{1,0:T(8,128)(2,1)S(1)}, u32[]{:S(2)}, u32[]{:S(2)}) collective-permute-start(bf16[192,640]{1,0:T(8,128)(2,1)S(1)} %get-tuple-element.42), channel_id=1, source_target_pairs={{0,224},{32,192},{64,160},{96,128},{128,96},{160,64},{192,32},{224... | collective-permute-start | bytes 737288 | tf_op jit(solution)/shard_map/ppermute | solution.py:275
  22.8 10.9 %collective-permute-done.1 = bf16[192,640]{1,0:T(8,128)(2,1)S(1)} collective-permute-done((bf16[192,640]{1,0:T(8,128)(2,1)S(1)}, bf16[192,640]{1,0:T(8,128)(2,1)S(1)}, u32[]{:S(2)}, u32[]{:S(2)}) %collective-permute-start.1) | collective-permute-done | bytes 245792 | tf_op jit(solution)/shard_map/ppermute | solution.py:275
  33.8 33.0 %all_to_all.22.met_ref = bf16[64,3,1408]{2,1,0:T(4,128)(2,1)S(1)} all-to-all(bf16[64,3,1408]{2,1,0:T(4,128)(2,1)S(1)} %bitcast.73), channel_id=1, replica_groups=mesh['z'=8,'yl'=2,'x'=4,'yh'=2,'core'=2] {'z','yl','x'}, dimensions={0} | all-to-all | bytes 1081344 | tf_op jit(solution)/shard_map/all_to_all | solution.py:294
  66.7 1.9 %shard_map.132 = bf16[64,3,1280]{2,1,0:T(4,128)(2,1)} custom-call(bf16[64,3,1408]{2,1,0:T(4,128)(2,1)S(1)} %all_to_all.22.met_ref), custom_call_target="tpu_custom_call" | custom-call | flops 500000000 | bytes 1500000 | tf_op jit(solution)/shard_map/pallas_call | solution.py:165
  68.6 8.4 %all-to-all-start.1 = ((bf16[64,3,1280]{2,1,0:T(4,128)(2,1)}), bf16[64,3,1280]{2,1,0:T(4,128)(2,1)S(1)}, u32[]{:S(2)}, u32[]{:S(2)}) async-start(bf16[64,3,1280]{2,1,0:T(4,128)(2,1)} %shard_map.132), calls=%async_computation.1 | async-start | bytes 1310720 | tf_op jit(solution)/shard_map/all_to_all | solution.py:297
  77.6 1.6 collective-permute-start.2
  79.2 22.0 %all-to-all-done.1 = bf16[64,3,1280]{2,1,0:T(4,128)(2,1)S(1)} async-done(((bf16[64,3,1280]{2,1,0:T(4,128)(2,1)}), bf16[64,3,1280]{2,1,0:T(4,128)(2,1)S(1)}, u32[]{:S(2)}, u32[]{:S(2)}) %all-to-all-start.1) | async-done | bytes 491552 | tf_op jit(solution)/shard_map/all_to_all | solution.py:297
  101.6 3.1 %fusion.2 = f32[192,1536]{1,0:T(8,128)S(1)} fusion(bf16[1280,1536]{1,0:T(8,128)(2,1)} %param.21, bf16[192,1280]{1,0:T(8,128)(2,1)S(1)} %reshape.217, f32[1280]{0:T(1024)S(1)} %copy-done.6), kind=kOutput, calls=%fused_computation.5 | convolution fusion | flops 755712000 | bytes 5608448 | tf_op jit(solution)/shard_map/dot_general | solution.py:30
  106.6 1.1 broadcast_in_dim_tile.4.row_ref
  107.7 3.0 %collective-permute-start.4 = (bf16[192,400]{1,0:T(8,128)(2,1)S(1)}, bf16[192,400]{1,0:T(8,128)(2,1)S(1)}, u32[]{:S(2)}, u32[]{:S(2)}) collective-permute-start(bf16[192,400]{1,0:T(8,128)(2,1)S(1)} %get-tuple-element.48), channel_id=1, source_target_pairs={{0,2},{1,3},{2,0},{3,1},{4,6},{5,7},{6,4},{7,5},{8,10},{9,11},{10,... | collective-permute-start | bytes 460808 | tf_op jit(solution)/shard_map/ppermute | solution.py:323
  112.0 4.9 %collective-permute-done.4 = bf16[192,400]{1,0:T(8,128)(2,1)S(1)} collective-permute-done((bf16[192,400]{1,0:T(8,128)(2,1)S(1)}, bf16[192,400]{1,0:T(8,128)(2,1)S(1)}, u32[]{:S(2)}, u32[]{:S(2)}) %collective-permute-start.4) | collective-permute-done | bytes 153632 | tf_op jit(solution)/shard_map/ppermute | solution.py:323
  117.0 3.3 %collective-permute-done.3 = bf16[192,400]{1,0:T(8,128)(2,1)S(1)} collective-permute-done((bf16[192,400]{1,0:T(8,128)(2,1)S(1)}, bf16[192,400]{1,0:T(8,128)(2,1)S(1)}, u32[]{:S(2)}, u32[]{:S(2)}) %collective-permute-start.3) | collective-permute-done | bytes 153632 | tf_op jit(solution)/shard_map/ppermute | solution.py:323
  122.1 9.1 %all-to-all-start.2 = ((f32[64,1,9]{2,1,0:T(1,128)}), f32[64,1,9]{2,1,0:T(1,128)S(1)}, u32[]{:S(2)}, u32[]{:S(2)}) async-start(f32[64,1,9]{2,1,0:T(1,128)} %bitcast.20), calls=%async_computation.2 | async-start | bytes 65536 | tf_op jit(solution)/shard_map/all_to_all | solution.py:350
  131.2 30.5 %shard_map.133 = bf16[2,192,640]{2,1,0:T(8,128)(2,1)} custom-call(s32[12]{0:T(128)} %pad_add_fusion.1.plan, bf16[2,192,640]{2,1,0:T(8,128)(2,1)} %pad_maximum_fusion.q_ref, s32[960,1]{1,0:T(8,128)} %broadcast_in_dim_tile.4.row_ref, bf16[8,4,2,2,192,128]{5,4,3,2,1,0:T(8,128)(2,1)} %bitcast.91, bf16[8,4,2,2,192,128]{5,4,3,2,1,0:T(8,128)(2,1)} %bitcast.92), custom_call_target="tpu_custom_call" | custom-call | flops 20000000000 | bytes 8000000 | tf_op jit(solution)/shard_map/pallas_call | solution.py:128
  161.7 1.1 slice_bitcast_fusion.1
  162.8 1.6 collective-permute-start.7
  164.4 2.7 %collective-permute-start.6 = (bf16[192,640]{1,0:T(8,128)(2,1)S(1)}, bf16[192,640]{1,0:T(8,128)(2,1)S(1)}, u32[]{:S(2)}, u32[]{:S(2)}) collective-permute-start(bf16[192,640]{1,0:T(8,128)(2,1)S(1)} %get-tuple-element.39), channel_id=1, source_target_pairs={{0,224},{32,192},{64,160},{96,128},{128,96},{160,64},{192,32},{224... | collective-permute-start | bytes 737288 | tf_op jit(solution)/shard_map/ppermute | solution.py:275
  167.5 6.7 %all-gather.2 = f32[4,3,3]{2,1,0:T(4,128)S(1)} all-gather(f32[1,3,3]{2,1,0:T(4,128)S(1)} %maximum_bitcast_fusion.1), channel_id=3, replica_groups=mesh['z'=8,'yl'=2,'x'=4,'yh'=2,'core'=2] {'yh','core'}, dimensions={0}, use_global_device_ids=true | all-gather | bytes 180 | tf_op jit(solution)/shard_map/all_gather | solution.py:355
  174.8 3.5 %collective-permute-done.6 = bf16[192,640]{1,0:T(8,128)(2,1)S(1)} collective-permute-done((bf16[192,640]{1,0:T(8,128)(2,1)S(1)}, bf16[192,640]{1,0:T(8,128)(2,1)S(1)}, u32[]{:S(2)}, u32[]{:S(2)}) %collective-permute-start.6) | collective-permute-done | bytes 245792 | tf_op jit(solution)/shard_map/ppermute | solution.py:275
  178.3 0.9 maximum_select_fusion
  (79 shorter events, 12.4 us)
Async XLA Ops:
  7.2 124.0 %all-gather.5.cloned.1.call-start = ((), (), s32[]{:S(2)}) async-start(), calls=%async_computation.3 | async-start | bytes 6488064 | tf_op jit(solution)/shard_map/all_gather | solution.py:291
  8.1 10.7 %collective-permute-start = (bf16[2,192,128]{2,1,0:T(8,128)(2,1)S(1)}, bf16[2,192,128]{2,1,0:T(8,128)(2,1)S(1)}, u32[]{:S(2)}, u32[]{:S(2)}) collective-permute-start(bf16[2,192,128]{2,1,0:T(8,128)(2,1)S(1)} %pad_maximum_fusion.4), channel_id=1, source_target_pairs={{0,16},{16,0},{1,17},{17,1},{2,18},{18,2},{3,19},{19,3},{4,20},{20... | collective-permute-start | bytes 294920 | tf_op jit(solution)/shard_map/ppermute | solution.py:224
  12.2 0.9 copy-start
  13.1 0.9 copy-start.1
  14.0 1.0 copy-start.2
  15.0 4.6 %copy-start.3 = (bf16[192,1280]{1,0:T(8,128)(2,1)S(1)}, bf16[192,1280]{1,0:T(8,128)(2,1)}, u32[]{:S(2)}) copy-start(bf16[192,1280]{1,0:T(8,128)(2,1)} %param.12) | copy-start | bytes 1474564
  18.3 58.8 %copy-start.4 = (s32[12288]{0:T(1024)S(1)}, s32[12288]{0:T(1024)}, u32[]{:S(2)}) copy-start(s32[12288]{0:T(1024)} %param.15) | copy-start | bytes 147460
  18.3 59.2 %copy-start.5 = (s32[3,64,32]{1,2,0:T(8,128)S(1)}, s32[3,64,32]{1,2,0:T(8,128)}, u32[]{:S(2)}) copy-start(s32[3,64,32]{1,2,0:T(8,128)} %param.22) | copy-start | bytes 73732
  18.3 60.9 %copy-start.7 = (s32[3,64]{1,0:T(4,128)S(1)}, s32[3,64]{1,0:T(4,128)}, u32[]{:S(2)}) copy-start(s32[3,64]{1,0:T(4,128)} %param.23) | copy-start | bytes 2308
  18.8 82.8 %copy-start.6 = (f32[1280]{0:T(1024)S(1)}, f32[1280]{0:T(1024)}, u32[]{:S(2)}) copy-start(f32[1280]{0:T(1024)} %param.20) | copy-start | bytes 15364
  19.6 14.2 %collective-permute-start.1 = (bf16[192,640]{1,0:T(8,128)(2,1)S(1)}, bf16[192,640]{1,0:T(8,128)(2,1)S(1)}, u32[]{:S(2)}, u32[]{:S(2)}) collective-permute-start(bf16[192,640]{1,0:T(8,128)(2,1)S(1)} %get-tuple-element.42), channel_id=1, source_target_pairs={{0,224},{32,192},{64,160},{96,128},{128,96},{160,64},{192,32},{224... | collective-permute-start | bytes 737288 | tf_op jit(solution)/shard_map/ppermute | solution.py:275
  68.6 32.6 %all-to-all-start.1 = ((bf16[64,3,1280]{2,1,0:T(4,128)(2,1)}), bf16[64,3,1280]{2,1,0:T(4,128)(2,1)S(1)}, u32[]{:S(2)}, u32[]{:S(2)}) async-start(bf16[64,3,1280]{2,1,0:T(4,128)(2,1)} %shard_map.132), calls=%async_computation.1 | async-start | bytes 1310720 | tf_op jit(solution)/shard_map/all_to_all | solution.py:297
  77.6 24.0 %collective-permute-start.2 = (bf16[192,640]{1,0:T(8,128)(2,1)S(1)}, bf16[192,640]{1,0:T(8,128)(2,1)S(1)}, u32[]{:S(2)}, u32[]{:S(2)}) collective-permute-start(bf16[192,640]{1,0:T(8,128)(2,1)S(1)} %get-tuple-element.17), channel_id=1, source_target_pairs={{0,16},{16,0},{1,17},{17,1},{2,18},{18,2},{3,19},{19,3},{4,20},{20... | collective-permute-start | bytes 737288 | tf_op jit(solution)/shard_map/ppermute | solution.py:224
  105.2 6.7 %collective-permute-start.5 = (bf16[192,400]{1,0:T(8,128)(2,1)S(1)}, bf16[192,400]{1,0:T(8,128)(2,1)S(1)}, u32[]{:S(2)}, u32[]{:S(2)}) collective-permute-start(bf16[192,400]{1,0:T(8,128)(2,1)S(1)} %get-tuple-element.49), channel_id=1, source_target_pairs={{0,1},{1,0},{2,3},{3,2},{4,5},{5,4},{6,7},{7,6},{8,9},{9,8},{10,11... | collective-permute-start | bytes 460808 | tf_op jit(solution)/shard_map/ppermute | solution.py:323
  107.7 9.2 %collective-permute-start.4 = (bf16[192,400]{1,0:T(8,128)(2,1)S(1)}, bf16[192,400]{1,0:T(8,128)(2,1)S(1)}, u32[]{:S(2)}, u32[]{:S(2)}) collective-permute-start(bf16[192,400]{1,0:T(8,128)(2,1)S(1)} %get-tuple-element.48), channel_id=1, source_target_pairs={{0,2},{1,3},{2,0},{3,1},{4,6},{5,7},{6,4},{7,5},{8,10},{9,11},{10,... | collective-permute-start | bytes 460808 | tf_op jit(solution)/shard_map/ppermute | solution.py:323
  110.7 9.7 %collective-permute-start.3 = (bf16[192,400]{1,0:T(8,128)(2,1)S(1)}, bf16[192,400]{1,0:T(8,128)(2,1)S(1)}, u32[]{:S(2)}, u32[]{:S(2)}) collective-permute-start(bf16[192,400]{1,0:T(8,128)(2,1)S(1)} %get-tuple-element.47), channel_id=1, source_target_pairs={{0,3},{1,2},{2,1},{3,0},{4,7},{5,6},{6,5},{7,4},{8,11},{9,10},{10,... | collective-permute-start | bytes 460808 | tf_op jit(solution)/shard_map/ppermute | solution.py:323
  122.1 39.6 %all-to-all-start.2 = ((f32[64,1,9]{2,1,0:T(1,128)}), f32[64,1,9]{2,1,0:T(1,128)S(1)}, u32[]{:S(2)}, u32[]{:S(2)}) async-start(f32[64,1,9]{2,1,0:T(1,128)} %bitcast.20), calls=%async_computation.2 | async-start | bytes 65536 | tf_op jit(solution)/shard_map/all_to_all | solution.py:350
  162.8 12.0 %collective-permute-start.7 = (bf16[192,640]{1,0:T(8,128)(2,1)S(1)}, bf16[192,640]{1,0:T(8,128)(2,1)S(1)}, u32[]{:S(2)}, u32[]{:S(2)}) collective-permute-start(bf16[192,640]{1,0:T(8,128)(2,1)S(1)} %get-tuple-element.40), channel_id=1, source_target_pairs={{0,16},{16,0},{1,17},{17,1},{2,18},{18,2},{3,19},{19,3},{4,20},{20... | collective-permute-start | bytes 737288 | tf_op jit(solution)/shard_map/ppermute | solution.py:224
  164.4 13.9 %collective-permute-start.6 = (bf16[192,640]{1,0:T(8,128)(2,1)S(1)}, bf16[192,640]{1,0:T(8,128)(2,1)S(1)}, u32[]{:S(2)}, u32[]{:S(2)}) collective-permute-start(bf16[192,640]{1,0:T(8,128)(2,1)S(1)} %get-tuple-element.39), channel_id=1, source_target_pairs={{0,224},{32,192},{64,160},{96,128},{128,96},{160,64},{192,32},{224... | collective-permute-start | bytes 737288 | tf_op jit(solution)/shard_map/ppermute | solution.py:275
Sparse Core Ops, SparseCore 0:
  19.7 103.1 all-gather.4

commit v5 on v4

--- a/solution.py
+++ b/solution.py
@@ -48,8 +48,8 @@
     return which, tile
 
 
-def attend_kernel(plan, q_ref, row_ref, k_ref, v_ref, out_ref, qs, peak, acc):
-    blocks, rows, width = q_ref.shape
+def attend_kernel(plan, qa_ref, qb_ref, row_ref, k_ref, v_ref, outa_ref, outb_ref, qs, peak, acc):
+    rows, width = qa_ref.shape
     group = width // HD
     keys = k_ref.shape[1] * rows
     step = pl.program_id(0)
@@ -58,9 +58,9 @@
 
     @pl.when(step == 0)
     def _():
-        for b in range(blocks):
+        for b, q_ref in enumerate((qa_ref, qb_ref)):
             for h in range(group):
-                q = q_ref[b, :, h * HD : (h + 1) * HD].astype(F32) * (HD**-0.5 * LOG2E)
+                q = q_ref[:, h * HD : (h + 1) * HD].astype(F32) * (HD**-0.5 * LOG2E)
                 high, low = two_parts(q)
                 qs[b, h * rows : (h + 1) * rows, 0:HD] = high
                 qs[b, h * rows : (h + 1) * rows, HD:] = low
@@ -103,14 +103,14 @@
 
     @pl.when(step == pl.num_programs(0) - 1)
     def _():
-        for b in range(blocks):
+        for b, out_ref in enumerate((outa_ref, outb_ref)):
             for h in range(group):
                 here = slice(h * rows, (h + 1) * rows)
-                out_ref[b, :, h * HD : (h + 1) * HD] = (acc[b, here, 0:HD] / acc[b, here, HD:]).astype(BF)
-
-
-def attend(plan, q, row, kv):
-    blocks, rows, width = q.shape
+                out_ref[:, h * HD : (h + 1) * HD] = (acc[b, here, 0:HD] / acc[b, here, HD:]).astype(BF)
+
+
+def attend(plan, qa, qb, row, kv):
+    rows, width = qa.shape
     nz, nx, ny, _, _, _ = kv.shape
     keys = nx * rows
 
@@ -127,16 +127,16 @@
     flat = width // HD * rows
     return pl.pallas_call(
         attend_kernel,
-        out_shape=jax.ShapeDtypeStruct(q.shape, BF),
+        out_shape=[jax.ShapeDtypeStruct(qa.shape, BF)] * 2,
         grid_spec=pltpu.PrefetchScalarGridSpec(
             num_scalar_prefetch=1,
             grid=(nz * ny + 2,),
-            in_specs=[whole(q.shape), whole(row.shape), tiles(0), tiles(1)],
-            out_specs=whole(q.shape),
+            in_specs=[whole(qa.shape), whole(qb.shape), whole(row.shape), tiles(0), tiles(1)],
+            out_specs=[whole(qa.shape)] * 2,
             scratch_shapes=[
-                pltpu.VMEM((blocks, flat, 2 * HD), BF),
-                pltpu.VMEM((blocks, flat, 1), F32),
-                pltpu.VMEM((blocks, flat, 2 * HD), F32),
+                pltpu.VMEM((2, flat, 2 * HD), BF),
+                pltpu.VMEM((2, flat, 1), F32),
+                pltpu.VMEM((2, flat, 2 * HD), F32),
             ],
         ),
         compiler_params=pltpu.CompilerParams(
@@ -145,7 +145,7 @@
         cost_estimate=pl.CostEstimate(
             flops=20_000_000_000, bytes_accessed=8_000_000, transcendentals=10_000_000
         ),
-    )(plan, q, row, kv, kv)
+    )(plan, qa, qb, row, kv, kv)
 
 
 def merge_kernel(met_ref, out_ref):
@@ -287,9 +287,8 @@
         keep.astype(jnp.int32).reshape(steps * lines, 256),
     )
     state = state.reshape(steps, lines, width + HD).transpose(1, 0, 2)
-    kv_pair, state = after((kv_pair, state))
+    kv_pair, state, q_far = after((kv_pair, state, q_far))
     kv_all = lax.all_gather(kv_pair, ("z", "x"), axis=0).reshape((nz, nx) + kv_pair.shape)
-    state, q_far = after((state, q_far))
 
     met = lax.all_to_all(state, CTX, 0, 0, tiled=True)
     attention = merge(met)
@@ -345,11 +344,11 @@
         return peak, mass, jnp.sum(target, axis=axis)
 
     stats = jnp.stack([top, mass, target], axis=-1).reshape(lines, steps * 3)
-    q_both, stats = after((jnp.stack([q_near, q_far]), stats))
-    output = attend(plan, q_both, row, kv_all)
+    q_near, q_far, stats = after((q_near, q_far, stats))
+    near, far = attend(plan, q_near, q_far, row, kv_all)
     stats = lax.all_to_all(stats, CTX, 0, 0, tiled=True)
-    stats, output = after((stats, output))
-    out_other, out_mine = swap(output[0], "yl"), mirror(output[1])
+    stats, near, far = after((stats, near, far))
+    out_other, out_mine = swap(near, "yl"), mirror(far)
     stats = stats.reshape(nctx, steps, 3)
     stats = jnp.stack(joined(*(stats[..., i] for i in range(3)), 0))
     stats = lax.all_gather(stats, TP, axis=0)

time: 188 us -> 173 us (0.920)
  waiting for transfers between devices: 44.7 us -> 32.5 us
  starting transfers between devices: 31.7 us -> 28.9 us
    ppermute x2, waiting for transfers between devices: 14.4 us -> 4.79 us  [mirror(): return lax.ppermute(value, 'z', [(i, nz - 1 - i) for i in range(nz)])]
    all_to_all x1, waiting for transfers between devices: 22 us -> 14.3 us  [local(): lax.all_to_all(attention, CTX, 0, 0, tiled=True)]
    all_gather x1, waiting for transfers between devices: 0.02 us -> 5.55 us  [local(): lax.all_gather(kv_pair, ('z', 'x'), axis=0)]
  transfers between devices with their start and end apart: 11 -> 11, of which waited for: 5 -> 6; matrix products, arithmetic and copies ran while one was open for 7% -> 9% of each run, Pallas kernels for 19% -> 21%
where the time goes in v5:
time: 173 us; the launch traced here: 171 us
  blocking collectives  39.8 us (23%)
  Pallas kernels  35.8 us (21%)
  waiting for transfers between devices  32.5 us (19%)
  starting transfers between devices  28.9 us (17%)
  between operations  14.4 us (8%)
  other arithmetic  8.51 us (5%)
  local copies, waits for them, and re-layouts  7.58 us (4%)
  matrix products  3.17 us (2%)
    all_to_all x1, blocking collectives, local(): met = lax.all_to_all(state, CTX, 0, 0, tiled=True)  32.3 us
    pallas_call x1, Pallas kernels, attend(): pl.pallas_call(attend_kernel, out_shape=[jax.ShapeDtypeStruct(qa.shape, B...  30.6 us
    all_to_all x1, waiting for transfers between devices, local(): lax.all_to_all(attention, CTX, 0, 0, tiled=True)  14.3 us
    all_to_all x1, starting transfers between devices, local(): lax.all_to_all(attention, CTX, 0, 0, tiled=True)  8.34 us
    ppermute x3, waiting for transfers between devices, local(): lax.ppermute(jnp.concatenate([sent, extra], axis=1), TP, [(i, i ^ away) f...  7.84 us
    all_to_all x1, starting transfers between devices, local(): stats = lax.all_to_all(stats, CTX, 0, 0, tiled=True)  7.71 us
    all_gather x1, blocking collectives, local(): stats = lax.all_gather(stats, TP, axis=0)  7.52 us
    all_gather x1, waiting for transfers between devices, local(): lax.all_gather(kv_pair, ('z', 'x'), axis=0)  5.55 us
  transfers between devices with their start and end apart: 11, of which 6 were waited for; matrix products, arithmetic and copies ran while one was open for 9% of the time, Pallas kernels for 21%

profile of v5, /device:TPU:96, one launch (start us, length us, event | category | flops | bytes accessed | tf_op | source)
XLA Modules:
  0.0 170.6 jit_solution(255083217484551164)
XLA Ops:
  8.1 1.7 collective-permute-start
  9.8 1.1 broadcast_select_fusion
  10.9 3.2 %collective-permute-start.1 = (bf16[192,640]{1,0:T(8,128)(2,1)S(1)}, bf16[192,640]{1,0:T(8,128)(2,1)S(1)}, u32[]{:S(2)}, u32[]{:S(2)}) collective-permute-start(bf16[192,640]{1,0:T(8,128)(2,1)S(1)} %get-tuple-element.45), channel_id=1, source_target_pairs={{0,224},{32,192},{64,160},{96,128},{128,96},{160,64},{192,32},{224... | collective-permute-start | bytes 737288 | tf_op jit(solution)/shard_map/ppermute | solution.py:275
  18.3 1.0 copy-done.2
  19.3 3.3 %shard_map.131 = bf16[192,1408]{1,0:T(8,128)(2,1)S(1)} custom-call(bf16[192,1280]{1,0:T(8,128)(2,1)S(1)} %bitcast.66, bf16[192,256]{1,0:T(8,128)(2,1)S(1)} %copy-done.1, bf16[192,256]{1,0:T(8,128)(2,1)S(1)} %copy-done, bf16[16,512]{1,0:T(8,128)(2,1)S(1)} %fusion.8.own_ref, s32[192,256]{1,0:T(8,128)S(1)} %bitcast.65), custom_call_target="tpu_custom_call" | custom-call | flops 4000000000 | bytes 1500000 | tf_op jit(solution)/shard_map/pallas_call | solution.py:209
  23.9 1.2 collective-permute-done.1.qb_ref
  25.1 32.3 %all_to_all.22.met_ref = bf16[64,3,1408]{2,1,0:T(4,128)(2,1)S(1)} all-to-all(bf16[64,3,1408]{2,1,0:T(4,128)(2,1)S(1)} %bitcast.67), channel_id=1, replica_groups=mesh['z'=8,'yl'=2,'x'=4,'yh'=2,'core'=2] {'z','yl','x'}, dimensions={0} | all-to-all | bytes 1081344 | tf_op jit(solution)/shard_map/all_to_all | solution.py:293
  57.4 1.9 %shard_map.132 = bf16[64,3,1280]{2,1,0:T(4,128)(2,1)} custom-call(bf16[64,3,1408]{2,1,0:T(4,128)(2,1)S(1)} %all_to_all.22.met_ref), custom_call_target="tpu_custom_call" | custom-call | flops 500000000 | bytes 1500000 | tf_op jit(solution)/shard_map/pallas_call | solution.py:165
  59.3 8.3 %all-to-all-start.1 = ((bf16[64,3,1280]{2,1,0:T(4,128)(2,1)}), bf16[64,3,1280]{2,1,0:T(4,128)(2,1)S(1)}, u32[]{:S(2)}, u32[]{:S(2)}) async-start(bf16[64,3,1280]{2,1,0:T(4,128)(2,1)} %shard_map.132), calls=%async_computation.1 | async-start | bytes 1310720 | tf_op jit(solution)/shard_map/all_to_all | solution.py:296
  68.0 1.6 collective-permute-start.2
  69.7 14.3 %all-to-all-done.1 = bf16[64,3,1280]{2,1,0:T(4,128)(2,1)S(1)} async-done(((bf16[64,3,1280]{2,1,0:T(4,128)(2,1)}), bf16[64,3,1280]{2,1,0:T(4,128)(2,1)S(1)}, u32[]{:S(2)}, u32[]{:S(2)}) %all-to-all-start.1) | async-done | bytes 491552 | tf_op jit(solution)/shard_map/all_to_all | solution.py:296
  84.4 3.2 %fusion.2 = f32[192,1536]{1,0:T(8,128)S(1)} fusion(bf16[1280,1536]{1,0:T(8,128)(2,1)} %param.21, bf16[192,1280]{1,0:T(8,128)(2,1)S(1)} %reshape.217, f32[1280]{0:T(1024)S(1)} %copy-done.5), kind=kOutput, calls=%fused_computation.5 | convolution fusion | flops 755712000 | bytes 5608448 | tf_op jit(solution)/shard_map/dot_general | solution.py:30
  88.3 3.1 %collective-permute-start.4 = (bf16[192,400]{1,0:T(8,128)(2,1)S(1)}, bf16[192,400]{1,0:T(8,128)(2,1)S(1)}, u32[]{:S(2)}, u32[]{:S(2)}) collective-permute-start(bf16[192,400]{1,0:T(8,128)(2,1)S(1)} %get-tuple-element.52), channel_id=1, source_target_pairs={{0,2},{1,3},{2,0},{3,1},{4,6},{5,7},{6,4},{7,5},{8,10},{9,11},{10,... | collective-permute-start | bytes 460808 | tf_op jit(solution)/shard_map/ppermute | solution.py:322
  92.8 1.1 broadcast_in_dim_tile.4.row_ref
  94.4 2.8 %collective-permute-done.4 = bf16[192,400]{1,0:T(8,128)(2,1)S(1)} collective-permute-done((bf16[192,400]{1,0:T(8,128)(2,1)S(1)}, bf16[192,400]{1,0:T(8,128)(2,1)S(1)}, u32[]{:S(2)}, u32[]{:S(2)}) %collective-permute-start.4) | collective-permute-done | bytes 153632 | tf_op jit(solution)/shard_map/ppermute | solution.py:322
  97.3 5.0 %collective-permute-done.3 = bf16[192,400]{1,0:T(8,128)(2,1)S(1)} collective-permute-done((bf16[192,400]{1,0:T(8,128)(2,1)S(1)}, bf16[192,400]{1,0:T(8,128)(2,1)S(1)}, u32[]{:S(2)}, u32[]{:S(2)}) %collective-permute-start.3) | collective-permute-done | bytes 153632 | tf_op jit(solution)/shard_map/ppermute | solution.py:322
  104.0 7.7 %all-to-all-start.2 = ((f32[64,1,9]{2,1,0:T(1,128)}), f32[64,1,9]{2,1,0:T(1,128)S(1)}, u32[]{:S(2)}, u32[]{:S(2)}) async-start(f32[64,1,9]{2,1,0:T(1,128)} %bitcast.18), calls=%async_computation.2 | async-start | bytes 65536 | tf_op jit(solution)/shard_map/all_to_all | solution.py:349
  111.7 5.5 %all-gather.5.cloned.1.call-done = bf16[64,2,192,128]{3,2,1,0:T(8,128)(2,1)} async-done(((bf16[2,2,192,128]{3,2,1,0:T(8,128)(2,1)}), bf16[64,2,192,128]{3,2,1,0:T(8,128)(2,1)}) %all-gather.5.cloned.1.call-update) | async-done | bytes 6291472 | tf_op jit(solution)/shard_map/all_gather | solution.py:291
  117.3 30.6 %shard_map.133 = (bf16[192,640]{1,0:T(8,128)(2,1)}, bf16[192,640]{1,0:T(8,128)(2,1)}) custom-call(s32[12]{0:T(128)} %pad_add_fusion.1.plan, bf16[192,640]{1,0:T(8,128)(2,1)} %copy-done.8, bf16[192,640]{1,0:T(8,128)(2,1)} %copy-done.7, s32[960,1]{1,0:T(8,128)} %broadcast_in_dim_tile.4.row_ref, bf16[8,4,2,2,192,128]{5,4,3,2,1,0:T(8,128)(2,1)} %bitcast.83, ...), custom_call_target="tpu_custom_call" | custom-call | flops 20000000000 | bytes 8000000 | tf_op jit(solution)/shard_map/pallas_call | solution.py:128
  147.9 1.5 collective-permute-start.7
  149.4 1.3 collective-permute-start.6
  151.1 7.5 %all-gather.2 = f32[4,3,3]{2,1,0:T(4,128)S(1)} all-gather(f32[1,3,3]{2,1,0:T(4,128)S(1)} %maximum_bitcast_fusion.1), channel_id=3, replica_groups=mesh['z'=8,'yl'=2,'x'=4,'yh'=2,'core'=2] {'yh','core'}, dimensions={0}, use_global_device_ids=true | all-gather | bytes 180 | tf_op jit(solution)/shard_map/all_gather | solution.py:354
  159.2 3.6 %collective-permute-done.6 = bf16[192,640]{1,0:T(8,128)(2,1)S(1)} collective-permute-done((bf16[192,640]{1,0:T(8,128)(2,1)}, bf16[192,640]{1,0:T(8,128)(2,1)S(1)}, u32[]{:S(2)}, u32[]{:S(2)}) %collective-permute-start.6) | collective-permute-done | bytes 245792 | tf_op jit(solution)/shard_map/ppermute | solution.py:275
  162.8 0.9 maximum_select_fusion
  (79 shorter events, 12.4 us)
Async XLA Ops:
  7.2 110.1 %all-gather.5.cloned.1.call-start = ((), (), s32[]{:S(2)}) async-start(), calls=%async_computation.3 | async-start | bytes 6488064 | tf_op jit(solution)/shard_map/all_gather | solution.py:291
  8.1 15.0 %collective-permute-start = (bf16[2,192,128]{2,1,0:T(8,128)(2,1)S(1)}, bf16[2,192,128]{2,1,0:T(8,128)(2,1)S(1)}, u32[]{:S(2)}, u32[]{:S(2)}) collective-permute-start(bf16[2,192,128]{2,1,0:T(8,128)(2,1)S(1)} %pad_maximum_fusion.3), channel_id=1, source_target_pairs={{0,16},{16,0},{1,17},{17,1},{2,18},{18,2},{3,19},{19,3},{4,20},{20... | collective-permute-start | bytes 294920 | tf_op jit(solution)/shard_map/ppermute | solution.py:224
  10.9 14.2 %collective-permute-start.1 = (bf16[192,640]{1,0:T(8,128)(2,1)S(1)}, bf16[192,640]{1,0:T(8,128)(2,1)S(1)}, u32[]{:S(2)}, u32[]{:S(2)}) collective-permute-start(bf16[192,640]{1,0:T(8,128)(2,1)S(1)} %get-tuple-element.45), channel_id=1, source_target_pairs={{0,224},{32,192},{64,160},{96,128},{128,96},{160,64},{192,32},{224... | collective-permute-start | bytes 737288 | tf_op jit(solution)/shard_map/ppermute | solution.py:275
  16.5 0.9 copy-start
  17.4 0.9 copy-start.1
  18.3 1.0 copy-start.2
  22.6 45.1 %copy-start.4 = (s32[3,64,32]{1,2,0:T(8,128)S(1)}, s32[3,64,32]{1,2,0:T(8,128)}, u32[]{:S(2)}) copy-start(s32[3,64,32]{1,2,0:T(8,128)} %param.22) | copy-start | bytes 73732
  22.6 45.2 %copy-start.3 = (s32[12288]{0:T(1024)S(1)}, s32[12288]{0:T(1024)}, u32[]{:S(2)}) copy-start(s32[12288]{0:T(1024)} %param.15) | copy-start | bytes 147460
  22.6 47.0 %copy-start.6 = (s32[3,64]{1,0:T(4,128)S(1)}, s32[3,64]{1,0:T(4,128)}, u32[]{:S(2)}) copy-start(s32[3,64]{1,0:T(4,128)} %param.23) | copy-start | bytes 2308
  22.7 61.7 %copy-start.5 = (f32[1280]{0:T(1024)S(1)}, f32[1280]{0:T(1024)}, u32[]{:S(2)}) copy-start(f32[1280]{0:T(1024)} %param.20) | copy-start | bytes 15364
  25.1 62.5 %copy-start.7 = (bf16[192,640]{1,0:T(8,128)(2,1)}, bf16[192,640]{1,0:T(8,128)(2,1)S(1)}, u32[]{:S(2)}) copy-start(bf16[192,640]{1,0:T(8,128)(2,1)S(1)} %collective-permute-done.1.qb_ref) | copy-start | bytes 737284
  59.3 24.7 %all-to-all-start.1 = ((bf16[64,3,1280]{2,1,0:T(4,128)(2,1)}), bf16[64,3,1280]{2,1,0:T(4,128)(2,1)S(1)}, u32[]{:S(2)}, u32[]{:S(2)}) async-start(bf16[64,3,1280]{2,1,0:T(4,128)(2,1)} %shard_map.132), calls=%async_computation.1 | async-start | bytes 1310720 | tf_op jit(solution)/shard_map/all_to_all | solution.py:296
  68.0 16.3 %collective-permute-start.2 = (bf16[192,640]{1,0:T(8,128)(2,1)S(1)}, bf16[192,640]{1,0:T(8,128)(2,1)S(1)}, u32[]{:S(2)}, u32[]{:S(2)}) collective-permute-start(bf16[192,640]{1,0:T(8,128)(2,1)S(1)} %get-tuple-element.19), channel_id=1, source_target_pairs={{0,16},{16,0},{1,17},{17,1},{2,18},{18,2},{3,19},{19,3},{4,20},{20... | collective-permute-start | bytes 737288 | tf_op jit(solution)/shard_map/ppermute | solution.py:224
  84.4 3.7 %copy-start.8 = (bf16[192,640]{1,0:T(8,128)(2,1)}, bf16[192,640]{1,0:T(8,128)(2,1)S(1)}, u32[]{:S(2)}) copy-start(bf16[192,640]{1,0:T(8,128)(2,1)S(1)} %collective-permute-done.2.qa_ref) | copy-start | bytes 737284
  88.0 6.2 %collective-permute-start.5 = (bf16[192,400]{1,0:T(8,128)(2,1)S(1)}, bf16[192,400]{1,0:T(8,128)(2,1)S(1)}, u32[]{:S(2)}, u32[]{:S(2)}) collective-permute-start(bf16[192,400]{1,0:T(8,128)(2,1)S(1)} %get-tuple-element.53), channel_id=1, source_target_pairs={{0,1},{1,0},{2,3},{3,2},{4,5},{5,4},{6,7},{7,6},{8,9},{9,8},{10,11... | collective-permute-start | bytes 460808 | tf_op jit(solution)/shard_map/ppermute | solution.py:322
  88.3 8.9 %collective-permute-start.4 = (bf16[192,400]{1,0:T(8,128)(2,1)S(1)}, bf16[192,400]{1,0:T(8,128)(2,1)S(1)}, u32[]{:S(2)}, u32[]{:S(2)}) collective-permute-start(bf16[192,400]{1,0:T(8,128)(2,1)S(1)} %get-tuple-element.52), channel_id=1, source_target_pairs={{0,2},{1,3},{2,0},{3,1},{4,6},{5,7},{6,4},{7,5},{8,10},{9,11},{10,... | collective-permute-start | bytes 460808 | tf_op jit(solution)/shard_map/ppermute | solution.py:322
  93.9 8.4 %collective-permute-start.3 = (bf16[192,400]{1,0:T(8,128)(2,1)S(1)}, bf16[192,400]{1,0:T(8,128)(2,1)S(1)}, u32[]{:S(2)}, u32[]{:S(2)}) collective-permute-start(bf16[192,400]{1,0:T(8,128)(2,1)S(1)} %get-tuple-element.51), channel_id=1, source_target_pairs={{0,3},{1,2},{2,1},{3,0},{4,7},{5,6},{6,5},{7,4},{8,11},{9,10},{10,... | collective-permute-start | bytes 460808 | tf_op jit(solution)/shard_map/ppermute | solution.py:322
  104.0 43.9 %all-to-all-start.2 = ((f32[64,1,9]{2,1,0:T(1,128)}), f32[64,1,9]{2,1,0:T(1,128)S(1)}, u32[]{:S(2)}, u32[]{:S(2)}) async-start(f32[64,1,9]{2,1,0:T(1,128)} %bitcast.18), calls=%async_computation.2 | async-start | bytes 65536 | tf_op jit(solution)/shard_map/all_to_all | solution.py:349
  147.9 11.3 %collective-permute-start.7 = (bf16[192,640]{1,0:T(8,128)(2,1)}, bf16[192,640]{1,0:T(8,128)(2,1)S(1)}, u32[]{:S(2)}, u32[]{:S(2)}) collective-permute-start(bf16[192,640]{1,0:T(8,128)(2,1)} %get-tuple-element.30), channel_id=1, source_target_pairs={{0,16},{16,0},{1,17},{17,1},{2,18},{18,2},{3,19},{19,3},{4,20},{20... | collective-permute-start | bytes 737288 | tf_op jit(solution)/shard_map/ppermute | solution.py:224
  149.4 13.4 %collective-permute-start.6 = (bf16[192,640]{1,0:T(8,128)(2,1)}, bf16[192,640]{1,0:T(8,128)(2,1)S(1)}, u32[]{:S(2)}, u32[]{:S(2)}) collective-permute-start(bf16[192,640]{1,0:T(8,128)(2,1)} %get-tuple-element.29), channel_id=1, source_target_pairs={{0,224},{32,192},{64,160},{96,128},{128,96},{160,64},{192,32},{224... | collective-permute-start | bytes 737288 | tf_op jit(solution)/shard_map/ppermute | solution.py:275
Sparse Core Ops, SparseCore 0:
  25.2 92.0 all-gather.4

commit v6 on v5

--- a/solution.py
+++ b/solution.py
@@ -275,20 +275,22 @@
         return lax.ppermute(value, "z", [(i, nz - 1 - i) for i in range(nz)])
 
     q_mine, q_other = mine_and_other(prefill_queries, half)
+    own = jnp.concatenate([decode_keys[:, 0], decode_values[:, 0]], axis=1)
+    own = jnp.pad(own, ((0, 16 - steps), (0, 0)))
+    keep = keep.astype(jnp.int32).reshape(steps * lines, 256)
+    kv_pair, keep, own, q_mine = after((kv_pair, keep, own, q_mine))
+    kv_all = lax.all_gather(kv_pair, ("z", "x"), axis=0).reshape((nz, nx) + kv_pair.shape)
     q_far = mirror(q_mine)
-
-    own = jnp.concatenate([decode_keys[:, 0], decode_values[:, 0]], axis=1)
     state = states(
         (steps, lines, kv_heads, group),
         decode_queries.reshape(steps * lines, width),
         prefill_keys,
         prefill_values,
-        jnp.pad(own, ((0, 16 - steps), (0, 0))),
-        keep.astype(jnp.int32).reshape(steps * lines, 256),
+        own,
+        keep,
     )
     state = state.reshape(steps, lines, width + HD).transpose(1, 0, 2)
-    kv_pair, state, q_far = after((kv_pair, state, q_far))
-    kv_all = lax.all_gather(kv_pair, ("z", "x"), axis=0).reshape((nz, nx) + kv_pair.shape)
+    state, q_far = after((state, q_far))
 
     met = lax.all_to_all(state, CTX, 0, 0, tiled=True)
     attention = merge(met)
@@ -296,11 +298,11 @@
     spread = lax.all_to_all(attention, CTX, 0, 0, tiled=True).reshape(lines * steps, width)
 
     q_near = swap(q_other, "yl")
-    spread, q_near = after((spread, q_near))
     row = jnp.tile(jnp.arange(rows, dtype=jnp.int32), group)[:, None]
     first_rows = jnp.stack([((z * ny + 1 - yl) * nx + x) * rows, ((nz - 1 - z) * ny + yl) * nx * rows + x * rows])
     first_keys = jnp.max(jnp.where(begins[None, :] <= first_rows[:, None], begins[None, :], 0), axis=1)
     plan = jnp.concatenate([first_keys, first_rows, begins])
+    spread, q_near, row, plan = after((spread, q_near, row, plan))
 
     widened = spread.astype(F32)
     squares = jnp.sum(widened * widened, axis=1, keepdims=True)

time: 173 us -> 180 us (1.040)
  waiting for transfers between devices: 32.5 us -> 36.7 us
  starting transfers between devices: 28.9 us -> 32 us
    all_to_all x1, waiting for transfers between devices: 14.3 us -> 21.5 us  [local(): lax.all_to_all(attention, CTX, 0, 0, tiled=True)]
    all_gather x1, waiting for transfers between devices: 5.55 us -> 0.02 us  [local(): lax.all_gather(kv_pair, ('z', 'x'), axis=0)]
    ppermute x2, waiting for transfers between devices: 4.79 us -> 7.93 us  [mirror(): return lax.ppermute(value, 'z', [(i, nz - 1 - i) for i in range(nz)])]
  transfers between devices with their start and end apart: 11 -> 11, of which waited for: 6 -> 5; matrix products, arithmetic and copies ran while one was open for 9% -> 8% of each run, Pallas kernels for 21% -> 20%
where the time goes in v6:
time: 180 us; the launch traced here: 177 us
  blocking collectives  39.4 us (22%)
  waiting for transfers between devices  36.7 us (20%)
  Pallas kernels  35.8 us (20%)
  starting transfers between devices  32 us (18%)
  between operations  14.4 us (8%)
  other arithmetic  8.36 us (5%)
  local copies, waits for them, and re-layouts  7.54 us (4%)
  matrix products  3.2 us (2%)
    all_to_all x1, blocking collectives, local(): met = lax.all_to_all(state, CTX, 0, 0, tiled=True)  32.8 us
    pallas_call x1, Pallas kernels, attend(): pl.pallas_call(attend_kernel, out_shape=[jax.ShapeDtypeStruct(qa.shape, B...  30.6 us
    all_to_all x1, waiting for transfers between devices, local(): lax.all_to_all(attention, CTX, 0, 0, tiled=True)  21.5 us
    all_to_all x1, starting transfers between devices, local(): stats = lax.all_to_all(stats, CTX, 0, 0, tiled=True)  9 us
    all_to_all x1, starting transfers between devices, local(): lax.all_to_all(attention, CTX, 0, 0, tiled=True)  8.55 us
    ppermute x2, waiting for transfers between devices, mirror(): return lax.ppermute(value, 'z', [(i, nz - 1 - i) for i in range(nz)])  7.93 us
    ppermute x3, waiting for transfers between devices, local(): lax.ppermute(jnp.concatenate([sent, extra], axis=1), TP, [(i, i ^ away) f...  7.22 us
    all_gather x1, blocking collectives, local(): stats = lax.all_gather(stats, TP, axis=0)  6.67 us
  transfers between devices with their start and end apart: 11, of which 5 were waited for; matrix products, arithmetic and copies ran while one was open for 8% of the time, Pallas kernels for 20%

profile of v6, /device:TPU:96, one launch (start us, length us, event | category | flops | bytes accessed | tf_op | source)
XLA Modules:
  0.0 177.4 jit_solution(6728440665641805544)
XLA Ops:
  7.2 0.9 select_bitcast_fusion.2
  8.1 1.7 collective-permute-start
  9.8 1.1 broadcast_select_fusion
  14.0 3.2 %collective-permute-start.1 = (bf16[192,640]{1,0:T(8,128)(2,1)S(1)}, bf16[192,640]{1,0:T(8,128)(2,1)S(1)}, u32[]{:S(2)}, u32[]{:S(2)}) collective-permute-start(bf16[192,640]{1,0:T(8,128)(2,1)S(1)} %get-tuple-element.24), channel_id=1, source_target_pairs={{0,224},{32,192},{64,160},{96,128},{128,96},{160,64},{192,32},{224... | collective-permute-start | bytes 737288 | tf_op jit(solution)/shard_map/ppermute | solution.py:275
  19.0 1.0 copy-done.2
  20.0 3.3 %shard_map.131 = bf16[192,1408]{1,0:T(8,128)(2,1)S(1)} custom-call(bf16[192,1280]{1,0:T(8,128)(2,1)S(1)} %bitcast.66, bf16[192,256]{1,0:T(8,128)(2,1)S(1)} %copy-done.1, bf16[192,256]{1,0:T(8,128)(2,1)S(1)} %copy-done, bf16[16,512]{1,0:T(8,128)(2,1)S(1)} %fusion.8.own_ref, s32[192,256]{1,0:T(8,128)S(1)} %bitcast.65), custom_call_target="tpu_custom_call" | custom-call | flops 4000000000 | bytes 1500000 | tf_op jit(solution)/shard_map/pallas_call | solution.py:209
  23.8 4.3 %collective-permute-done.1.qb_ref = bf16[192,640]{1,0:T(8,128)(2,1)S(1)} collective-permute-done((bf16[192,640]{1,0:T(8,128)(2,1)S(1)}, bf16[192,640]{1,0:T(8,128)(2,1)S(1)}, u32[]{:S(2)}, u32[]{:S(2)}) %collective-permute-start.1) | collective-permute-done | bytes 245792 | tf_op jit(solution)/shard_map/ppermute | solution.py:275
  28.2 32.8 %all_to_all.22.met_ref = bf16[64,3,1408]{2,1,0:T(4,128)(2,1)S(1)} all-to-all(bf16[64,3,1408]{2,1,0:T(4,128)(2,1)S(1)} %bitcast.67), channel_id=1, replica_groups=mesh['z'=8,'yl'=2,'x'=4,'yh'=2,'core'=2] {'z','yl','x'}, dimensions={0} | all-to-all | bytes 1081344 | tf_op jit(solution)/shard_map/all_to_all | solution.py:295
  60.9 1.9 %shard_map.132 = bf16[64,3,1280]{2,1,0:T(4,128)(2,1)} custom-call(bf16[64,3,1408]{2,1,0:T(4,128)(2,1)S(1)} %all_to_all.22.met_ref), custom_call_target="tpu_custom_call" | custom-call | flops 500000000 | bytes 1500000 | tf_op jit(solution)/shard_map/pallas_call | solution.py:165
  62.8 8.6 %all-to-all-start.1 = ((bf16[64,3,1280]{2,1,0:T(4,128)(2,1)}), bf16[64,3,1280]{2,1,0:T(4,128)(2,1)S(1)}, u32[]{:S(2)}, u32[]{:S(2)}) async-start(bf16[64,3,1280]{2,1,0:T(4,128)(2,1)} %shard_map.132), calls=%async_computation.1 | async-start | bytes 1310720 | tf_op jit(solution)/shard_map/all_to_all | solution.py:298
  71.9 1.6 collective-permute-start.2
  74.1 21.5 %all-to-all-done.1 = bf16[64,3,1280]{2,1,0:T(4,128)(2,1)S(1)} async-done(((bf16[64,3,1280]{2,1,0:T(4,128)(2,1)}), bf16[64,3,1280]{2,1,0:T(4,128)(2,1)S(1)}, u32[]{:S(2)}, u32[]{:S(2)}) %all-to-all-start.1) | async-done | bytes 491552 | tf_op jit(solution)/shard_map/all_to_all | solution.py:298
  96.1 3.2 %fusion.2 = f32[192,1536]{1,0:T(8,128)S(1)} fusion(bf16[1280,1536]{1,0:T(8,128)(2,1)} %param.21, bf16[192,1280]{1,0:T(8,128)(2,1)S(1)} %reshape.217, f32[1280]{0:T(1024)S(1)} %copy-done.5), kind=kOutput, calls=%fused_computation.5 | convolution fusion | flops 755712000 | bytes 5608448 | tf_op jit(solution)/shard_map/dot_general | solution.py:30
  99.9 3.0 %collective-permute-start.4 = (bf16[192,400]{1,0:T(8,128)(2,1)S(1)}, bf16[192,400]{1,0:T(8,128)(2,1)S(1)}, u32[]{:S(2)}, u32[]{:S(2)}) collective-permute-start(bf16[192,400]{1,0:T(8,128)(2,1)S(1)} %get-tuple-element.62), channel_id=1, source_target_pairs={{0,2},{1,3},{2,0},{3,1},{4,6},{5,7},{6,4},{7,5},{8,10},{9,11},{10,... | collective-permute-start | bytes 460808 | tf_op jit(solution)/shard_map/ppermute | solution.py:324
  104.3 1.0 copy.37.row_ref
  105.4 3.4 %collective-permute-done.4 = bf16[192,400]{1,0:T(8,128)(2,1)S(1)} collective-permute-done((bf16[192,400]{1,0:T(8,128)(2,1)S(1)}, bf16[192,400]{1,0:T(8,128)(2,1)S(1)}, u32[]{:S(2)}, u32[]{:S(2)}) %collective-permute-start.4) | collective-permute-done | bytes 153632 | tf_op jit(solution)/shard_map/ppermute | solution.py:324
  108.9 3.8 %collective-permute-done.3 = bf16[192,400]{1,0:T(8,128)(2,1)S(1)} collective-permute-done((bf16[192,400]{1,0:T(8,128)(2,1)S(1)}, bf16[192,400]{1,0:T(8,128)(2,1)S(1)}, u32[]{:S(2)}, u32[]{:S(2)}) %collective-permute-start.3) | collective-permute-done | bytes 153632 | tf_op jit(solution)/shard_map/ppermute | solution.py:324
  114.5 9.0 %all-to-all-start.2 = ((f32[64,1,9]{2,1,0:T(1,128)}), f32[64,1,9]{2,1,0:T(1,128)S(1)}, u32[]{:S(2)}, u32[]{:S(2)}) async-start(f32[64,1,9]{2,1,0:T(1,128)} %bitcast.20), calls=%async_computation.2 | async-start | bytes 65536 | tf_op jit(solution)/shard_map/all_to_all | solution.py:351
  123.5 30.6 %shard_map.133 = (bf16[192,640]{1,0:T(8,128)(2,1)}, bf16[192,640]{1,0:T(8,128)(2,1)}) custom-call(s32[12]{0:T(128)} %pad_add_fusion.1.plan, bf16[192,640]{1,0:T(8,128)(2,1)} %copy-done.8, bf16[192,640]{1,0:T(8,128)(2,1)} %copy-done.7, s32[960,1]{1,0:T(8,128)} %copy.37.row_ref, bf16[8,4,2,2,192,128]{5,4,3,2,1,0:T(8,128)(2,1)} %bitcast.83, ...), custom_call_target="tpu_custom_call" | custom-call | flops 20000000000 | bytes 8000000 | tf_op jit(solution)/shard_map/pallas_call | solution.py:128
  154.1 1.5 collective-permute-start.7
  155.6 2.7 %collective-permute-start.6 = (bf16[192,640]{1,0:T(8,128)(2,1)}, bf16[192,640]{1,0:T(8,128)(2,1)S(1)}, u32[]{:S(2)}, u32[]{:S(2)}) collective-permute-start(bf16[192,640]{1,0:T(8,128)(2,1)} %get-tuple-element.39), channel_id=1, source_target_pairs={{0,224},{32,192},{64,160},{96,128},{128,96},{160,64},{192,32},{224... | collective-permute-start | bytes 737288 | tf_op jit(solution)/shard_map/ppermute | solution.py:275
  158.8 6.7 %all-gather.2 = f32[4,3,3]{2,1,0:T(4,128)S(1)} all-gather(f32[1,3,3]{2,1,0:T(4,128)S(1)} %maximum_bitcast_fusion.1), channel_id=3, replica_groups=mesh['z'=8,'yl'=2,'x'=4,'yh'=2,'core'=2] {'yh','core'}, dimensions={0}, use_global_device_ids=true | all-gather | bytes 180 | tf_op jit(solution)/shard_map/all_gather | solution.py:356
  166.0 3.6 %collective-permute-done.6 = bf16[192,640]{1,0:T(8,128)(2,1)S(1)} collective-permute-done((bf16[192,640]{1,0:T(8,128)(2,1)}, bf16[192,640]{1,0:T(8,128)(2,1)S(1)}, u32[]{:S(2)}, u32[]{:S(2)}) %collective-permute-start.6) | collective-permute-done | bytes 245792 | tf_op jit(solution)/shard_map/ppermute | solution.py:275
  169.6 0.9 maximum_select_fusion
  (79 shorter events, 11.8 us)
Async XLA Ops:
  7.2 116.3 %all-gather.5.cloned.1.call-start = ((), (), s32[]{:S(2)}) async-start(), calls=%async_computation.3 | async-start | bytes 6488064 | tf_op jit(solution)/shard_map/all_gather | solution.py:282
  8.1 5.1 %collective-permute-start = (bf16[2,192,128]{2,1,0:T(8,128)(2,1)S(1)}, bf16[2,192,128]{2,1,0:T(8,128)(2,1)S(1)}, u32[]{:S(2)}, u32[]{:S(2)}) collective-permute-start(bf16[2,192,128]{2,1,0:T(8,128)(2,1)S(1)} %pad_maximum_fusion.3), channel_id=1, source_target_pairs={{0,16},{16,0},{1,17},{17,1},{2,18},{18,2},{3,19},{19,3},{4,20},{20... | collective-permute-start | bytes 294920 | tf_op jit(solution)/shard_map/ppermute | solution.py:224
  14.0 14.2 %collective-permute-start.1 = (bf16[192,640]{1,0:T(8,128)(2,1)S(1)}, bf16[192,640]{1,0:T(8,128)(2,1)S(1)}, u32[]{:S(2)}, u32[]{:S(2)}) collective-permute-start(bf16[192,640]{1,0:T(8,128)(2,1)S(1)} %get-tuple-element.24), channel_id=1, source_target_pairs={{0,224},{32,192},{64,160},{96,128},{128,96},{160,64},{192,32},{224... | collective-permute-start | bytes 737288 | tf_op jit(solution)/shard_map/ppermute | solution.py:275
  17.2 0.9 copy-start
  18.1 0.9 copy-start.1
  19.0 1.0 copy-start.2
  23.3 48.1 %copy-start.3 = (s32[12288]{0:T(1024)S(1)}, s32[12288]{0:T(1024)}, u32[]{:S(2)}) copy-start(s32[12288]{0:T(1024)} %param.15) | copy-start | bytes 147460
  23.3 50.8 %copy-start.6 = (s32[3,64]{1,0:T(4,128)S(1)}, s32[3,64]{1,0:T(4,128)}, u32[]{:S(2)}) copy-start(s32[3,64]{1,0:T(4,128)} %param.23) | copy-start | bytes 2308
  23.3 72.7 %copy-start.5 = (f32[1280]{0:T(1024)S(1)}, f32[1280]{0:T(1024)}, u32[]{:S(2)}) copy-start(f32[1280]{0:T(1024)} %param.20) | copy-start | bytes 15364
  28.1 71.1 %copy-start.7 = (bf16[192,640]{1,0:T(8,128)(2,1)}, bf16[192,640]{1,0:T(8,128)(2,1)S(1)}, u32[]{:S(2)}) copy-start(bf16[192,640]{1,0:T(8,128)(2,1)S(1)} %collective-permute-done.1.qb_ref) | copy-start | bytes 737284
  62.8 32.8 %all-to-all-start.1 = ((bf16[64,3,1280]{2,1,0:T(4,128)(2,1)}), bf16[64,3,1280]{2,1,0:T(4,128)(2,1)S(1)}, u32[]{:S(2)}, u32[]{:S(2)}) async-start(bf16[64,3,1280]{2,1,0:T(4,128)(2,1)} %shard_map.132), calls=%async_computation.1 | async-start | bytes 1310720 | tf_op jit(solution)/shard_map/all_to_all | solution.py:298
  71.9 24.2 %collective-permute-start.2 = (bf16[192,640]{1,0:T(8,128)(2,1)S(1)}, bf16[192,640]{1,0:T(8,128)(2,1)S(1)}, u32[]{:S(2)}, u32[]{:S(2)}) collective-permute-start(bf16[192,640]{1,0:T(8,128)(2,1)S(1)} %get-tuple-element.27), channel_id=1, source_target_pairs={{0,16},{16,0},{1,17},{17,1},{2,18},{18,2},{3,19},{19,3},{4,20},{20... | collective-permute-start | bytes 737288 | tf_op jit(solution)/shard_map/ppermute | solution.py:224
  96.0 6.9 %copy-start.4 = (s32[3,64,32]{1,2,0:T(8,128)S(1)}, s32[3,64,32]{1,2,0:T(8,128)}, u32[]{:S(2)}) copy-start(s32[3,64,32]{1,2,0:T(8,128)} %param.22) | copy-start | bytes 73732
  96.1 3.7 %copy-start.8 = (bf16[192,640]{1,0:T(8,128)(2,1)}, bf16[192,640]{1,0:T(8,128)(2,1)S(1)}, u32[]{:S(2)}) copy-start(bf16[192,640]{1,0:T(8,128)(2,1)S(1)} %collective-permute-done.2.qa_ref) | copy-start | bytes 737284
  99.7 5.6 %collective-permute-start.5 = (bf16[192,400]{1,0:T(8,128)(2,1)S(1)}, bf16[192,400]{1,0:T(8,128)(2,1)S(1)}, u32[]{:S(2)}, u32[]{:S(2)}) collective-permute-start(bf16[192,400]{1,0:T(8,128)(2,1)S(1)} %get-tuple-element.63), channel_id=1, source_target_pairs={{0,1},{1,0},{2,3},{3,2},{4,5},{5,4},{6,7},{7,6},{8,9},{9,8},{10,11... | collective-permute-start | bytes 460808 | tf_op jit(solution)/shard_map/ppermute | solution.py:324
  99.9 9.0 %collective-permute-start.4 = (bf16[192,400]{1,0:T(8,128)(2,1)S(1)}, bf16[192,400]{1,0:T(8,128)(2,1)S(1)}, u32[]{:S(2)}, u32[]{:S(2)}) collective-permute-start(bf16[192,400]{1,0:T(8,128)(2,1)S(1)} %get-tuple-element.62), channel_id=1, source_target_pairs={{0,2},{1,3},{2,0},{3,1},{4,6},{5,7},{6,4},{7,5},{8,10},{9,11},{10,... | collective-permute-start | bytes 460808 | tf_op jit(solution)/shard_map/ppermute | solution.py:324
  103.7 9.0 %collective-permute-start.3 = (bf16[192,400]{1,0:T(8,128)(2,1)S(1)}, bf16[192,400]{1,0:T(8,128)(2,1)S(1)}, u32[]{:S(2)}, u32[]{:S(2)}) collective-permute-start(bf16[192,400]{1,0:T(8,128)(2,1)S(1)} %get-tuple-element.61), channel_id=1, source_target_pairs={{0,3},{1,2},{2,1},{3,0},{4,7},{5,6},{6,5},{7,4},{8,11},{9,10},{10,... | collective-permute-start | bytes 460808 | tf_op jit(solution)/shard_map/ppermute | solution.py:324
  114.5 39.7 %all-to-all-start.2 = ((f32[64,1,9]{2,1,0:T(1,128)}), f32[64,1,9]{2,1,0:T(1,128)S(1)}, u32[]{:S(2)}, u32[]{:S(2)}) async-start(f32[64,1,9]{2,1,0:T(1,128)} %bitcast.20), calls=%async_computation.2 | async-start | bytes 65536 | tf_op jit(solution)/shard_map/all_to_all | solution.py:351
  154.1 11.9 %collective-permute-start.7 = (bf16[192,640]{1,0:T(8,128)(2,1)}, bf16[192,640]{1,0:T(8,128)(2,1)S(1)}, u32[]{:S(2)}, u32[]{:S(2)}) collective-permute-start(bf16[192,640]{1,0:T(8,128)(2,1)} %get-tuple-element.40), channel_id=1, source_target_pairs={{0,16},{16,0},{1,17},{17,1},{2,18},{18,2},{3,19},{19,3},{4,20},{20... | collective-permute-start | bytes 737288 | tf_op jit(solution)/shard_map/ppermute | solution.py:224
  155.6 14.0 %collective-permute-start.6 = (bf16[192,640]{1,0:T(8,128)(2,1)}, bf16[192,640]{1,0:T(8,128)(2,1)S(1)}, u32[]{:S(2)}, u32[]{:S(2)}) collective-permute-start(bf16[192,640]{1,0:T(8,128)(2,1)} %get-tuple-element.39), channel_id=1, source_target_pairs={{0,224},{32,192},{64,160},{96,128},{128,96},{160,64},{192,32},{224... | collective-permute-start | bytes 737288 | tf_op jit(solution)/shard_map/ppermute | solution.py:275
Sparse Core Ops, SparseCore 0:
  14.1 103.1 all-gather.4

commit v7 on v5

--- a/solution.py
+++ b/solution.py
@@ -48,7 +48,7 @@
     return which, tile
 
 
-def attend_kernel(plan, qa_ref, qb_ref, row_ref, k_ref, v_ref, outa_ref, outb_ref, qs, peak, acc):
+def attend_kernel(plan, qa_ref, qb_ref, k_ref, v_ref, outa_ref, outb_ref, qs, peak, acc):
     rows, width = qa_ref.shape
     group = width // HD
     keys = k_ref.shape[1] * rows
@@ -86,7 +86,8 @@
                 ahead = dot(qs[which, (i + 1) * CHUNK : (i + 2) * CHUNK], k)
             here = slice(i * CHUNK, (i + 1) * CHUNK)
             if masked:
-                row = row_ref[here]
+                row = i * CHUNK + lax.broadcasted_iota(jnp.int32, (CHUNK, 1), 0)
+                row = row - sum(jnp.where(row >= h * rows, rows, 0) for h in range(1, group))
                 s = jnp.where((at <= row) & (row < end), s, BELOW)
             old = peak[which, here]
             new = jnp.maximum(old, jnp.max(s, axis=1, keepdims=True))
@@ -109,7 +110,7 @@
                 out_ref[:, h * HD : (h + 1) * HD] = (acc[b, here, 0:HD] / acc[b, here, HD:]).astype(BF)
 
 
-def attend(plan, qa, qb, row, kv):
+def attend(plan, qa, qb, kv):
     rows, width = qa.shape
     nz, nx, ny, _, _, _ = kv.shape
     keys = nx * rows
@@ -131,7 +132,7 @@
         grid_spec=pltpu.PrefetchScalarGridSpec(
             num_scalar_prefetch=1,
             grid=(nz * ny + 2,),
-            in_specs=[whole(qa.shape), whole(qb.shape), whole(row.shape), tiles(0), tiles(1)],
+            in_specs=[whole(qa.shape), whole(qb.shape), tiles(0), tiles(1)],
             out_specs=[whole(qa.shape)] * 2,
             scratch_shapes=[
                 pltpu.VMEM((2, flat, 2 * HD), BF),
@@ -145,7 +146,7 @@
         cost_estimate=pl.CostEstimate(
             flops=20_000_000_000, bytes_accessed=8_000_000, transcendentals=10_000_000
         ),
-    )(plan, qa, qb, row, kv, kv)
+    )(plan, qa, qb, kv, kv)
 
 
 def merge_kernel(met_ref, out_ref):
@@ -296,11 +297,10 @@
     spread = lax.all_to_all(attention, CTX, 0, 0, tiled=True).reshape(lines * steps, width)
 
     q_near = swap(q_other, "yl")
-    spread, q_near = after((spread, q_near))
-    row = jnp.tile(jnp.arange(rows, dtype=jnp.int32), group)[:, None]
     first_rows = jnp.stack([((z * ny + 1 - yl) * nx + x) * rows, ((nz - 1 - z) * ny + yl) * nx * rows + x * rows])
     first_keys = jnp.max(jnp.where(begins[None, :] <= first_rows[:, None], begins[None, :], 0), axis=1)
     plan = jnp.concatenate([first_keys, first_rows, begins])
+    spread, q_near, plan = after((spread, q_near, plan))
 
     widened = spread.astype(F32)
     squares = jnp.sum(widened * widened, axis=1, keepdims=True)
@@ -345,7 +345,7 @@
 
     stats = jnp.stack([top, mass, target], axis=-1).reshape(lines, steps * 3)
     q_near, q_far, stats = after((q_near, q_far, stats))
-    near, far = attend(plan, q_near, q_far, row, kv_all)
+    near, far = attend(plan, q_near, q_far, kv_all)
     stats = lax.all_to_all(stats, CTX, 0, 0, tiled=True)
     stats, near, far = after((stats, near, far))
     out_other, out_mine = swap(near, "yl"), mirror(far)

time: 173 us -> 170 us (0.983)
  the two profiles are of different devices: /device:TPU:96 before, /device:TPU:1 now
where the time goes in v7:
time: 170 us; the launch traced here: 171 us
  starting transfers between devices  37.1 us (22%)
  Pallas kernels  35.7 us (21%)
  blocking collectives  35.7 us (21%)
  waiting for transfers between devices  29.8 us (18%)
  between operations  14.4 us (8%)
  other arithmetic  8.5 us (5%)
  local copies, waits for them, and re-layouts  6.45 us (4%)
  matrix products  3.14 us (2%)
    pallas_call x1, Pallas kernels, attend(): pl.pallas_call(attend_kernel, out_shape=[jax.ShapeDtypeStruct(qa.shape, B...  30.6 us
    all_to_all x1, blocking collectives, local(): met = lax.all_to_all(state, CTX, 0, 0, tiled=True)  27.5 us
    all_to_all x1, waiting for transfers between devices, local(): lax.all_to_all(attention, CTX, 0, 0, tiled=True)  12.9 us
    ppermute x3, starting transfers between devices, local(): lax.ppermute(jnp.concatenate([sent, extra], axis=1), TP, [(i, i ^ away) f...  9.94 us
    ppermute x2, starting transfers between devices, mirror(): return lax.ppermute(value, 'z', [(i, nz - 1 - i) for i in range(nz)])  8.92 us
    all_to_all x1, starting transfers between devices, local(): lax.all_to_all(attention, CTX, 0, 0, tiled=True)  8.9 us
    all_gather x1, blocking collectives, local(): stats = lax.all_gather(stats, TP, axis=0)  8.12 us
    ppermute x3, waiting for transfers between devices, local(): lax.ppermute(jnp.concatenate([sent, extra], axis=1), TP, [(i, i ^ away) f...  7.88 us
  transfers between devices with their start and end apart: 11, of which 5 were waited for; matrix products, arithmetic and copies ran while one was open for 8% of the time, Pallas kernels for 21%

profile of v7, /device:TPU:1, one launch (start us, length us, event | category | flops | bytes accessed | tf_op | source)
XLA Modules:
  0.0 170.7 jit_solution(8403126286323941272)
XLA Ops:
  7.2 0.9 select_bitcast_fusion.2
  8.1 2.2 %collective-permute-start = (bf16[2,192,128]{2,1,0:T(8,128)(2,1)S(1)}, bf16[2,192,128]{2,1,0:T(8,128)(2,1)S(1)}, u32[]{:S(2)}, u32[]{:S(2)}) collective-permute-start(bf16[2,192,128]{2,1,0:T(8,128)(2,1)S(1)} %pad_maximum_fusion.3), channel_id=1, source_target_pairs={{0,16},{16,0},{1,17},{17,1},{2,18},{18,2},{3,19},{19,3},{4,20},{20... | collective-permute-start | bytes 294920 | tf_op jit(solution)/shard_map/ppermute | solution.py:225
  10.3 1.1 broadcast_select_fusion
  11.5 5.7 %collective-permute-start.1 = (bf16[192,640]{1,0:T(8,128)(2,1)S(1)}, bf16[192,640]{1,0:T(8,128)(2,1)S(1)}, u32[]{:S(2)}, u32[]{:S(2)}) collective-permute-start(bf16[192,640]{1,0:T(8,128)(2,1)S(1)} %get-tuple-element.47), channel_id=1, source_target_pairs={{0,224},{32,192},{64,160},{96,128},{128,96},{160,64},{192,32},{224... | collective-permute-start | bytes 737288 | tf_op jit(solution)/shard_map/ppermute | solution.py:276
  20.4 0.9 copy-done.1
  21.3 1.0 copy-done.2
  22.3 3.3 %shard_map.131 = bf16[192,1408]{1,0:T(8,128)(2,1)S(1)} custom-call(bf16[192,1280]{1,0:T(8,128)(2,1)S(1)} %bitcast.66, bf16[192,256]{1,0:T(8,128)(2,1)S(1)} %copy-done.1, bf16[192,256]{1,0:T(8,128)(2,1)S(1)} %copy-done, bf16[16,512]{1,0:T(8,128)(2,1)S(1)} %fusion.8.own_ref, s32[192,256]{1,0:T(8,128)S(1)} %bitcast.65), custom_call_target="tpu_custom_call" | custom-call | flops 4000000000 | bytes 1500000 | tf_op jit(solution)/shard_map/pallas_call | solution.py:210
  26.9 1.5 collective-permute-done.1.qb_ref
  28.4 27.5 %all_to_all.22.met_ref = bf16[64,3,1408]{2,1,0:T(4,128)(2,1)S(1)} all-to-all(bf16[64,3,1408]{2,1,0:T(4,128)(2,1)S(1)} %bitcast.67), channel_id=1, replica_groups=mesh['z'=8,'yl'=2,'x'=4,'yh'=2,'core'=2] {'z','yl','x'}, dimensions={0} | all-to-all | bytes 1081344 | tf_op jit(solution)/shard_map/all_to_all | solution.py:294
  55.9 1.9 %shard_map.132 = bf16[64,3,1280]{2,1,0:T(4,128)(2,1)} custom-call(bf16[64,3,1408]{2,1,0:T(4,128)(2,1)S(1)} %all_to_all.22.met_ref), custom_call_target="tpu_custom_call" | custom-call | flops 500000000 | bytes 1500000 | tf_op jit(solution)/shard_map/pallas_call | solution.py:166
  57.8 8.9 %all-to-all-start.1 = ((bf16[64,3,1280]{2,1,0:T(4,128)(2,1)}), bf16[64,3,1280]{2,1,0:T(4,128)(2,1)S(1)}, u32[]{:S(2)}, u32[]{:S(2)}) async-start(bf16[64,3,1280]{2,1,0:T(4,128)(2,1)} %shard_map.132), calls=%async_computation.1 | async-start | bytes 1310720 | tf_op jit(solution)/shard_map/all_to_all | solution.py:297
  67.2 1.1 collective-permute-start.2
  68.9 12.9 %all-to-all-done.1 = bf16[64,3,1280]{2,1,0:T(4,128)(2,1)S(1)} async-done(((bf16[64,3,1280]{2,1,0:T(4,128)(2,1)}), bf16[64,3,1280]{2,1,0:T(4,128)(2,1)S(1)}, u32[]{:S(2)}, u32[]{:S(2)}) %all-to-all-start.1) | async-done | bytes 491552 | tf_op jit(solution)/shard_map/all_to_all | solution.py:297
  82.3 3.1 %fusion.2 = f32[192,1536]{1,0:T(8,128)S(1)} fusion(bf16[1280,1536]{1,0:T(8,128)(2,1)} %param.21, bf16[192,1280]{1,0:T(8,128)(2,1)S(1)} %reshape.217, f32[1280]{0:T(1024)S(1)} %copy-done.5), kind=kOutput, calls=%fused_computation.5 | convolution fusion | flops 755712000 | bytes 5608448 | tf_op jit(solution)/shard_map/dot_general | solution.py:30
  85.9 6.4 %collective-permute-start.5 = (bf16[192,400]{1,0:T(8,128)(2,1)S(1)}, bf16[192,400]{1,0:T(8,128)(2,1)S(1)}, u32[]{:S(2)}, u32[]{:S(2)}) collective-permute-start(bf16[192,400]{1,0:T(8,128)(2,1)S(1)} %get-tuple-element.55), channel_id=1, source_target_pairs={{0,1},{1,0},{2,3},{3,2},{4,5},{5,4},{6,7},{7,6},{8,9},{9,8},{10,11... | collective-permute-start | bytes 460808 | tf_op jit(solution)/shard_map/ppermute | solution.py:322
  92.3 2.9 %collective-permute-start.4 = (bf16[192,400]{1,0:T(8,128)(2,1)S(1)}, bf16[192,400]{1,0:T(8,128)(2,1)S(1)}, u32[]{:S(2)}, u32[]{:S(2)}) collective-permute-start(bf16[192,400]{1,0:T(8,128)(2,1)S(1)} %get-tuple-element.54), channel_id=1, source_target_pairs={{0,2},{1,3},{2,0},{3,1},{4,6},{5,7},{6,4},{7,5},{8,10},{9,11},{10,... | collective-permute-start | bytes 460808 | tf_op jit(solution)/shard_map/ppermute | solution.py:322
  96.7 3.5 %collective-permute-done.4 = bf16[192,400]{1,0:T(8,128)(2,1)S(1)} collective-permute-done((bf16[192,400]{1,0:T(8,128)(2,1)S(1)}, bf16[192,400]{1,0:T(8,128)(2,1)S(1)}, u32[]{:S(2)}, u32[]{:S(2)}) %collective-permute-start.4) | collective-permute-done | bytes 153632 | tf_op jit(solution)/shard_map/ppermute | solution.py:322
  100.4 4.3 %collective-permute-done.3 = bf16[192,400]{1,0:T(8,128)(2,1)S(1)} collective-permute-done((bf16[192,400]{1,0:T(8,128)(2,1)S(1)}, bf16[192,400]{1,0:T(8,128)(2,1)S(1)}, u32[]{:S(2)}, u32[]{:S(2)}) %collective-permute-start.3) | collective-permute-done | bytes 153632 | tf_op jit(solution)/shard_map/ppermute | solution.py:322
  106.5 5.9 %all-to-all-start.2 = ((f32[64,1,9]{2,1,0:T(1,128)}), f32[64,1,9]{2,1,0:T(1,128)S(1)}, u32[]{:S(2)}, u32[]{:S(2)}) async-start(f32[64,1,9]{2,1,0:T(1,128)} %bitcast.20), calls=%async_computation.2 | async-start | bytes 65536 | tf_op jit(solution)/shard_map/all_to_all | solution.py:349
  112.4 7.6 %all-gather.5.cloned.1.call-done = bf16[64,2,192,128]{3,2,1,0:T(8,128)(2,1)} async-done(((bf16[2,2,192,128]{3,2,1,0:T(8,128)(2,1)}), bf16[64,2,192,128]{3,2,1,0:T(8,128)(2,1)}) %all-gather.5.cloned.1.call-update) | async-done | bytes 6291472 | tf_op jit(solution)/shard_map/all_gather | solution.py:292
  119.9 30.6 %shard_map.133 = (bf16[192,640]{1,0:T(8,128)(2,1)}, bf16[192,640]{1,0:T(8,128)(2,1)}) custom-call(s32[12]{0:T(128)} %pad_add_fusion.1.plan, bf16[192,640]{1,0:T(8,128)(2,1)} %copy-done.8, bf16[192,640]{1,0:T(8,128)(2,1)} %copy-done.7, bf16[8,4,2,2,192,128]{5,4,3,2,1,0:T(8,128)(2,1)} %bitcast.83, bf16[8,4,2,2,192,128]{5,4,3,2,1,0:T(8,128)(2,1)} %bitcast.84), custom_call_target="tpu_custom_call" | custom-call | flops 20000000000 | bytes 8000000 | tf_op jit(solution)/shard_map/pallas_call | solution.py:129
  150.6 3.3 %collective-permute-start.6 = (bf16[192,640]{1,0:T(8,128)(2,1)}, bf16[192,640]{1,0:T(8,128)(2,1)S(1)}, u32[]{:S(2)}, u32[]{:S(2)}) collective-permute-start(bf16[192,640]{1,0:T(8,128)(2,1)} %get-tuple-element.31), channel_id=1, source_target_pairs={{0,224},{32,192},{64,160},{96,128},{128,96},{160,64},{192,32},{224... | collective-permute-start | bytes 737288 | tf_op jit(solution)/shard_map/ppermute | solution.py:276
  154.3 8.1 %all-gather.2 = f32[4,3,3]{2,1,0:T(4,128)S(1)} all-gather(f32[1,3,3]{2,1,0:T(4,128)S(1)} %maximum_bitcast_fusion.1), channel_id=3, replica_groups=mesh['z'=8,'yl'=2,'x'=4,'yh'=2,'core'=2] {'yh','core'}, dimensions={0}, use_global_device_ids=true | all-gather | bytes 180 | tf_op jit(solution)/shard_map/all_gather | solution.py:354
  163.0 0.9 maximum_select_fusion
  (77 shorter events, 10.9 us)
Async XLA Ops:
  7.2 112.8 %all-gather.5.cloned.1.call-start = ((), (), s32[]{:S(2)}) async-start(), calls=%async_computation.3 | async-start | bytes 6488064 | tf_op jit(solution)/shard_map/all_gather | solution.py:292
  8.1 18.0 %collective-permute-start = (bf16[2,192,128]{2,1,0:T(8,128)(2,1)S(1)}, bf16[2,192,128]{2,1,0:T(8,128)(2,1)S(1)}, u32[]{:S(2)}, u32[]{:S(2)}) collective-permute-start(bf16[2,192,128]{2,1,0:T(8,128)(2,1)S(1)} %pad_maximum_fusion.3), channel_id=1, source_target_pairs={{0,16},{16,0},{1,17},{17,1},{2,18},{18,2},{3,19},{19,3},{4,20},{20... | collective-permute-start | bytes 294920 | tf_op jit(solution)/shard_map/ppermute | solution.py:225
  11.5 16.9 %collective-permute-start.1 = (bf16[192,640]{1,0:T(8,128)(2,1)S(1)}, bf16[192,640]{1,0:T(8,128)(2,1)S(1)}, u32[]{:S(2)}, u32[]{:S(2)}) collective-permute-start(bf16[192,640]{1,0:T(8,128)(2,1)S(1)} %get-tuple-element.47), channel_id=1, source_target_pairs={{0,224},{32,192},{64,160},{96,128},{128,96},{160,64},{192,32},{224... | collective-permute-start | bytes 737288 | tf_op jit(solution)/shard_map/ppermute | solution.py:276
  19.5 0.9 copy-start
  20.4 0.9 copy-start.1
  21.3 1.0 copy-start.2
  25.6 41.2 %copy-start.3 = (s32[12288]{0:T(1024)S(1)}, s32[12288]{0:T(1024)}, u32[]{:S(2)}) copy-start(s32[12288]{0:T(1024)} %param.15) | copy-start | bytes 147460
  25.6 43.3 %copy-start.6 = (s32[3,64]{1,0:T(4,128)S(1)}, s32[3,64]{1,0:T(4,128)}, u32[]{:S(2)}) copy-start(s32[3,64]{1,0:T(4,128)} %param.23) | copy-start | bytes 2308
  25.6 56.6 %copy-start.5 = (f32[1280]{0:T(1024)S(1)}, f32[1280]{0:T(1024)}, u32[]{:S(2)}) copy-start(f32[1280]{0:T(1024)} %param.20) | copy-start | bytes 15364
  28.3 57.1 %copy-start.7 = (bf16[192,640]{1,0:T(8,128)(2,1)}, bf16[192,640]{1,0:T(8,128)(2,1)S(1)}, u32[]{:S(2)}) copy-start(bf16[192,640]{1,0:T(8,128)(2,1)S(1)} %collective-permute-done.1.qb_ref) | copy-start | bytes 737284
  57.8 24.0 %all-to-all-start.1 = ((bf16[64,3,1280]{2,1,0:T(4,128)(2,1)}), bf16[64,3,1280]{2,1,0:T(4,128)(2,1)S(1)}, u32[]{:S(2)}, u32[]{:S(2)}) async-start(bf16[64,3,1280]{2,1,0:T(4,128)(2,1)} %shard_map.132), calls=%async_computation.1 | async-start | bytes 1310720 | tf_op jit(solution)/shard_map/all_to_all | solution.py:297
  67.2 15.0 %collective-permute-start.2 = (bf16[192,640]{1,0:T(8,128)(2,1)S(1)}, bf16[192,640]{1,0:T(8,128)(2,1)S(1)}, u32[]{:S(2)}, u32[]{:S(2)}) collective-permute-start(bf16[192,640]{1,0:T(8,128)(2,1)S(1)} %get-tuple-element.20), channel_id=1, source_target_pairs={{0,16},{16,0},{1,17},{17,1},{2,18},{18,2},{3,19},{19,3},{4,20},{20... | collective-permute-start | bytes 737288 | tf_op jit(solution)/shard_map/ppermute | solution.py:225
  82.2 13.0 %copy-start.4 = (s32[3,64,32]{1,2,0:T(8,128)S(1)}, s32[3,64,32]{1,2,0:T(8,128)}, u32[]{:S(2)}) copy-start(s32[3,64,32]{1,2,0:T(8,128)} %param.22) | copy-start | bytes 73732
  82.2 3.6 %copy-start.8 = (bf16[192,640]{1,0:T(8,128)(2,1)}, bf16[192,640]{1,0:T(8,128)(2,1)S(1)}, u32[]{:S(2)}) copy-start(bf16[192,640]{1,0:T(8,128)(2,1)S(1)} %collective-permute-done.2.qa_ref) | copy-start | bytes 737284
  85.9 10.8 %collective-permute-start.5 = (bf16[192,400]{1,0:T(8,128)(2,1)S(1)}, bf16[192,400]{1,0:T(8,128)(2,1)S(1)}, u32[]{:S(2)}, u32[]{:S(2)}) collective-permute-start(bf16[192,400]{1,0:T(8,128)(2,1)S(1)} %get-tuple-element.55), channel_id=1, source_target_pairs={{0,1},{1,0},{2,3},{3,2},{4,5},{5,4},{6,7},{7,6},{8,9},{9,8},{10,11... | collective-permute-start | bytes 460808 | tf_op jit(solution)/shard_map/ppermute | solution.py:322
  92.3 8.0 %collective-permute-start.4 = (bf16[192,400]{1,0:T(8,128)(2,1)S(1)}, bf16[192,400]{1,0:T(8,128)(2,1)S(1)}, u32[]{:S(2)}, u32[]{:S(2)}) collective-permute-start(bf16[192,400]{1,0:T(8,128)(2,1)S(1)} %get-tuple-element.54), channel_id=1, source_target_pairs={{0,2},{1,3},{2,0},{3,1},{4,6},{5,7},{6,4},{7,5},{8,10},{9,11},{10,... | collective-permute-start | bytes 460808 | tf_op jit(solution)/shard_map/ppermute | solution.py:322
  96.0 8.7 %collective-permute-start.3 = (bf16[192,400]{1,0:T(8,128)(2,1)S(1)}, bf16[192,400]{1,0:T(8,128)(2,1)S(1)}, u32[]{:S(2)}, u32[]{:S(2)}) collective-permute-start(bf16[192,400]{1,0:T(8,128)(2,1)S(1)} %get-tuple-element.53), channel_id=1, source_target_pairs={{0,3},{1,2},{2,1},{3,0},{4,7},{5,6},{6,5},{7,4},{8,11},{9,10},{10,... | collective-permute-start | bytes 460808 | tf_op jit(solution)/shard_map/ppermute | solution.py:322
  106.5 44.1 %all-to-all-start.2 = ((f32[64,1,9]{2,1,0:T(1,128)}), f32[64,1,9]{2,1,0:T(1,128)S(1)}, u32[]{:S(2)}, u32[]{:S(2)}) async-start(f32[64,1,9]{2,1,0:T(1,128)} %bitcast.20), calls=%async_computation.2 | async-start | bytes 65536 | tf_op jit(solution)/shard_map/all_to_all | solution.py:349
  150.5 12.4 %collective-permute-start.7 = (bf16[192,640]{1,0:T(8,128)(2,1)}, bf16[192,640]{1,0:T(8,128)(2,1)S(1)}, u32[]{:S(2)}, u32[]{:S(2)}) collective-permute-start(bf16[192,640]{1,0:T(8,128)(2,1)} %get-tuple-element.32), channel_id=1, source_target_pairs={{0,16},{16,0},{1,17},{17,1},{2,18},{18,2},{3,19},{19,3},{4,20},{20... | collective-permute-start | bytes 737288 | tf_op jit(solution)/shard_map/ppermute | solution.py:225
  150.6 12.4 %collective-permute-start.6 = (bf16[192,640]{1,0:T(8,128)(2,1)}, bf16[192,640]{1,0:T(8,128)(2,1)S(1)}, u32[]{:S(2)}, u32[]{:S(2)}) collective-permute-start(bf16[192,640]{1,0:T(8,128)(2,1)} %get-tuple-element.31), channel_id=1, source_target_pairs={{0,224},{32,192},{64,160},{96,128},{128,96},{160,64},{192,32},{224... | collective-permute-start | bytes 737288 | tf_op jit(solution)/shard_map/ppermute | solution.py:276
Sparse Core Ops, SparseCore 0:
  28.5 91.3 all-gather.4
